TPU v7x, 32 devices: a whole 2x2x4 slice. The times are simulated.
32 devices in a mesh: dp: 4 (over y, x), rows: 8 (over z, core).
Axes of the slice: x: 2, y: 2, z: 4, core: 2. Of those that a mesh axis runs over, the one named last changes fastest.
Arguments:
- inputs: bfloat16 [4, 512, 64, 384], P('dp', 'rows'), may hold values from -6 to 6
- cotangent: bfloat16 [4, 512, 64, 384], P('dp', 'rows'), may hold values from -6 to 6
- weight_one: bfloat16 [3456, 384], replicated, may hold values from -0.109375 to 0.109375
- weight_two: bfloat16 [3456, 384], replicated, may hold values from -0.109375 to 0.109375
Outputs:
- output: bfloat16 [4, 512, 64, 384], P('dp', 'rows')
- grad_one: float32 [3456, 384], P('rows', 'dp')
- grad_two: float32 [3456, 384], P('rows', 'dp')
All inputs are finite; a program needn't handle non-finite values.
Results may differ from a plain program's by a relative error of at most 0.006.
Values may be sent and summed in bfloat16 or wider, within the bound.
A program may use at most 192 MiB of HBM per device.

v0:
```python
import math

import jax
import jax.numpy as jnp
from jax import lax
from jax.sharding import PartitionSpec as P


def padded_2(block, sides, width):
    for axis, dim in sides:
        count = lax.axis_size(axis)
        forward = [(i, i + 1) for i in range(count - 1)]
        backward = [(target, source) for source, target in forward]
        low = lax.ppermute(
            lax.slice_in_dim(block, block.shape[dim] - width, None, axis=dim), axis, forward
        )
        high = lax.ppermute(lax.slice_in_dim(block, 0, width, axis=dim), axis, backward)
        block = jnp.concatenate([low, block, high], axis=dim)
    return block


def tap_window(padded, frame, tap_number):
    count_rows, count_cols, pad_rows, pad_cols, step_rows, step_cols, direction = frame
    offset_row = tap_number // 3 - 1
    offset_col = tap_number % 3 - 1
    first_row = pad_rows + direction * offset_row * step_rows
    first_col = pad_cols + direction * offset_col * step_cols
    window = padded[first_row : first_row + count_rows, first_col : first_col + count_cols, :]
    return window.reshape(-1, padded.shape[-1])


def conv_taps(padded, frame, weights, transposed):
    channel_count = padded.shape[-1]
    summed = None
    for tap_number in range(9):
        window = tap_window(padded, frame, tap_number)
        kernel_block = weights[tap_number * channel_count : (tap_number + 1) * channel_count]
        if transposed:
            product = lax.dot_general(
                window, kernel_block, (((1,), (1,)), ((), ())), preferred_element_type=jnp.float32
            )
        else:
            product = jnp.dot(window, kernel_block, preferred_element_type=jnp.float32)
        summed = product if summed is None else summed + product
    return summed


def grad_taps(padded, frame, target):
    blocks = []
    for tap_number in range(9):
        window = tap_window(padded, frame, tap_number)
        blocks.append(
            lax.dot_general(
                window, target, (((0,), (0,)), ((), ())), preferred_element_type=jnp.float32
            )
        )
    return jnp.concatenate(blocks, axis=0)


def reduce_grad(partial_grad):
    shared = lax.psum_scatter(partial_grad, "rows", scatter_dimension=0, tiled=True)
    return lax.psum_scatter(shared, "dp", scatter_dimension=1, tiled=True)


def on_device(inputs, cotangent, weight_one, weight_two):
    picture = inputs[0]
    upstream_gradient = cotangent[0]
    row_count, col_count, channel_count = picture.shape
    group_size = lax.axis_size("rows")
    spacing = 2 * group_size
    factor = 1.0 / math.sqrt(lax.axis_size("dp") * row_count * group_size * col_count)
    rimmed = padded_2(picture, (("rows", 0),), 4)
    rimmed = jnp.pad(rimmed, ((0, 0), (4, 4), (0, 0)))
    near_frame = (row_count, col_count, 4, 4, 4, 4, 1)
    before = conv_taps(rimmed, near_frame, weight_one, False)
    hidden_state = (
        jnp.maximum(before, 0.0).astype(jnp.bfloat16).reshape(row_count, col_count, channel_count)
    )
    widths = ((0, 0), (spacing, spacing), (0, 0))
    hidden_pad = jnp.pad(padded_2(hidden_state, (("rows", 0),), spacing), widths)
    far_frame = (row_count, col_count, spacing, spacing, spacing, spacing, 1)
    output = (
        conv_taps(hidden_pad, far_frame, weight_two, False)
        .astype(jnp.bfloat16)
        .reshape(row_count, col_count, channel_count)
    )
    grad_two = reduce_grad(
        grad_taps(hidden_pad, far_frame, upstream_gradient.reshape(-1, channel_count))
    )
    upstream_pad = jnp.pad(padded_2(upstream_gradient, (("rows", 0),), spacing), widths)
    mirror_frame = (row_count, col_count, spacing, spacing, spacing, spacing, -1)
    backward_signal = conv_taps(upstream_pad, mirror_frame, weight_two, True).astype(jnp.bfloat16)
    masked = jnp.where(before > 0.0, backward_signal, jnp.zeros_like(backward_signal))
    grad_one = reduce_grad(grad_taps(rimmed, near_frame, masked))
    return (output[None], grad_one * factor, grad_two * factor)


def solution(mesh):
    return jax.shard_map(
        on_device,
        mesh=mesh,
        in_specs=(P("dp", "rows", None, None), P("dp", "rows", None, None), P(), P()),
        out_specs=(P("dp", "rows", None, None), P("rows", "dp"), P("rows", "dp")),
        check_vma=False,
    )
```

profile of v0, /device:TPU:0, one launch (start us, length us, event | category | flops | bytes accessed | tf_op | source)
XLA Modules:
  0.0 409.1 jit_solution(5628201466334399325)
XLA Ops:
  14.6 5.2 %collective-permute-start.4 = (bf16[16,64,384]{2,1,0:T(8,128)(2,1)}, bf16[16,64,384]{2,1,0:T(8,128)(2,1)S(1)}, u32[]{:S(2)}, u32[]{:S(2)}) collective-permute-start(bf16[16,64,384]{2,1,0:T(8,128)(2,1)} %get-tuple-element.30), channel_id=1, source_target_pairs={{0,1},{1,2},{2,3},{3,4},{4,5},{5,6},{6,7},{8,9},{9,10},{10,11},{11... | collective-permute-start | bytes 2359304 | tf_op jit(solution)/shard_map/ppermute | solution.py:14
  21.2 5.9 %fusion.16 = f32[4096,384]{1,0:T(8,128)} fusion(bf16[4096,384]{1,0:T(8,128)(2,1)S(1)} %bitcast.125, bf16[3456,384]{1,0:T(8,128)(2,1)} %param.6), kind=kOutput, calls=%fused_computation.55 | convolution fusion | flops 1207959552 | bytes 9732096 | tf_op jit(solution)/shard_map/dot_general | solution.py:43
  27.0 5.7 %fusion.46 = f32[4096,384]{1,0:T(8,128)} fusion(bf16[4096,384]{1,0:T(8,128)(2,1)S(1)} %bitcast.113, bf16[3456,384]{1,0:T(8,128)(2,1)} %param.7), kind=kOutput, calls=%fused_computation.81 | convolution fusion | flops 1207959552 | bytes 9732096 | tf_op jit(solution)/shard_map/dot_general | solution.py:39
  32.8 4.4 %fusion.7 = bf16[72,72,384]{2,1,0:T(8,128)(2,1)S(1)} fusion(bf16[4,64,384]{2,1,0:T(8,128)(2,1)S(1)} %collective-permute-done.1, bf16[64,64,384]{2,1,0:T(8,128)(2,1)S(1)} %bitcast.126, bf16[4,64,384]{2,1,0:T(8,128)(2,1)S(1)} %collective-permute-done), kind=kLoop, calls=%fused_computation.20 | loop fusion | flops 23887872 | bytes 7520256 | tf_op jit(solution)/shard_map/concatenate | solution.py:18
  37.2 7.5 %fusion.68 = (bf16[64,64,384]{2,1,0:T(8,128)(2,1)}, bf16[64,64,384]{2,1,0:T(8,128)(2,1)}, bf16[64,64,384]{2,1,0:T(8,128)(2,1)}, bf16[64,64,384]{2,1,0:T(8,128)(2...) fusion(bf16[72,72,384]{2,1,0:T(8,128)(2,1)S(1)} %fusion.7), kind=kLoop, calls=%fused_computation.107 | loop fusion | bytes 37748736 | tf_op jit(solution)/shard_map/slice | solution.py:28
  44.7 6.7 %fusion.12 = f32[4096,384]{1,0:T(8,128)} fusion(bf16[4096,384]{1,0:T(8,128)(2,1)} %bitcast.133, bf16[3456,384]{1,0:T(8,128)(2,1)S(1)} %copy-done.39), kind=kOutput, calls=%fused_computation.51 | convolution fusion | flops 1207959552 | bytes 9732096 | tf_op jit(solution)/shard_map/dot_general | solution.py:43
  51.4 4.8 %fusion.14 = f32[4096,384]{1,0:T(8,128)} fusion(bf16[4096,384]{1,0:T(8,128)(2,1)S(1)} %bitcast.135, bf16[3456,384]{1,0:T(8,128)(2,1)S(1)} %copy-done.39), kind=kOutput, calls=%fused_computation.53 | convolution fusion | flops 1207959552 | bytes 9732096 | tf_op jit(solution)/shard_map/dot_general | solution.py:43
  56.2 4.8 %fusion.18 = f32[4096,384]{1,0:T(8,128)} fusion(bf16[4096,384]{1,0:T(8,128)(2,1)S(1)} %bitcast.137, bf16[3456,384]{1,0:T(8,128)(2,1)S(1)} %copy-done.39), kind=kOutput, calls=%fused_computation.57 | convolution fusion | flops 1207959552 | bytes 9732096 | tf_op jit(solution)/shard_map/dot_general | solution.py:43
  61.1 4.9 %fusion.20 = f32[4096,384]{1,0:T(8,128)} fusion(bf16[4096,384]{1,0:T(8,128)(2,1)S(1)} %bitcast.139, bf16[3456,384]{1,0:T(8,128)(2,1)S(1)} %copy-done.39), kind=kOutput, calls=%fused_computation.59 | convolution fusion | flops 1207959552 | bytes 9732096 | tf_op jit(solution)/shard_map/dot_general | solution.py:43
  65.9 4.8 %fusion.24 = f32[4096,384]{1,0:T(8,128)} fusion(bf16[4096,384]{1,0:T(8,128)(2,1)S(1)} %bitcast.142, bf16[3456,384]{1,0:T(8,128)(2,1)S(1)} %copy-done.39), kind=kOutput, calls=%fused_computation.63 | convolution fusion | flops 1207959552 | bytes 9732096 | tf_op jit(solution)/shard_map/dot_general | solution.py:43
  70.7 5.2 %fusion.9 = f32[4096,384]{1,0:T(8,128)} fusion(bf16[4096,384]{1,0:T(8,128)(2,1)S(1)} %bitcast.131, bf16[3456,384]{1,0:T(8,128)(2,1)S(1)} %copy-done.39), kind=kOutput, calls=%fused_computation.48 | convolution fusion | flops 1207959552 | bytes 9732096 | tf_op jit(solution)/shard_map/dot_general | solution.py:43
  76.7 5.9 %fusion.22 = f32[4096,384]{1,0:T(8,128)} fusion(bf16[4096,384]{1,0:T(8,128)(2,1)S(1)} %bitcast.162, bf16[3456,384]{1,0:T(8,128)(2,1)} %param.6), kind=kOutput, calls=%fused_computation.61 | convolution fusion | flops 1207959552 | bytes 9732096 | tf_op jit(solution)/shard_map/dot_general | solution.py:43
  82.6 19.9 %maximum_convert_fusion = (bf16[4096,384]{1,0:T(8,128)(2,1)S(1)}, f32[4096,384]{1,0:T(8,128)}) fusion(f32[4096,384]{1,0:T(8,128)} %fusion.9, bf16[4096,384]{1,0:T(8,128)(2,1)S(1)} %bitcast.167, bf16[3456,384]{1,0:T(8,128)(2,1)} %param.6, f32[4096,384]{1,0:T(8,128)} %fusion.12, f32[4096,384]{1,0:T(8,128)} %fusion.14, f32[4096,384]{1,0:T(8,128)} %fusion.16, ...), kind=kOutput, calls=%fused_computation.13 | convolution fusion | flops 1223688192 | bytes 63209472 | tf_op jit(solution)/shard_map/dot_general | solution.py:43
  102.5 8.7 %select_maximum_fusion = bf16[96,96,384]{2,1,0:T(8,128)(2,1)S(1)} fusion(bf16[16,64,384]{2,1,0:T(8,128)(2,1)S(1)} %collective-permute-done.5, bf16[64,64,384]{2,1,0:T(8,128)(2,1)S(1)} %bitcast.114, bf16[16,64,384]{2,1,0:T(8,128)(2,1)S(1)} %collective-permute-done.4), kind=kLoop, calls=%fused_computation.6 | loop fusion | flops 42467328 | bytes 11796480 | tf_op jit(solution)/shard_map/concatenate | solution.py:18
  111.2 7.2 %fusion.66 = (bf16[64,64,384]{2,1,0:T(8,128)(2,1)}, bf16[64,64,384]{2,1,0:T(8,128)(2,1)}, bf16[64,64,384]{2,1,0:T(8,128)(2,1)}, bf16[64,64,384]{2,1,0:T(8,128)(2...) fusion(bf16[96,96,384]{2,1,0:T(8,128)(2,1)S(1)} %select_maximum_fusion), kind=kLoop, calls=%fused_computation.105 | loop fusion | bytes 37748736 | tf_op jit(solution)/shard_map/slice | solution.py:28
  118.5 6.8 %fusion.38 = f32[4096,384]{1,0:T(8,128)} fusion(bf16[4096,384]{1,0:T(8,128)(2,1)} %bitcast.157, bf16[3456,384]{1,0:T(8,128)(2,1)} %param.7), kind=kOutput, calls=%fused_computation.73 | convolution fusion | flops 1207959552 | bytes 9732096 | tf_op jit(solution)/shard_map/dot_general | solution.py:39
  125.3 4.7 %fusion.42 = f32[4096,384]{1,0:T(8,128)} fusion(bf16[4096,384]{1,0:T(8,128)(2,1)S(1)} %bitcast.156, bf16[3456,384]{1,0:T(8,128)(2,1)S(1)} %copy-done.37), kind=kOutput, calls=%fused_computation.77 | convolution fusion | flops 1207959552 | bytes 9732096 | tf_op jit(solution)/shard_map/dot_general | solution.py:39
  130.0 4.8 %fusion.50 = f32[4096,384]{1,0:T(8,128)} fusion(bf16[4096,384]{1,0:T(8,128)(2,1)S(1)} %bitcast.155, bf16[3456,384]{1,0:T(8,128)(2,1)S(1)} %copy-done.37), kind=kOutput, calls=%fused_computation.85 | convolution fusion | flops 1207959552 | bytes 9732096 | tf_op jit(solution)/shard_map/dot_general | solution.py:39
  134.8 4.8 %fusion.54 = f32[4096,384]{1,0:T(8,128)} fusion(bf16[4096,384]{1,0:T(8,128)(2,1)S(1)} %bitcast.154, bf16[3456,384]{1,0:T(8,128)(2,1)S(1)} %copy-done.37), kind=kOutput, calls=%fused_computation.89 | convolution fusion | flops 1207959552 | bytes 9732096 | tf_op jit(solution)/shard_map/dot_general | solution.py:39
  139.7 4.7 %fusion.62 = f32[4096,384]{1,0:T(8,128)} fusion(bf16[4096,384]{1,0:T(8,128)(2,1)S(1)} %bitcast.153, bf16[3456,384]{1,0:T(8,128)(2,1)S(1)} %copy-done.37), kind=kOutput, calls=%fused_computation.97 | convolution fusion | flops 1207959552 | bytes 9732096 | tf_op jit(solution)/shard_map/dot_general | solution.py:39
  145.6 4.8 %fusion.34 = f32[4096,384]{1,0:T(8,128)} fusion(bf16[4096,384]{1,0:T(8,128)(2,1)S(1)} %bitcast.165, bf16[3456,384]{1,0:T(8,128)(2,1)S(1)} %copy-done.37), kind=kOutput, calls=%fused_computation.69 | convolution fusion | flops 1207959552 | bytes 9732096 | tf_op jit(solution)/shard_map/dot_general | solution.py:39
  150.4 4.7 %fusion.58 = f32[4096,384]{1,0:T(8,128)} fusion(bf16[4096,384]{1,0:T(8,128)(2,1)S(1)} %bitcast.164, bf16[3456,384]{1,0:T(8,128)(2,1)S(1)} %copy-done.37), kind=kOutput, calls=%fused_computation.93 | convolution fusion | flops 1207959552 | bytes 9732096 | tf_op jit(solution)/shard_map/dot_general | solution.py:39
  155.1 20.0 %compare_select_fusion = bf16[4096,384]{1,0:T(8,128)(2,1)} fusion(f32[4096,384]{1,0:T(8,128)} %get-tuple-element.40, f32[4096,384]{1,0:T(8,128)} %fusion.34, f32[4096,384]{1,0:T(8,128)} %fusion.38, f32[4096,384]{1,0:T(8,128)} %fusion.42, f32[4096,384]{1,0:T(8,128)S(1)} %bitcast.130, f32[4096,384]{1,0:T(8,128)} %fusion.50, f32[4096,384]{1,0:T(8,128)} %fusion.54, ...), kind=kOutput, calls=%fused_computation.15 | convolution fusion | flops 1225261056 | bytes 63209472 | tf_op jit(solution)/shard_map/dot_general | solution.py:39
  175.1 5.6 %convolution_dynamic-update-slice_fusion.16 = f32[3456,384]{1,0:T(8,128)} fusion(bf16[4096,384]{1,0:T(8,128)(2,1)} %bitcast.141, bf16[4096,384]{1,0:T(8,128)(2,1)} %compare_select_fusion), kind=kOutput, calls=%fused_computation.43 | convolution fusion | flops 1207959552 | bytes 6881280 | tf_op jit(solution)/shard_map/dot_general | solution.py:53
  186.0 2.7 convolution_dynamic-update-slice_fusion.13
  188.8 2.7 fusion.8
  199.4 2.7 convolution_dynamic-update-slice_fusion.9
  202.3 4.3 %collective-permute-start.2 = (bf16[16,64,384]{2,1,0:T(8,128)(2,1)S(1)}, bf16[16,64,384]{2,1,0:T(8,128)(2,1)S(1)}, u32[]{:S(2)}, u32[]{:S(2)}) collective-permute-start(bf16[16,64,384]{2,1,0:T(8,128)(2,1)S(1)} %bitcast.175), channel_id=1, source_target_pairs={{0,1},{1,2},{2,3},{3,4},{4,5},{5,6},{6,7},{8,9},{9,10},{10,11},{11... | collective-permute-start | bytes 2359304 | tf_op jit(solution)/shard_map/ppermute | solution.py:14
  208.4 3.5 collective-permute-done.3
  211.9 3.2 pad_maximum_fusion.3
  215.2 8.7 %select_maximum_fusion.2 = bf16[96,96,384]{2,1,0:T(8,128)(2,1)S(1)} fusion(bf16[16,64,384]{2,1,0:T(8,128)(2,1)S(1)} %collective-permute-done.3, bf16[64,64,384]{2,1,0:T(8,128)(2,1)S(1)} %bitcast.112, bf16[16,64,384]{2,1,0:T(8,128)(2,1)S(1)} %collective-permute-done.2), kind=kLoop, calls=%fused_computation.8 | loop fusion | flops 42467328 | bytes 11796480 | tf_op jit(solution)/shard_map/concatenate | solution.py:18
  223.9 7.1 %fusion.67 = (bf16[64,64,384]{2,1,0:T(8,128)(2,1)}, bf16[64,64,384]{2,1,0:T(8,128)(2,1)}, bf16[64,64,384]{2,1,0:T(8,128)(2,1)}, bf16[64,64,384]{2,1,0:T(8,128)(2...) fusion(bf16[96,96,384]{2,1,0:T(8,128)(2,1)S(1)} %select_maximum_fusion.2), kind=kLoop, calls=%fused_computation.106 | loop fusion | bytes 37748736 | tf_op jit(solution)/shard_map/slice | solution.py:28
  231.0 4.7 %convolution_dynamic-update-slice_fusion.8 = f32[3456,384]{1,0:T(8,128)} fusion(bf16[4096,384]{1,0:T(8,128)(2,1)} %bitcast.143, bf16[4096,384]{1,0:T(8,128)(2,1)S(1)} %bitcast.116), kind=kOutput, calls=%fused_computation.35 | convolution fusion | flops 1207959552 | bytes 6881280 | tf_op jit(solution)/shard_map/dot_general | solution.py:53
  235.7 2.7 convolution_dynamic-update-slice_fusion.7
  238.4 2.7 convolution_dynamic-update-slice_fusion.6
  243.7 2.7 convolution_dynamic-update-slice_fusion.4
  257.3 5.8 %fusion.48 = f32[4096,384]{1,0:T(8,128)} fusion(bf16[4096,384]{1,0:T(8,128)(2,1)S(1)} %get-tuple-element.39, bf16[3456,384]{1,0:T(8,128)(2,1)} %param.7), kind=kOutput, calls=%fused_computation.83 | convolution fusion | flops 1207959552 | bytes 9732096 | tf_op jit(solution)/shard_map/dot_general | solution.py:43
  263.1 6.0 %fusion.40 = f32[4096,384]{1,0:T(8,128)} fusion(bf16[4096,384]{1,0:T(8,128)(2,1)S(1)} %bitcast.152, bf16[3456,384]{1,0:T(8,128)(2,1)} %param.7), kind=kOutput, calls=%fused_computation.75 | convolution fusion | flops 1207959552 | bytes 9732096 | tf_op jit(solution)/shard_map/dot_general | solution.py:43
  269.1 5.9 %fusion.44 = f32[4096,384]{1,0:T(8,128)} fusion(bf16[4096,384]{1,0:T(8,128)(2,1)S(1)} %bitcast.150, bf16[3456,384]{1,0:T(8,128)(2,1)} %param.7), kind=kOutput, calls=%fused_computation.79 | convolution fusion | flops 1207959552 | bytes 9732096 | tf_op jit(solution)/shard_map/dot_general | solution.py:43
  275.0 5.9 %fusion.52 = f32[4096,384]{1,0:T(8,128)} fusion(bf16[4096,384]{1,0:T(8,128)(2,1)S(1)} %bitcast.148, bf16[3456,384]{1,0:T(8,128)(2,1)} %param.7), kind=kOutput, calls=%fused_computation.87 | convolution fusion | flops 1207959552 | bytes 9732096 | tf_op jit(solution)/shard_map/dot_general | solution.py:43
  280.9 6.0 %fusion.56 = f32[4096,384]{1,0:T(8,128)} fusion(bf16[4096,384]{1,0:T(8,128)(2,1)S(1)} %bitcast.146, bf16[3456,384]{1,0:T(8,128)(2,1)} %param.7), kind=kOutput, calls=%fused_computation.91 | convolution fusion | flops 1207959552 | bytes 9732096 | tf_op jit(solution)/shard_map/dot_general | solution.py:43
  289.5 5.9 %fusion.64 = f32[4096,384]{1,0:T(8,128)} fusion(bf16[4096,384]{1,0:T(8,128)(2,1)S(1)} %bitcast.144, bf16[3456,384]{1,0:T(8,128)(2,1)} %param.7), kind=kOutput, calls=%fused_computation.99 | convolution fusion | flops 1207959552 | bytes 9732096 | tf_op jit(solution)/shard_map/dot_general | solution.py:43
  295.5 5.9 %fusion.36 = f32[4096,384]{1,0:T(8,128)} fusion(bf16[4096,384]{1,0:T(8,128)(2,1)S(1)} %bitcast.161, bf16[3456,384]{1,0:T(8,128)(2,1)} %param.7), kind=kOutput, calls=%fused_computation.71 | convolution fusion | flops 1207959552 | bytes 9732096 | tf_op jit(solution)/shard_map/dot_general | solution.py:43
  301.4 5.9 %fusion.60 = f32[4096,384]{1,0:T(8,128)} fusion(bf16[4096,384]{1,0:T(8,128)(2,1)S(1)} %bitcast.159, bf16[3456,384]{1,0:T(8,128)(2,1)} %param.7), kind=kOutput, calls=%fused_computation.95 | convolution fusion | flops 1207959552 | bytes 9732096 | tf_op jit(solution)/shard_map/dot_general | solution.py:43
  307.3 36.7 %reduce-scatter.11.cloned.1.call-done = f32[432,384]{1,0:T(8,128)} async-done(((f32[3456,384]{1,0:T(8,128)}), f32[432,384]{1,0:T(8,128)}) %reduce-scatter.11.cloned.1.call-update) | async-done | bytes 663568 | tf_op jit(solution)/shard_map/reduce_scatter | solution.py:61
  346.3 19.4 %add_convert_fusion.1 = bf16[4096,384]{1,0:T(8,128)(2,1)} fusion(f32[4096,384]{1,0:T(8,128)} %fusion.36, f32[4096,384]{1,0:T(8,128)} %fusion.40, f32[4096,384]{1,0:T(8,128)} %fusion.44, f32[4096,384]{1,0:T(8,128)} %fusion.48, f32[4096,384]{1,0:T(8,128)} %fusion.52, f32[4096,384]{1,0:T(8,128)} %fusion.56, f32[4096,384]{1,0:T(8,128)} %fusion.64, ...), kind=kOutput, calls=%fused_computation.12 | convolution fusion | flops 1222115328 | bytes 56918016 | tf_op jit(solution)/shard_map/dot_general | solution.py:43
  365.7 5.7 %reduce-scatter.13.cloned.1.call-done = f32[96,432]{1,0:T(8,128)} async-done(((f32[384,432]{1,0:T(8,128)}), f32[96,432]{1,0:T(8,128)}) %reduce-scatter.13.cloned.1.call-update) | async-done | bytes 165904
  373.2 27.0 %reduce-scatter.15.cloned.1.call-done = f32[96,432]{1,0:T(8,128)} async-done(((f32[384,432]{1,0:T(8,128)}), f32[96,432]{1,0:T(8,128)}) %reduce-scatter.15.cloned.1.call-update) | async-done | bytes 165904
  (126 shorter events, 48.1 us)
Async XLA Ops:
  7.2 14.0 %copy-start.2 = (bf16[1,64,64,384]{3,2,1,0:T(8,128)(2,1)S(1)}, bf16[1,64,64,384]{3,2,1,0:T(8,128)(2,1)}, u32[]{:S(2)}) copy-start(bf16[1,64,64,384]{3,2,1,0:T(8,128)(2,1)} %param.4) | copy-start | bytes 9437188
  7.2 279.7 %reduce-scatter.9.cloned.1.call-start = ((), (), s32[]{:S(2)}) async-start(), calls=%async_computation.4 | async-start | bytes 5971968 | tf_op jit(solution)/shard_map/reduce_scatter | solution.py:61
  8.4 24.3 %collective-permute-start = (bf16[4,64,384]{2,1,0:T(8,128)(2,1)S(1)}, bf16[4,64,384]{2,1,0:T(8,128)(2,1)S(1)}, u32[]{:S(2)}, u32[]{:S(2)}) collective-permute-start(bf16[4,64,384]{2,1,0:T(8,128)(2,1)S(1)} %get-tuple-element.37), channel_id=1, source_target_pairs={{0,1},{1,2},{2,3},{3,4},{4,5},{5,6},{6,7},{8,9},{9,10},{10,11},{11... | collective-permute-start | bytes 589832 | tf_op jit(solution)/shard_map/ppermute | solution.py:14
  10.8 22.0 %collective-permute-start.1 = (bf16[4,64,384]{2,1,0:T(8,128)(2,1)S(1)}, bf16[4,64,384]{2,1,0:T(8,128)(2,1)S(1)}, u32[]{:S(2)}, u32[]{:S(2)}) collective-permute-start(bf16[4,64,384]{2,1,0:T(8,128)(2,1)S(1)} %get-tuple-element.38), channel_id=1, source_target_pairs={{1,0},{2,1},{3,2},{4,3},{5,4},{6,5},{7,6},{9,8},{10,9},{11,10},{12... | collective-permute-start | bytes 589832 | tf_op jit(solution)/shard_map/ppermute | solution.py:17
  14.6 87.9 %collective-permute-start.4 = (bf16[16,64,384]{2,1,0:T(8,128)(2,1)}, bf16[16,64,384]{2,1,0:T(8,128)(2,1)S(1)}, u32[]{:S(2)}, u32[]{:S(2)}) collective-permute-start(bf16[16,64,384]{2,1,0:T(8,128)(2,1)} %get-tuple-element.30), channel_id=1, source_target_pairs={{0,1},{1,2},{2,3},{3,4},{4,5},{5,6},{6,7},{8,9},{9,10},{10,11},{11... | collective-permute-start | bytes 2359304 | tf_op jit(solution)/shard_map/ppermute | solution.py:14
  19.9 82.6 %collective-permute-start.5 = (bf16[16,64,384]{2,1,0:T(8,128)(2,1)S(1)}, bf16[16,64,384]{2,1,0:T(8,128)(2,1)S(1)}, u32[]{:S(2)}, u32[]{:S(2)}) collective-permute-start(bf16[16,64,384]{2,1,0:T(8,128)(2,1)S(1)} %get-tuple-element.29), channel_id=1, source_target_pairs={{1,0},{2,1},{3,2},{4,3},{5,4},{6,5},{7,6},{9,8},{10,9},{11,10},{12... | collective-permute-start | bytes 2359304 | tf_op jit(solution)/shard_map/ppermute | solution.py:17
  21.2 5.9 %copy-start = (bf16[1,64,64,384]{3,2,1,0:T(8,128)(2,1)S(1)}, bf16[1,64,64,384]{3,2,1,0:T(8,128)(2,1)}, u32[]{:S(2)}) copy-start(bf16[1,64,64,384]{3,2,1,0:T(8,128)(2,1)} %param.5) | copy-start | bytes 9437188
  37.2 7.5 %copy-start.39 = (bf16[3456,384]{1,0:T(8,128)(2,1)S(1)}, bf16[3456,384]{1,0:T(8,128)(2,1)}, u32[]{:S(2)}) copy-start(bf16[3456,384]{1,0:T(8,128)(2,1)} %param.6) | copy-start | bytes 7962628
  44.7 6.7 %copy-start.7 = (bf16[64,64,384]{2,1,0:T(8,128)(2,1)S(1)}, bf16[64,64,384]{2,1,0:T(8,128)(2,1)}, u32[]{:S(2)}) copy-start(bf16[64,64,384]{2,1,0:T(8,128)(2,1)} %get-tuple-element.23) | copy-start | bytes 9437188
  51.4 4.8 %copy-start.9 = (bf16[64,64,384]{2,1,0:T(8,128)(2,1)S(1)}, bf16[64,64,384]{2,1,0:T(8,128)(2,1)}, u32[]{:S(2)}) copy-start(bf16[64,64,384]{2,1,0:T(8,128)(2,1)} %get-tuple-element.24) | copy-start | bytes 9437188
  56.2 4.8 %copy-start.11 = (bf16[64,64,384]{2,1,0:T(8,128)(2,1)S(1)}, bf16[64,64,384]{2,1,0:T(8,128)(2,1)}, u32[]{:S(2)}) copy-start(bf16[64,64,384]{2,1,0:T(8,128)(2,1)} %get-tuple-element.25) | copy-start | bytes 9437188
  61.1 4.9 %copy-start.13 = (bf16[64,64,384]{2,1,0:T(8,128)(2,1)S(1)}, bf16[64,64,384]{2,1,0:T(8,128)(2,1)}, u32[]{:S(2)}) copy-start(bf16[64,64,384]{2,1,0:T(8,128)(2,1)} %get-tuple-element.21) | copy-start | bytes 9437188
  65.9 4.8 %copy-start.4 = (bf16[64,64,384]{2,1,0:T(8,128)(2,1)S(1)}, bf16[64,64,384]{2,1,0:T(8,128)(2,1)}, u32[]{:S(2)}) copy-start(bf16[64,64,384]{2,1,0:T(8,128)(2,1)} %get-tuple-element.26) | copy-start | bytes 9437188
  76.6 5.9 %copy-start.31 = (bf16[64,64,384]{2,1,0:T(8,128)(2,1)}, bf16[64,64,384]{2,1,0:T(8,128)(2,1)S(1)}, u32[]{:S(2)}) copy-start(bf16[64,64,384]{2,1,0:T(8,128)(2,1)S(1)} %get-tuple-element.36) | copy-start | bytes 9437188
  76.7 5.9 %copy-start.33 = (bf16[64,64,384]{2,1,0:T(8,128)(2,1)}, bf16[64,64,384]{2,1,0:T(8,128)(2,1)S(1)}, u32[]{:S(2)}) copy-start(bf16[64,64,384]{2,1,0:T(8,128)(2,1)S(1)} %get-tuple-element.35) | copy-start | bytes 9437188
  118.4 6.9 %copy-start.26 = (bf16[64,64,384]{2,1,0:T(8,128)(2,1)S(1)}, bf16[64,64,384]{2,1,0:T(8,128)(2,1)}, u32[]{:S(2)}) copy-start(bf16[64,64,384]{2,1,0:T(8,128)(2,1)} %get-tuple-element.11) | copy-start | bytes 9437188
  118.5 6.8 %copy-start.37 = (bf16[3456,384]{1,0:T(8,128)(2,1)S(1)}, bf16[3456,384]{1,0:T(8,128)(2,1)}, u32[]{:S(2)}) copy-start(bf16[3456,384]{1,0:T(8,128)(2,1)} %param.7) | copy-start | bytes 7962628
  125.3 4.7 %copy-start.25 = (bf16[64,64,384]{2,1,0:T(8,128)(2,1)S(1)}, bf16[64,64,384]{2,1,0:T(8,128)(2,1)}, u32[]{:S(2)}) copy-start(bf16[64,64,384]{2,1,0:T(8,128)(2,1)} %get-tuple-element.12) | copy-start | bytes 9437188
  130.0 4.8 %copy-start.24 = (bf16[64,64,384]{2,1,0:T(8,128)(2,1)S(1)}, bf16[64,64,384]{2,1,0:T(8,128)(2,1)}, u32[]{:S(2)}) copy-start(bf16[64,64,384]{2,1,0:T(8,128)(2,1)} %get-tuple-element.13) | copy-start | bytes 9437188
  134.8 4.8 %copy-start.23 = (bf16[64,64,384]{2,1,0:T(8,128)(2,1)S(1)}, bf16[64,64,384]{2,1,0:T(8,128)(2,1)}, u32[]{:S(2)}) copy-start(bf16[64,64,384]{2,1,0:T(8,128)(2,1)} %get-tuple-element.14) | copy-start | bytes 9437188
  150.4 4.7 %slice-start = ((s8[6291456]{0:T(1024)(128)(4,1)}), s8[4194304]{0:T(1024)(128)(4,1)S(1)}, s32[]{:S(2)}) async-start(s8[6291456]{0:T(1024)(128)(4,1)} %bitcast.129), calls=%async_computation.8 | async-start | bytes 8388608
  150.4 4.7 %slice-start.1 = ((s8[6291456]{0:T(1024)(128)(4,1)}), s8[2097152]{0:T(1024)(128)(4,1)S(1)}, s32[]{:S(2)}) async-start(s8[6291456]{0:T(1024)(128)(4,1)} %bitcast.129), calls=%async_computation.9 | async-start | bytes 4194304
  175.1 5.6 %copy-start.32 = (bf16[64,64,384]{2,1,0:T(8,128)(2,1)S(1)}, bf16[64,64,384]{2,1,0:T(8,128)(2,1)}, u32[]{:S(2)}) copy-start(bf16[64,64,384]{2,1,0:T(8,128)(2,1)} %copy-done.31) | copy-start | bytes 9437188
  175.1 5.6 %copy-start.38 = (bf16[4096,384]{1,0:T(8,128)(2,1)S(1)}, bf16[4096,384]{1,0:T(8,128)(2,1)}, u32[]{:S(2)}) copy-start(bf16[4096,384]{1,0:T(8,128)(2,1)} %compare_select_fusion) | copy-start | bytes 9437188
  180.7 2.7 copy-start.12
  183.4 2.7 copy-start.10
  186.0 2.7 copy-start.3
  188.8 2.7 copy-start.8
  194.1 2.7 copy-start.34
  202.1 141.9 %reduce-scatter.11.cloned.1.call-start = ((), (), s32[]{:S(2)}) async-start(), calls=%async_computation.5 | async-start | bytes 5971968 | tf_op jit(solution)/shard_map/reduce_scatter | solution.py:61
  202.3 6.1 %collective-permute-start.2 = (bf16[16,64,384]{2,1,0:T(8,128)(2,1)S(1)}, bf16[16,64,384]{2,1,0:T(8,128)(2,1)S(1)}, u32[]{:S(2)}, u32[]{:S(2)}) collective-permute-start(bf16[16,64,384]{2,1,0:T(8,128)(2,1)S(1)} %bitcast.175), channel_id=1, source_target_pairs={{0,1},{1,2},{2,3},{3,4},{4,5},{5,6},{6,7},{8,9},{9,10},{10,11},{11... | collective-permute-start | bytes 2359304 | tf_op jit(solution)/shard_map/ppermute | solution.py:14
  206.6 5.4 %collective-permute-start.3 = (bf16[16,64,384]{2,1,0:T(8,128)(2,1)S(1)}, bf16[16,64,384]{2,1,0:T(8,128)(2,1)S(1)}, u32[]{:S(2)}, u32[]{:S(2)}) collective-permute-start(bf16[16,64,384]{2,1,0:T(8,128)(2,1)S(1)} %bitcast.174), channel_id=1, source_target_pairs={{1,0},{2,1},{3,2},{4,3},{5,4},{6,5},{7,6},{9,8},{10,9},{11,10},{12... | collective-permute-start | bytes 2359304 | tf_op jit(solution)/shard_map/ppermute | solution.py:17
  223.9 7.1 %copy-start.1 = (bf16[1,64,64,384]{3,2,1,0:T(8,128)(2,1)S(1)}, bf16[1,64,64,384]{3,2,1,0:T(8,128)(2,1)}, u32[]{:S(2)}) copy-start(bf16[1,64,64,384]{3,2,1,0:T(8,128)(2,1)} %param.5) | copy-start | bytes 9437188
  231.0 4.7 %copy-start.27 = (bf16[64,64,384]{2,1,0:T(8,128)(2,1)S(1)}, bf16[64,64,384]{2,1,0:T(8,128)(2,1)}, u32[]{:S(2)}) copy-start(bf16[64,64,384]{2,1,0:T(8,128)(2,1)} %get-tuple-element.31) | copy-start | bytes 9437188
  235.7 2.7 copy-start.15
  238.4 2.7 copy-start.17
  243.7 2.7 copy-start.19
  246.4 2.7 copy-start.21
  257.0 114.4 %reduce-scatter.13.cloned.1.call-start = ((), (), s32[]{:S(2)}) async-start(), calls=%async_computation.6 | async-start | bytes 983040
  257.2 5.9 %copy-start.22 = (bf16[64,64,384]{2,1,0:T(8,128)(2,1)S(1)}, bf16[64,64,384]{2,1,0:T(8,128)(2,1)}, u32[]{:S(2)}) copy-start(bf16[64,64,384]{2,1,0:T(8,128)(2,1)} %get-tuple-element.16) | copy-start | bytes 9437188
  263.1 6.0 %copy-start.20 = (bf16[64,64,384]{2,1,0:T(8,128)(2,1)S(1)}, bf16[64,64,384]{2,1,0:T(8,128)(2,1)}, u32[]{:S(2)}) copy-start(bf16[64,64,384]{2,1,0:T(8,128)(2,1)} %get-tuple-element.17) | copy-start | bytes 9437188
  269.1 5.9 %copy-start.18 = (bf16[64,64,384]{2,1,0:T(8,128)(2,1)S(1)}, bf16[64,64,384]{2,1,0:T(8,128)(2,1)}, u32[]{:S(2)}) copy-start(bf16[64,64,384]{2,1,0:T(8,128)(2,1)} %get-tuple-element.18) | copy-start | bytes 9437188
  275.0 6.0 %copy-start.16 = (bf16[64,64,384]{2,1,0:T(8,128)(2,1)S(1)}, bf16[64,64,384]{2,1,0:T(8,128)(2,1)}, u32[]{:S(2)}) copy-start(bf16[64,64,384]{2,1,0:T(8,128)(2,1)} %get-tuple-element.19) | copy-start | bytes 9437188
  280.9 8.6 %copy-start.14 = (bf16[64,64,384]{2,1,0:T(8,128)(2,1)S(1)}, bf16[64,64,384]{2,1,0:T(8,128)(2,1)}, u32[]{:S(2)}) copy-start(bf16[64,64,384]{2,1,0:T(8,128)(2,1)} %get-tuple-element.20) | copy-start | bytes 9437188
  289.2 111.0 %reduce-scatter.15.cloned.1.call-start = ((), (), s32[]{:S(2)}) async-start(), calls=%async_computation.7 | async-start | bytes 983040
  289.5 5.9 %copy-start.30 = (bf16[64,64,384]{2,1,0:T(8,128)(2,1)S(1)}, bf16[64,64,384]{2,1,0:T(8,128)(2,1)}, u32[]{:S(2)}) copy-start(bf16[64,64,384]{2,1,0:T(8,128)(2,1)} %get-tuple-element.32) | copy-start | bytes 9437188
  295.4 5.9 %copy-start.28 = (bf16[64,64,384]{2,1,0:T(8,128)(2,1)S(1)}, bf16[64,64,384]{2,1,0:T(8,128)(2,1)}, u32[]{:S(2)}) copy-start(bf16[64,64,384]{2,1,0:T(8,128)(2,1)} %get-tuple-element.31) | copy-start | bytes 9437188
  301.4 44.9 %copy-start.36 = (bf16[64,64,384]{2,1,0:T(8,128)(2,1)S(1)}, bf16[64,64,384]{2,1,0:T(8,128)(2,1)}, u32[]{:S(2)}) copy-start(bf16[64,64,384]{2,1,0:T(8,128)(2,1)} %get-tuple-element.15) | copy-start | bytes 9437188
  (4 other events, 10.6 us)
Sparse Core Ops, SparseCore 0:
  202.2 72.4 reduce-scatter.8
  277.0 66.9 reduce-scatter.10
  346.9 24.4 reduce-scatter.12
  374.1 26.0 reduce-scatter.14
where the time goes:
time: 415 us; the launch traced here: 409 us
  matrix products  244 us (59%)
  waiting for transfers between devices  73.4 us (18%)
  local copies, waits for them, and re-layouts  34 us (8%)
  other arithmetic  27 us (7%)
  starting transfers between devices  16.4 us (4%)
  between operations  14.6 us (4%)
    dot_general x18, matrix products, conv_taps(): product = jnp.dot(window, kernel_block, preferred_element_type=jnp.float32)  130 us
    dot_general x9, matrix products, conv_taps(): lax.dot_general(window, kernel_block, (((1,), (1,)), ((), ())), preferred...  61.2 us
    dot_general x18, matrix products, grad_taps(): lax.dot_general(window, target, (((0,), (0,)), ((), ())), preferred_eleme...  52.8 us
    reduce_scatter x2, waiting for transfers between devices, reduce_grad(): lax.psum_scatter(partial_grad, 'rows', scatter_dimension=0, tiled=True)  36.7 us
    unnamed x6, waiting for transfers between devices  32.7 us
    concatenate x6, other arithmetic, padded_2(): block = jnp.concatenate([low, block, high], axis=dim)  26.9 us
    slice x3, local copies, waits for them, and re-layouts, tap_window(): padded[first_row:first_row + count_rows, first_col:first_col + count_cols...  21.8 us
    ppermute x3, starting transfers between devices, padded_2(): lax.ppermute(lax.slice_in_dim(block, block.shape[dim] - width, None, axis...  11.9 us
  transfers between devices with their start and end apart: 10, of which 5 were waited for; matrix products, arithmetic and copies ran while one was open for 49% of the time, Pallas kernels for 0%

commit v1 on v0

v1 whole, which is shorter than its diff:
```python
import functools
import math

import jax
import jax.numpy as jnp
from jax import lax
from jax.experimental import pallas as pl
from jax.experimental.pallas import tpu as pltpu
from jax.sharding import PartitionSpec as P

NEAR = 4
VMEM_LIMIT = 56 * 1024 * 1024
F32 = jnp.float32
BF16 = jnp.bfloat16


def edge_rows(block, width):
    count = lax.axis_size("rows")
    forward = [(i, i + 1) for i in range(count - 1)]
    backward = [(i + 1, i) for i in range(count - 1)]
    low = lax.ppermute(block[block.shape[0] - width :], "rows", forward)
    high = lax.ppermute(block[:width], "rows", backward)
    return low, high


def fill_padded(scratch, low, mid, high, margin):
    width, cols, channels = low.shape
    rows = mid.shape[0]
    side = jnp.zeros((scratch.shape[0], margin, channels), scratch.dtype)
    scratch[:, 0:margin, :] = side
    scratch[:, margin + cols : margin + cols + margin, :] = side
    scratch[0:width, margin : margin + cols, :] = low[...]
    scratch[width : width + rows, margin : margin + cols, :] = mid[...]
    scratch[width + rows : width + rows + width, margin : margin + cols, :] = high[...]


def fill_shifted(scratch, low, mid, high):
    width, cols, channels = low.shape
    rows = mid.shape[0]
    for ref, start, count in ((low, 0, width), (mid, width, rows), (high, width + rows, width)):

        @pl.loop(0, count)
        def _(r):
            line = ref[r].astype(F32)
            zero = jnp.zeros((NEAR, channels), F32)
            scratch[0, start + r] = jnp.concatenate([zero, line[: cols - NEAR]], axis=0).astype(BF16)
            scratch[1, start + r] = ref[r]
            scratch[2, start + r] = jnp.concatenate([line[NEAR:], zero], axis=0).astype(BF16)


def near_kernel(tile, low, mid, high, weight, hidden, shifted):
    step = pl.program_id(0)

    @pl.when(step == 0)
    def _():
        fill_shifted(shifted, low, mid, high)

    cols, channels = mid.shape[1:]
    pieces = []
    for a in range(3):
        for b in range(3):
            window = shifted[b, pl.ds(step * tile + a * NEAR, tile)]
            pieces.append(window.reshape(tile * cols, channels))
    before = jnp.dot(jnp.concatenate(pieces, axis=1), weight[...], preferred_element_type=F32)
    hidden[...] = jnp.maximum(before, 0.0).astype(BF16).reshape(tile, cols, channels)


def far_windows(padded, step, tile, spacing, cols, direction):
    pieces = []
    for a in (-1, 0, 1):
        for b in (-1, 0, 1):
            first_col = spacing + direction * b * spacing
            window = padded[
                pl.ds(step * tile + spacing + direction * a * spacing, tile),
                first_col : first_col + cols,
                :,
            ]
            pieces.append(window.reshape(tile * cols, padded.shape[-1]))
    return jnp.concatenate(pieces, axis=1)


def output_kernel(tile, spacing, low, mid, high, weight, out, padded):
    step = pl.program_id(0)

    @pl.when(step == 0)
    def _():
        fill_padded(padded, low, mid, high, spacing)

    cols, channels = mid.shape[1:]
    stacked = far_windows(padded, step, tile, spacing, cols, 1)
    result = jnp.dot(stacked, weight[...], preferred_element_type=F32)
    out[...] = result.astype(BF16).reshape(tile, cols, channels)


def back_kernel(tile, spacing, low, mid, high, weight, hidden, masked, padded, turned):
    step = pl.program_id(0)
    cols, channels = mid.shape[1:]

    @pl.when(step == 0)
    def _():
        fill_padded(padded, low, mid, high, spacing)
        for t in range(9):
            turned[t * channels : (t + 1) * channels, :] = weight[
                t * channels : (t + 1) * channels, :
            ].T

    stacked = far_windows(padded, step, tile, spacing, cols, -1)
    back = jnp.dot(stacked, turned[...], preferred_element_type=F32).astype(BF16)
    back = back.reshape(tile, cols, channels)
    masked[...] = jnp.where(hidden[...] > 0, back, jnp.zeros_like(back))


def far_grad_kernel(spacing, low, mid, high, hidden, out, padded, turned):
    tap = pl.program_id(0)
    rows, cols, channels = mid.shape

    @pl.when(tap == 0)
    def _():
        fill_padded(padded, low, mid, high, spacing)
        turned[...] = hidden[...].reshape(rows * cols, channels).T

    first_row = (2 - tap // 3) * spacing
    first_col = pl.multiple_of((2 - tap % 3) * spacing, 16)
    window = padded[pl.ds(first_row, rows), pl.ds(first_col, cols), :]
    out[...] = jnp.dot(
        turned[...], window.reshape(rows * cols, channels), preferred_element_type=F32
    )


def near_grad_kernel(low, mid, high, masked, out, shifted, turned):
    tap = pl.program_id(0)
    rows, cols, channels = mid.shape

    @pl.when(tap == 0)
    def _():
        fill_shifted(shifted, low, mid, high)
        turned[...] = masked[...].reshape(rows * cols, channels).T

    window = shifted[tap % 3, pl.ds((tap // 3) * NEAR, rows)]
    product = jnp.dot(
        turned[...], window.reshape(rows * cols, channels), preferred_element_type=F32
    )
    out[...] = product.T


def run(kernel, out_shape, grid, out_spec, scratch, args, specs, flops):
    whole = pl.BlockSpec(memory_space=pltpu.VMEM)
    return pl.pallas_call(
        kernel,
        out_shape=out_shape,
        grid=(grid,),
        in_specs=[whole if spec is None else spec for spec in specs],
        out_specs=out_spec,
        scratch_shapes=scratch,
        compiler_params=pltpu.CompilerParams(vmem_limit_bytes=VMEM_LIMIT),
        cost_estimate=pl.CostEstimate(
            flops=flops, bytes_accessed=12 * 1024 * 1024, transcendentals=0
        ),
    )(*args)


def halve(total, axis, bit):
    count = lax.axis_size(axis)
    mine = (lax.axis_index(axis) >> bit) & 1
    pairs = [(i, i ^ (1 << bit)) for i in range(count)]
    sent = lax.dynamic_index_in_dim(total, 1 - mine, 0, keepdims=False).astype(BF16)
    kept = lax.dynamic_index_in_dim(total, mine, 0, keepdims=False)
    return kept + lax.ppermute(sent, axis, pairs).astype(F32)


def reduce_grad(grad):
    rows, dp = lax.axis_size("rows"), lax.axis_size("dp")
    taps, channels = grad.shape
    height, width = taps // rows, channels // dp
    outer = rows // 2
    total = jnp.moveaxis(grad.reshape(outer, 2, height, channels), 1, 0)
    total = halve(total, "rows", 0).reshape(outer * height, channels).T
    for bit in reversed(range(dp.bit_length() - 1)):
        total = halve(total.reshape(2, total.shape[0] // 2, outer * height), "dp", bit)
    total = total.T.reshape(outer, height, width)
    for bit in reversed(range(1, rows.bit_length() - 1)):
        total = halve(total.reshape(2, total.shape[0] // 2, height, width), "rows", bit)
    return total.reshape(height, width)


def on_device(inputs, cotangent, weight_one, weight_two):
    picture, upstream = inputs[0], cotangent[0]
    rows, cols, channels = picture.shape
    group = lax.axis_size("rows")
    spacing = 2 * group
    factor = 1.0 / math.sqrt(lax.axis_size("dp") * rows * group * cols)
    flops = 2 * rows * cols * weight_one.shape[0] * channels
    tile = 8
    steps = rows // tile
    map_shape = jax.ShapeDtypeStruct((rows, cols, channels), BF16)
    map_spec = pl.BlockSpec((tile, cols, channels), lambda i: (i, 0, 0))
    grad_shape = jax.ShapeDtypeStruct(weight_one.shape, F32)
    grad_spec = pl.BlockSpec((channels, channels), lambda t: (t, 0))
    padded = pltpu.VMEM((rows + 2 * spacing, cols + 2 * spacing, channels), BF16)
    shifted = pltpu.VMEM((3, rows + 2 * NEAR, cols, channels), BF16)
    turned = pltpu.VMEM((channels, rows * cols), BF16)

    near_low, near_high = edge_rows(picture, NEAR)
    far_low, far_high = edge_rows(upstream, spacing)
    near = (near_low, picture, near_high)
    far = (far_low, upstream, far_high)

    hidden = run(
        functools.partial(near_kernel, tile),
        map_shape, steps, map_spec, [shifted],
        (*near, weight_one), [None] * 4, flops,
    )
    grad_two = run(
        functools.partial(far_grad_kernel, spacing),
        grad_shape, 9, grad_spec, [padded, turned],
        (*far, hidden), [None] * 4, flops,
    )
    masked = run(
        functools.partial(back_kernel, tile, spacing),
        map_shape, steps, map_spec, [padded, pltpu.VMEM(weight_two.shape, BF16)],
        (*far, weight_two, hidden), [None] * 4 + [map_spec], flops,
    )
    grad_one = run(
        near_grad_kernel,
        grad_shape, 9, grad_spec, [shifted, turned],
        (*near, masked), [None] * 4, flops,
    )
    hidden_low, hidden_high = edge_rows(hidden, spacing)
    output = run(
        functools.partial(output_kernel, tile, spacing),
        map_shape, steps, map_spec, [padded],
        (hidden_low, hidden, hidden_high, weight_two), [None] * 4, flops,
    )
    grad_two = reduce_grad(grad_two)
    grad_one = reduce_grad(grad_one)
    return (output[None], grad_one * factor, grad_two * factor)


def solution(mesh):
    return jax.shard_map(
        on_device,
        mesh=mesh,
        in_specs=(P("dp", "rows", None, None), P("dp", "rows", None, None), P(), P()),
        out_specs=(P("dp", "rows", None, None), P("rows", "dp"), P("rows", "dp")),
        check_vma=False,
    )
```

time: 415 us -> 204 us (0.49); the launches traced: 409 us -> 204 us
  matrix products: 244 us -> 0 us
  Pallas kernels: 0 us -> 109 us
  waiting for transfers between devices: 73.4 us -> 32.7 us
  other arithmetic: 27 us -> 8.35 us
  between operations: 14.6 us -> 0.85 us
  starting transfers between devices: 16.4 us -> 28.8 us
  local copies, waits for them, and re-layouts: 34 us -> 23.9 us
    dot_general x45 -> x0, matrix products: 244 us -> none  [the longest x18 130 us: conv_taps(): product = jnp.dot(window, kernel_block, preferred_element_type=jnp.float32)]
    pallas_call x0 -> x5, Pallas kernels: none -> 109 us  [run(): pl.pallas_call(kernel, out_shape=out_shape, grid=(grid,), in_specs=[whole...]
    reduce_scatter x2 -> x0, waiting for transfers between devices: 36.7 us -> none  [reduce_grad(): lax.psum_scatter(partial_grad, 'rows', scatter_dimension=0, tiled=True)]
    unnamed x6 -> x0, waiting for transfers between devices: 32.7 us -> none
    ppermute x6 -> x16, waiting for transfers between devices: 4.07 us -> 32.7 us  [the longest x10 32.7 us: halve(): return kept + lax.ppermute(sent, axis, pairs).astype(F32)]
    concatenate x6 -> x0, other arithmetic: 26.9 us -> none  [padded_2(): block = jnp.concatenate([low, block, high], axis=dim)]
    slice x6 -> x3, local copies, waits for them, and re-layouts: 25.6 us -> 5.02 us  [edge_rows(): high = lax.ppermute(block[:width], 'rows', backward)]
    ppermute x6 -> x16, starting transfers between devices: 15.8 us -> 28.8 us  [the longest x3 12.8 us: edge_rows(): low = lax.ppermute(block[block.shape[0] - width:], 'rows', forward)]
  transfers between devices with their start and end apart: 10 -> 16, of which waited for: 5 -> 6; matrix products, arithmetic and copies ran while one was open for 49% -> 14% of each run, Pallas kernels for 0% -> 54%
where the time goes in v1:
time: 204 us
  Pallas kernels  109 us (53%)
  waiting for transfers between devices  32.7 us (16%)
  starting transfers between devices  28.8 us (14%)
  local copies, waits for them, and re-layouts  23.9 us (12%)
  other arithmetic  8.35 us (4%)
    pallas_call x5, Pallas kernels, run(): pl.pallas_call(kernel, out_shape=out_shape, grid=(grid,), in_specs=[whole...  109 us
    ppermute x10, waiting for transfers between devices, halve(): return kept + lax.ppermute(sent, axis, pairs).astype(F32)  32.7 us
    ppermute x3, starting transfers between devices, edge_rows(): low = lax.ppermute(block[block.shape[0] - width:], 'rows', forward)  12.8 us
    ppermute x10, starting transfers between devices, halve(): return kept + lax.ppermute(sent, axis, pairs).astype(F32)  12 us
    convert_element_type x10, local copies, waits for them, and re-layouts, halve(): lax.dynamic_index_in_dim(total, 1 - mine, 0, keepdims=False).astype(BF16)  10.2 us
    add x6, other arithmetic, halve(): return kept + lax.ppermute(sent, axis, pairs).astype(F32)  7.48 us
    slice x3, local copies, waits for them, and re-layouts, edge_rows(): high = lax.ppermute(block[:width], 'rows', backward)  5.02 us
    transpose x2, local copies, waits for them, and re-layouts, reduce_grad(): total = halve(total, 'rows', 0).reshape(outer * height, channels).T  4.62 us
  transfers between devices with their start and end apart: 16, of which 6 were waited for; matrix products, arithmetic and copies ran while one was open for 14% of the time, Pallas kernels for 54%

profile of v1, /device:TPU:0, one launch (start us, length us, event | category | flops | bytes accessed | tf_op | source)
XLA Modules:
  0.0 203.7 jit_solution(14127344566461541333)
XLA Ops:
  0.6 1.1 slice_bitcast_fusion.2
  1.7 2.4 %collective-permute-start = (bf16[4,64,384]{2,1,0:T(8,128)(2,1)S(1)}, bf16[4,64,384]{2,1,0:T(8,128)(2,1)S(1)}, u32[]{:S(2)}, u32[]{:S(2)}) collective-permute-start(bf16[4,64,384]{2,1,0:T(8,128)(2,1)S(1)} %get-tuple-element.8), channel_id=1, source_target_pairs={{0,1},{1,2},{2,3},{3,4},{4,5},{5,6},{6,7},{8,9},{9,10},{10,11},{11... | collective-permute-start | bytes 589832 | tf_op jit(solution)/shard_map/ppermute | solution.py:21
  4.1 1.3 collective-permute-start.1
  5.4 1.5 slice_bitcast_fusion
  6.9 6.1 %collective-permute-start.4 = (bf16[16,64,384]{2,1,0:T(8,128)(2,1)S(1)}, bf16[16,64,384]{2,1,0:T(8,128)(2,1)}, u32[]{:S(2)}, u32[]{:S(2)}) collective-permute-start(bf16[16,64,384]{2,1,0:T(8,128)(2,1)S(1)} %get-tuple-element.4), channel_id=1, source_target_pairs={{0,1},{1,2},{2,3},{3,4},{4,5},{5,6},{6,7},{8,9},{9,10},{10,11},{11... | collective-permute-start | bytes 2359304 | tf_op jit(solution)/shard_map/ppermute | solution.py:21
  13.0 1.3 collective-permute-start.5
  14.4 0.6 copy-done.1
  15.1 21.1 %shard_map.67.mid.hidden = bf16[64,64,384]{2,1,0:T(8,128)(2,1)} custom-call(bf16[4,64,384]{2,1,0:T(8,128)(2,1)} %copy-done.1, bf16[64,64,384]{2,1,0:T(8,128)(2,1)} %bitcast.103, bf16[4,64,384]{2,1,0:T(8,128)(2,1)} %copy-done.2, bf16[3456,384]{1,0:T(8,128)(2,1)} %weight.3), custom_call_target="tpu_custom_call" | custom-call | flops 10871635968 | bytes 12582912 | tf_op jit(solution)/shard_map/pallas_call | solution.py:148
  36.1 2.4 %fusion.10 = (bf16[16,64,384]{2,1,0:T(8,128)(2,1)S(1)}, bf16[16,64,384]{2,1,0:T(8,128)(2,1)}) fusion(bf16[64,64,384]{2,1,0:T(8,128)(2,1)} %shard_map.67.mid.hidden), kind=kLoop, calls=%fused_computation.36 | loop fusion | bytes 3145728 | tf_op jit(solution)/shard_map/slice | solution.py:22
  38.6 4.3 %collective-permute-start.2 = (bf16[16,64,384]{2,1,0:T(8,128)(2,1)}, bf16[16,64,384]{2,1,0:T(8,128)(2,1)}, u32[]{:S(2)}, u32[]{:S(2)}) collective-permute-start(bf16[16,64,384]{2,1,0:T(8,128)(2,1)} %get-tuple-element.6), channel_id=1, source_target_pairs={{0,1},{1,2},{2,3},{3,4},{4,5},{5,6},{6,7},{8,9},{9,10},{10,11},{11... | collective-permute-start | bytes 2359304 | tf_op jit(solution)/shard_map/ppermute | solution.py:21
  42.8 1.5 collective-permute-start.3
  44.3 22.2 %shard_map.71 = f32[3456,384]{1,0:T(8,128)} custom-call(bf16[16,64,384]{2,1,0:T(8,128)(2,1)} %collective-permute-done.4.low, bf16[64,64,384]{2,1,0:T(8,128)(2,1)} %bitcast.99, bf16[16,64,384]{2,1,0:T(8,128)(2,1)} %collective-permute-done.5.high, bf16[64,64,384]{2,1,0:T(8,128)(2,1)} %shard_map.67.mid.hidden), custom_call_target="tpu_custom_call" | custom-call | flops 10871635968 | bytes 12582912 | tf_op jit(solution)/shard_map/pallas_call | solution.py:148
  66.5 1.9 fusion.1
  68.4 1.6 collective-permute-start.11
  70.0 21.7 %shard_map.69.masked = bf16[64,64,384]{2,1,0:T(8,128)(2,1)} custom-call(bf16[16,64,384]{2,1,0:T(8,128)(2,1)} %collective-permute-done.4.low, bf16[64,64,384]{2,1,0:T(8,128)(2,1)} %bitcast.100, bf16[16,64,384]{2,1,0:T(8,128)(2,1)} %collective-permute-done.5.high, bf16[3456,384]{1,0:T(8,128)(2,1)} %weight.5, bf16[64,64,384]{2,1,0:T(8,128)(2,1)} %shard_map.67.mid.hidden), custom_call_target="tpu_custom_call" | custom-call | flops 10871635968 | bytes 12582912 | tf_op jit(solution)/shard_map/pallas_call | solution.py:148
  91.6 23.4 %shard_map.70 = f32[3456,384]{1,0:T(8,128)} custom-call(bf16[4,64,384]{2,1,0:T(8,128)(2,1)} %copy-done.1, bf16[64,64,384]{2,1,0:T(8,128)(2,1)} %bitcast.104, bf16[4,64,384]{2,1,0:T(8,128)(2,1)} %copy-done.2, bf16[64,64,384]{2,1,0:T(8,128)(2,1)} %shard_map.69.masked), custom_call_target="tpu_custom_call" | custom-call | flops 10871635968 | bytes 12582912 | tf_op jit(solution)/shard_map/pallas_call | solution.py:148
  115.1 3.0 %fusion = bf16[4,432,384]{2,1,0:T(8,128)(2,1)} fusion(f32[4,2,432,384]{3,2,1,0:T(8,128)} %bitcast.95, s32[]{:T(128)S(6)} %select_n.46), kind=kLoop, calls=%fused_computation.8 | loop fusion | bytes 2654212 | tf_op jit(solution)/shard_map/convert_element_type | solution.py:166
  118.1 2.0 bitcast_add_fusion
  120.1 2.3 %copy.13 = f32[384,1728]{1,0:T(8,128)} copy(f32[384,1728]{0,1:T(8,128)S(1)} %bitcast.86) | data formatting | bytes 5308416 | tf_op jit(solution)/shard_map/transpose | solution.py:177
  122.4 2.3 %fusion.3 = bf16[192,1728]{1,0:T(8,128)(2,1)} fusion(f32[2,192,1728]{2,1,0:T(8,128)} %bitcast.87, s32[]{:T(128)S(6)} %select_n.48), kind=kLoop, calls=%fused_computation.13 | loop fusion | bytes 1327108 | tf_op jit(solution)/shard_map/convert_element_type | solution.py:166
  124.7 1.5 collective-permute-start.12
  126.2 20.9 %shard_map.68 = bf16[64,64,384]{2,1,0:T(8,128)(2,1)} custom-call(bf16[16,64,384]{2,1,0:T(8,128)(2,1)} %collective-permute-done.2.low, bf16[64,64,384]{2,1,0:T(8,128)(2,1)} %shard_map.67.mid.hidden, bf16[16,64,384]{2,1,0:T(8,128)(2,1)} %collective-permute-done.3.high, bf16[3456,384]{1,0:T(8,128)(2,1)} %weight.5), custom_call_target="tpu_custom_call" | custom-call | flops 10871635968 | bytes 12582912 | tf_op jit(solution)/shard_map/pallas_call | solution.py:148
  147.1 2.4 %bitcast_add_fusion.1 = f32[4,432,384]{2,1,0:T(8,128)S(1)} fusion(bf16[4,432,384]{2,1,0:T(8,128)(2,1)} %collective-permute-done.6, f32[4,2,432,384]{3,2,1,0:T(8,128)} %bitcast.96, s32[]{:T(128)S(6)} %select_n.45), kind=kLoop, calls=%fused_computation.3 | loop fusion | flops 1327104 | bytes 6635524 | tf_op jit(solution)/shard_map/add | solution.py:168
  149.5 2.3 %copy.11 = f32[384,1728]{1,0:T(8,128)} copy(f32[384,1728]{0,1:T(8,128)S(1)} %bitcast.85) | data formatting | bytes 5308416 | tf_op jit(solution)/shard_map/transpose | solution.py:177
  151.8 1.6 fusion.2
  153.4 0.6 collective-permute-start.7
  153.9 1.7 bitcast_add_fusion.2
  155.7 1.6 collective-permute-start.13
  157.2 13.7 %collective-permute-done.7 = bf16[192,1728]{1,0:T(8,128)(2,1)S(1)} collective-permute-done((bf16[192,1728]{1,0:T(8,128)(2,1)S(1)}, bf16[192,1728]{1,0:T(8,128)(2,1)S(1)}, u32[]{:S(2)}, u32[]{:S(2)}) %collective-permute-start.7) | collective-permute-done | bytes 663584 | tf_op jit(solution)/shard_map/ppermute | solution.py:168
  171.1 1.6 collective-permute-start.8
  172.8 1.0 reshape_reshape.7
  173.8 0.8 fusion.9
  174.6 2.7 %collective-permute-start.14 = (bf16[2,432,96]{1,0,2:T(2,128)(2,1)}, bf16[2,432,96]{1,0,2:T(2,128)(2,1)}, u32[]{:S(2)}, u32[]{:S(2)}) collective-permute-start(bf16[2,432,96]{1,0,2:T(2,128)(2,1)} %fusion.9), channel_id=1, source_target_pairs={{0,4},{1,5},{2,6},{3,7},{4,0},{5,1},{6,2},{7,3},{8,12},{9,13},{10,... | collective-permute-start | bytes 497672 | tf_op jit(solution)/shard_map/ppermute | solution.py:168
  177.2 3.3 %collective-permute-done.8 = bf16[96,1728]{1,0:T(8,128)(2,1)S(1)} collective-permute-done((bf16[96,1728]{1,0:T(8,128)(2,1)S(1)}, bf16[96,1728]{1,0:T(8,128)(2,1)S(1)}, u32[]{:S(2)}, u32[]{:S(2)}) %collective-permute-start.8) | collective-permute-done | bytes 331808 | tf_op jit(solution)/shard_map/ppermute | solution.py:168
  180.6 1.0 reshape_reshape.6
  181.7 2.2 %collective-permute-start.9 = (bf16[2,432,96]{1,0,2:T(2,128)(2,1)S(1)}, bf16[2,432,96]{1,0,2:T(2,128)(2,1)S(1)}, u32[]{:S(2)}, u32[]{:S(2)}) collective-permute-start(bf16[2,432,96]{1,0,2:T(2,128)(2,1)S(1)} %fusion.8), channel_id=1, source_target_pairs={{0,4},{1,5},{2,6},{3,7},{4,0},{5,1},{6,2},{7,3},{8,12},{9,13},{10,... | collective-permute-start | bytes 497672 | tf_op jit(solution)/shard_map/ppermute | solution.py:168
  184.0 6.9 %collective-permute-done.14 = bf16[2,432,96]{1,0,2:T(2,128)(2,1)} collective-permute-done((bf16[2,432,96]{1,0,2:T(2,128)(2,1)}, bf16[2,432,96]{1,0,2:T(2,128)(2,1)}, u32[]{:S(2)}, u32[]{:S(2)}) %collective-permute-start.14) | collective-permute-done | bytes 165920 | tf_op jit(solution)/shard_map/ppermute | solution.py:168
  190.9 1.1 bitcast_add_fusion.6
  192.0 0.2 dynamic-slice_convert_fusion.5
  192.3 2.0 %collective-permute-done.9 = bf16[2,432,96]{1,0,2:T(2,128)(2,1)S(1)} collective-permute-done((bf16[2,432,96]{1,0,2:T(2,128)(2,1)S(1)}, bf16[2,432,96]{1,0,2:T(2,128)(2,1)S(1)}, u32[]{:S(2)}, u32[]{:S(2)}) %collective-permute-start.9) | collective-permute-done | bytes 165920 | tf_op jit(solution)/shard_map/ppermute | solution.py:168
  194.3 0.2 bitcast_add_fusion.7
  194.7 0.2 collective-permute-start.10
  194.9 5.2 %collective-permute-done.15 = bf16[1,432,96]{1,0,2:T(2,128)(2,1)S(1)} collective-permute-done((bf16[1,432,96]{1,0,2:T(2,128)(2,1)S(1)}, bf16[1,432,96]{1,0,2:T(2,128)(2,1)S(1)}, u32[]{:S(2)}, u32[]{:S(2)}) %collective-permute-start.15) | collective-permute-done | bytes 82976 | tf_op jit(solution)/shard_map/ppermute | solution.py:168
  200.1 0.4 add_multiply_fusion
  200.5 0.7 copy.22
  201.1 1.5 collective-permute-done.10
  202.7 0.4 add_multiply_fusion.1
  203.0 0.7 copy.23
  (24 shorter events, 0.9 us)
Async XLA Ops:
  1.7 12.6 %collective-permute-start = (bf16[4,64,384]{2,1,0:T(8,128)(2,1)S(1)}, bf16[4,64,384]{2,1,0:T(8,128)(2,1)S(1)}, u32[]{:S(2)}, u32[]{:S(2)}) collective-permute-start(bf16[4,64,384]{2,1,0:T(8,128)(2,1)S(1)} %get-tuple-element.8), channel_id=1, source_target_pairs={{0,1},{1,2},{2,3},{3,4},{4,5},{5,6},{6,7},{8,9},{9,10},{10,11},{11... | collective-permute-start | bytes 589832 | tf_op jit(solution)/shard_map/ppermute | solution.py:21
  4.1 10.3 %collective-permute-start.1 = (bf16[4,64,384]{2,1,0:T(8,128)(2,1)S(1)}, bf16[4,64,384]{2,1,0:T(8,128)(2,1)S(1)}, u32[]{:S(2)}, u32[]{:S(2)}) collective-permute-start(bf16[4,64,384]{2,1,0:T(8,128)(2,1)S(1)} %get-tuple-element.7), channel_id=1, source_target_pairs={{1,0},{2,1},{3,2},{4,3},{5,4},{6,5},{7,6},{9,8},{10,9},{11,10},{12... | collective-permute-start | bytes 589832 | tf_op jit(solution)/shard_map/ppermute | solution.py:22
  6.9 37.4 %collective-permute-start.4 = (bf16[16,64,384]{2,1,0:T(8,128)(2,1)S(1)}, bf16[16,64,384]{2,1,0:T(8,128)(2,1)}, u32[]{:S(2)}, u32[]{:S(2)}) collective-permute-start(bf16[16,64,384]{2,1,0:T(8,128)(2,1)S(1)} %get-tuple-element.4), channel_id=1, source_target_pairs={{0,1},{1,2},{2,3},{3,4},{4,5},{5,6},{6,7},{8,9},{9,10},{10,11},{11... | collective-permute-start | bytes 2359304 | tf_op jit(solution)/shard_map/ppermute | solution.py:21
  13.0 31.3 %collective-permute-start.5 = (bf16[16,64,384]{2,1,0:T(8,128)(2,1)S(1)}, bf16[16,64,384]{2,1,0:T(8,128)(2,1)}, u32[]{:S(2)}, u32[]{:S(2)}) collective-permute-start(bf16[16,64,384]{2,1,0:T(8,128)(2,1)S(1)} %get-tuple-element.3), channel_id=1, source_target_pairs={{1,0},{2,1},{3,2},{4,3},{5,4},{6,5},{7,6},{9,8},{10,9},{11,10},{12... | collective-permute-start | bytes 2359304 | tf_op jit(solution)/shard_map/ppermute | solution.py:22
  14.3 0.7 copy-start.1
  14.3 0.7 copy-start.2
  38.6 87.7 %collective-permute-start.2 = (bf16[16,64,384]{2,1,0:T(8,128)(2,1)}, bf16[16,64,384]{2,1,0:T(8,128)(2,1)}, u32[]{:S(2)}, u32[]{:S(2)}) collective-permute-start(bf16[16,64,384]{2,1,0:T(8,128)(2,1)} %get-tuple-element.6), channel_id=1, source_target_pairs={{0,1},{1,2},{2,3},{3,4},{4,5},{5,6},{6,7},{8,9},{9,10},{10,11},{11... | collective-permute-start | bytes 2359304 | tf_op jit(solution)/shard_map/ppermute | solution.py:21
  42.8 83.4 %collective-permute-start.3 = (bf16[16,64,384]{2,1,0:T(8,128)(2,1)S(1)}, bf16[16,64,384]{2,1,0:T(8,128)(2,1)}, u32[]{:S(2)}, u32[]{:S(2)}) collective-permute-start(bf16[16,64,384]{2,1,0:T(8,128)(2,1)S(1)} %get-tuple-element.5), channel_id=1, source_target_pairs={{1,0},{2,1},{3,2},{4,3},{5,4},{6,5},{7,6},{9,8},{10,9},{11,10},{12... | collective-permute-start | bytes 2359304 | tf_op jit(solution)/shard_map/ppermute | solution.py:22
  68.4 49.7 %collective-permute-start.11 = (bf16[4,432,384]{2,1,0:T(8,128)(2,1)S(1)}, bf16[4,432,384]{2,1,0:T(8,128)(2,1)S(1)}, u32[]{:S(2)}, u32[]{:S(2)}) collective-permute-start(bf16[4,432,384]{2,1,0:T(8,128)(2,1)S(1)} %fusion.1), channel_id=1, source_target_pairs={{0,1},{1,0},{2,3},{3,2},{4,5},{5,4},{6,7},{7,6},{8,9},{9,8},{10,11... | collective-permute-start | bytes 3981320 | tf_op jit(solution)/shard_map/ppermute | solution.py:168
  118.1 29.0 %collective-permute-start.6 = (bf16[4,432,384]{2,1,0:T(8,128)(2,1)}, bf16[4,432,384]{2,1,0:T(8,128)(2,1)}, u32[]{:S(2)}, u32[]{:S(2)}) collective-permute-start(bf16[4,432,384]{2,1,0:T(8,128)(2,1)} %fusion), channel_id=1, source_target_pairs={{0,1},{1,0},{2,3},{3,2},{4,5},{5,4},{6,7},{7,6},{8,9},{9,8},{10,11... | collective-permute-start | bytes 3981320 | tf_op jit(solution)/shard_map/ppermute | solution.py:168
  124.7 29.2 %collective-permute-start.12 = (bf16[192,1728]{1,0:T(8,128)(2,1)}, bf16[192,1728]{1,0:T(8,128)(2,1)}, u32[]{:S(2)}, u32[]{:S(2)}) collective-permute-start(bf16[192,1728]{1,0:T(8,128)(2,1)} %fusion.3), channel_id=1, source_target_pairs={{0,16},{8,24},{16,0},{24,8},{1,17},{9,25},{17,1},{25,9},{2,18},{10... | collective-permute-start | bytes 1990664 | tf_op jit(solution)/shard_map/ppermute | solution.py:168
  151.8 19.2 %copy-start = (f32[384,1728]{1,0:T(8,128)S(1)}, f32[384,1728]{1,0:T(8,128)}, u32[]{:S(2)}) copy-start(f32[384,1728]{1,0:T(8,128)} %copy.11) | copy-start | bytes 7962628
  153.4 17.6 %collective-permute-start.7 = (bf16[192,1728]{1,0:T(8,128)(2,1)S(1)}, bf16[192,1728]{1,0:T(8,128)(2,1)S(1)}, u32[]{:S(2)}, u32[]{:S(2)}) collective-permute-start(bf16[192,1728]{1,0:T(8,128)(2,1)S(1)} %fusion.2), channel_id=1, source_target_pairs={{0,16},{8,24},{16,0},{24,8},{1,17},{9,25},{17,1},{25,9},{2,18},{10... | collective-permute-start | bytes 1990664 | tf_op jit(solution)/shard_map/ppermute | solution.py:168
  155.7 17.0 %collective-permute-start.13 = (bf16[96,1728]{1,0:T(8,128)(2,1)S(1)}, bf16[96,1728]{1,0:T(8,128)(2,1)S(1)}, u32[]{:S(2)}, u32[]{:S(2)}) collective-permute-start(bf16[96,1728]{1,0:T(8,128)(2,1)S(1)} %fusion.7), channel_id=1, source_target_pairs={{0,8},{8,0},{16,24},{24,16},{1,9},{9,1},{17,25},{25,17},{2,10},{10... | collective-permute-start | bytes 995336 | tf_op jit(solution)/shard_map/ppermute | solution.py:168
  171.1 9.4 %collective-permute-start.8 = (bf16[96,1728]{1,0:T(8,128)(2,1)S(1)}, bf16[96,1728]{1,0:T(8,128)(2,1)S(1)}, u32[]{:S(2)}, u32[]{:S(2)}) collective-permute-start(bf16[96,1728]{1,0:T(8,128)(2,1)S(1)} %fusion.6), channel_id=1, source_target_pairs={{0,8},{8,0},{16,24},{24,16},{1,9},{9,1},{17,25},{25,17},{2,10},{10... | collective-permute-start | bytes 995336 | tf_op jit(solution)/shard_map/ppermute | solution.py:168
  174.6 16.3 %collective-permute-start.14 = (bf16[2,432,96]{1,0,2:T(2,128)(2,1)}, bf16[2,432,96]{1,0,2:T(2,128)(2,1)}, u32[]{:S(2)}, u32[]{:S(2)}) collective-permute-start(bf16[2,432,96]{1,0,2:T(2,128)(2,1)} %fusion.9), channel_id=1, source_target_pairs={{0,4},{1,5},{2,6},{3,7},{4,0},{5,1},{6,2},{7,3},{8,12},{9,13},{10,... | collective-permute-start | bytes 497672 | tf_op jit(solution)/shard_map/ppermute | solution.py:168
  181.7 12.6 %collective-permute-start.9 = (bf16[2,432,96]{1,0,2:T(2,128)(2,1)S(1)}, bf16[2,432,96]{1,0,2:T(2,128)(2,1)S(1)}, u32[]{:S(2)}, u32[]{:S(2)}) collective-permute-start(bf16[2,432,96]{1,0,2:T(2,128)(2,1)S(1)} %fusion.8), channel_id=1, source_target_pairs={{0,4},{1,5},{2,6},{3,7},{4,0},{5,1},{6,2},{7,3},{8,12},{9,13},{10,... | collective-permute-start | bytes 497672 | tf_op jit(solution)/shard_map/ppermute | solution.py:168
  192.2 7.9 %collective-permute-start.15 = (bf16[1,432,96]{1,0,2:T(2,128)(2,1)S(1)}, bf16[1,432,96]{1,0,2:T(2,128)(2,1)S(1)}, u32[]{:S(2)}, u32[]{:S(2)}) collective-permute-start(bf16[1,432,96]{1,0,2:T(2,128)(2,1)S(1)} %dynamic-slice_convert_fusion.5), channel_id=1, source_target_pairs={{0,2},{1,3},{2,0},{3,1},{4,6},{5,7},{6,4},{7,5},{8,10},{9,11},{10,... | collective-permute-start | bytes 248840 | tf_op jit(solution)/shard_map/ppermute | solution.py:168
  194.7 7.9 %collective-permute-start.10 = (bf16[1,432,96]{1,0,2:T(2,128)(2,1)S(1)}, bf16[1,432,96]{1,0,2:T(2,128)(2,1)S(1)}, u32[]{:S(2)}, u32[]{:S(2)}) collective-permute-start(bf16[1,432,96]{1,0,2:T(2,128)(2,1)S(1)} %dynamic-slice_convert_fusion.6), channel_id=1, source_target_pairs={{0,2},{1,3},{2,0},{3,1},{4,6},{5,7},{6,4},{7,5},{8,10},{9,11},{10,... | collective-permute-start | bytes 248840 | tf_op jit(solution)/shard_map/ppermute | solution.py:168

commit v2 on v1

--- a/solution.py
+++ b/solution.py
@@ -79,7 +79,7 @@
     return jnp.concatenate(pieces, axis=1)
 
 
-def output_kernel(tile, spacing, low, mid, high, weight, out, padded):
+def output_kernel(tile, spacing, first, low, mid, high, weight, out, padded):
     step = pl.program_id(0)
 
     @pl.when(step == 0)
@@ -87,7 +87,7 @@
         fill_padded(padded, low, mid, high, spacing)
 
     cols, channels = mid.shape[1:]
-    stacked = far_windows(padded, step, tile, spacing, cols, 1)
+    stacked = far_windows(padded, first + step, tile, spacing, cols, 1)
     result = jnp.dot(stacked, weight[...], preferred_element_type=F32)
     out[...] = result.astype(BF16).reshape(tile, cols, channels)
 
@@ -143,44 +143,76 @@
     out[...] = product.T
 
 
-def run(kernel, out_shape, grid, out_spec, scratch, args, specs, flops):
+def run(kernel, out_shape, grid, out_spec, scratch, args, specs, flops, after=(), aliases=None):
     whole = pl.BlockSpec(memory_space=pltpu.VMEM)
+    first, last = len(args), len(args) + len(after)
+
+    def body(*refs):
+        kernel(*refs[:first], *refs[last:])
+
     return pl.pallas_call(
-        kernel,
+        body,
         out_shape=out_shape,
         grid=(grid,),
-        in_specs=[whole if spec is None else spec for spec in specs],
+        in_specs=[whole if spec is None else spec for spec in specs]
+        + [pl.BlockSpec(memory_space=pl.ANY)] * len(after),
         out_specs=out_spec,
         scratch_shapes=scratch,
+        input_output_aliases=aliases or {},
         compiler_params=pltpu.CompilerParams(vmem_limit_bytes=VMEM_LIMIT),
         cost_estimate=pl.CostEstimate(
-            flops=flops, bytes_accessed=12 * 1024 * 1024, transcendentals=0
+            flops=flops // 64, bytes_accessed=1024, transcendentals=0
         ),
-    )(*args)
-
-
-def halve(total, axis, bit):
+    )(*args, *after)
+
+
+def shared(pieces, axis, shift):
+    owners = pieces.shape[0]
+    mine = lax.axis_index(axis) >> shift
+    kept = lax.dynamic_index_in_dim(pieces, mine, 0, keepdims=False)
+    sent = [
+        lax.dynamic_index_in_dim(pieces, mine ^ k, 0, keepdims=False).astype(BF16)
+        for k in range(1, owners)
+    ]
+    return kept, sent
+
+
+def joined(kept, sent, axis, shift):
     count = lax.axis_size(axis)
-    mine = (lax.axis_index(axis) >> bit) & 1
-    pairs = [(i, i ^ (1 << bit)) for i in range(count)]
-    sent = lax.dynamic_index_in_dim(total, 1 - mine, 0, keepdims=False).astype(BF16)
-    kept = lax.dynamic_index_in_dim(total, mine, 0, keepdims=False)
-    return kept + lax.ppermute(sent, axis, pairs).astype(F32)
-
-
-def reduce_grad(grad):
-    rows, dp = lax.axis_size("rows"), lax.axis_size("dp")
+    total = kept
+    for k, piece in enumerate(sent, 1):
+        pairs = [(i, i ^ (k << shift)) for i in range(count)]
+        total = total + lax.ppermute(piece, axis, pairs).astype(F32)
+    return total
+
+
+def split_pair(grad):
     taps, channels = grad.shape
-    height, width = taps // rows, channels // dp
-    outer = rows // 2
-    total = jnp.moveaxis(grad.reshape(outer, 2, height, channels), 1, 0)
-    total = halve(total, "rows", 0).reshape(outer * height, channels).T
-    for bit in reversed(range(dp.bit_length() - 1)):
-        total = halve(total.reshape(2, total.shape[0] // 2, outer * height), "dp", bit)
-    total = total.T.reshape(outer, height, width)
-    for bit in reversed(range(1, rows.bit_length() - 1)):
-        total = halve(total.reshape(2, total.shape[0] // 2, height, width), "rows", bit)
-    return total.reshape(height, width)
+    rows = lax.axis_size("rows")
+    pieces = jnp.moveaxis(grad.reshape(rows // 2, 2, taps // rows, channels), 1, 0)
+    mine = lax.axis_index("rows") & 1
+    kept = lax.dynamic_index_in_dim(pieces, mine, 0, keepdims=False)
+    sent = lax.dynamic_index_in_dim(pieces, 1 - mine, 0, keepdims=False).astype(BF16)
+    return kept, [sent]
+
+
+def split_samples(kept, sent):
+    total = joined(kept, sent, "rows", 0)
+    dp = lax.axis_size("dp")
+    channels = total.shape[-1]
+    turned = total.reshape(-1, channels).T
+    return shared(turned.reshape(dp, channels // dp, turned.shape[1]), "dp", 0)
+
+
+def split_rows(kept, sent):
+    total = joined(kept, sent, "dp", 0)
+    outer = lax.axis_size("rows") // 2
+    pieces = jnp.moveaxis(total.reshape(total.shape[0], outer, -1), 1, 0)
+    return shared(pieces, "rows", 1)
+
+
+def finish(kept, sent):
+    return joined(kept, sent, "rows", 1).T
 
 
 def on_device(inputs, cotangent, weight_one, weight_two):
@@ -210,29 +242,45 @@
         map_shape, steps, map_spec, [shifted],
         (*near, weight_one), [None] * 4, flops,
     )
+    hidden_low, hidden_high = edge_rows(hidden, spacing)
     grad_two = run(
         functools.partial(far_grad_kernel, spacing),
         grad_shape, 9, grad_spec, [padded, turned],
         (*far, hidden), [None] * 4, flops,
     )
+    pair_two = split_pair(grad_two)
     masked = run(
         functools.partial(back_kernel, tile, spacing),
         map_shape, steps, map_spec, [padded, pltpu.VMEM(weight_two.shape, BF16)],
-        (*far, weight_two, hidden), [None] * 4 + [map_spec], flops,
-    )
+        (*far, weight_two, hidden), [None] * 4 + [map_spec], flops, pair_two[1],
+    )
+    samples_two = split_samples(*pair_two)
     grad_one = run(
         near_grad_kernel,
         grad_shape, 9, grad_spec, [shifted, turned],
-        (*near, masked), [None] * 4, flops,
-    )
-    hidden_low, hidden_high = edge_rows(hidden, spacing)
+        (*near, masked), [None] * 4, flops, samples_two[1],
+    )
+    pair_one = split_pair(grad_one)
+    rows_two = split_rows(*samples_two)
+    early = max(1, steps // 4)
     output = run(
-        functools.partial(output_kernel, tile, spacing),
-        map_shape, steps, map_spec, [padded],
-        (hidden_low, hidden, hidden_high, weight_two), [None] * 4, flops,
-    )
-    grad_two = reduce_grad(grad_two)
-    grad_one = reduce_grad(grad_one)
+        functools.partial(output_kernel, tile, spacing, 0),
+        map_shape, early, map_spec, [padded],
+        (hidden_low, hidden, hidden_high, weight_two), [None] * 4,
+        flops * early // steps, pair_one[1] + rows_two[1],
+    )
+    kept_one, output = lax.optimization_barrier((pair_one[0], output))
+    samples_one = split_samples(kept_one, pair_one[1])
+    if early < steps:
+        output = run(
+            functools.partial(output_kernel, tile, spacing, early),
+            map_shape, steps - early,
+            pl.BlockSpec((tile, cols, channels), lambda i: (i + early, 0, 0)), [padded],
+            (hidden_low, hidden, hidden_high, weight_two), [None] * 4,
+            flops * (steps - early) // steps, [output] + samples_one[1], {4: 0},
+        )
+    grad_two = finish(*rows_two)
+    grad_one = finish(*split_rows(*samples_one))
     return (output[None], grad_one * factor, grad_two * factor)
 
 

time: 204 us -> 208 us (1.020)
  waiting for transfers between devices: 32.7 us -> 15.2 us
  starting transfers between devices: 28.8 us -> 36.4 us
  local copies, waits for them, and re-layouts: 23.9 us -> 30.2 us
  Pallas kernels: 109 us -> 114 us
  other arithmetic: 8.35 us -> 10.9 us
    ppermute x10 -> x14, waiting for transfers between devices: 32.7 us -> 14 us  [joined(): total = total + lax.ppermute(piece, axis, pairs).astype(F32)]
    ppermute x10 -> x14, starting transfers between devices: 12 us -> 22.2 us  [joined(): total = total + lax.ppermute(piece, axis, pairs).astype(F32)]
    reshape x0 -> x4, local copies, waits for them, and re-layouts: none -> 8.16 us  [the longest x2 4.45 us: split_samples(): turned = total.reshape(-1, channels).T]
    pallas_call x5 -> x6, Pallas kernels: 109 us -> 114 us  [run(): pl.pallas_call(body, out_shape=out_shape, grid=(grid,), in_specs=[whole i...]
    transpose x2 -> x0, local copies, waits for them, and re-layouts: 4.62 us -> none  [reduce_grad(): total = halve(total, 'rows', 0).reshape(outer * height, channels).T]
    convert_element_type x10 -> x4, local copies, waits for them, and re-layouts: 10.2 us -> 6.16 us  [the longest x2 4.94 us: split_pair(): lax.dynamic_index_in_dim(pieces, 1 - mine, 0, keepdims=False).astype(BF16)]
    unnamed x8 -> x36, local copies, waits for them, and re-layouts: 2.1 us -> 4.93 us
    another operation x2 -> x4, local copies, waits for them, and re-layouts: 1.95 us -> 4.31 us  [reduce_grad(): total.reshape(2, total.shape[0] // 2, height, width)]
  transfers between devices with their start and end apart: 16 -> 20, of which waited for: 6 -> 6; matrix products, arithmetic and copies ran while one was open for 14% -> 11% of each run, Pallas kernels for 54% -> 33%
where the time goes in v2:
time: 208 us
  Pallas kernels  114 us (55%)
  starting transfers between devices  36.4 us (18%)
  local copies, waits for them, and re-layouts  30.2 us (15%)
  waiting for transfers between devices  15.2 us (7%)
  other arithmetic  10.9 us (5%)
    pallas_call x6, Pallas kernels, run(): pl.pallas_call(body, out_shape=out_shape, grid=(grid,), in_specs=[whole i...  114 us
    ppermute x14, starting transfers between devices, joined(): total = total + lax.ppermute(piece, axis, pairs).astype(F32)  22.2 us
    ppermute x14, waiting for transfers between devices, joined(): total = total + lax.ppermute(piece, axis, pairs).astype(F32)  14 us
    ppermute x3, starting transfers between devices, edge_rows(): low = lax.ppermute(block[block.shape[0] - width:], 'rows', forward)  10.4 us
    add x4, other arithmetic, joined(): total = total + lax.ppermute(piece, axis, pairs).astype(F32)  8.44 us
    convert_element_type x2, local copies, waits for them, and re-layouts, split_pair(): lax.dynamic_index_in_dim(pieces, 1 - mine, 0, keepdims=False).astype(BF16)  4.94 us
    unnamed x36, local copies, waits for them, and re-layouts  4.93 us
    slice x3, local copies, waits for them, and re-layouts, edge_rows(): high = lax.ppermute(block[:width], 'rows', backward)  4.67 us
  transfers between devices with their start and end apart: 20, of which 6 were waited for; matrix products, arithmetic and copies ran while one was open for 11% of the time, Pallas kernels for 33%

profile of v2, /device:TPU:0, one launch (start us, length us, event | category | flops | bytes accessed | tf_op | source)
XLA Modules:
  0.0 207.6 jit_solution(13167962055721563604)
XLA Ops:
  0.6 1.5 slice_bitcast_fusion
  2.2 1.3 collective-permute-start.5
  3.5 3.1 %collective-permute-start.4 = (bf16[16,64,384]{2,1,0:T(8,128)(2,1)S(1)}, bf16[16,64,384]{2,1,0:T(8,128)(2,1)S(1)}, u32[]{:S(2)}, u32[]{:S(2)}) collective-permute-start(bf16[16,64,384]{2,1,0:T(8,128)(2,1)S(1)} %get-tuple-element.8), channel_id=1, source_target_pairs={{0,1},{1,2},{2,3},{3,4},{4,5},{5,6},{6,7},{8,9},{9,10},{10,11},{11... | collective-permute-start | bytes 2359304 | tf_op jit(solution)/shard_map/ppermute | solution.py:21
  6.6 1.8 slice_bitcast_fusion.2
  8.4 1.3 collective-permute-start.1
  9.6 5.1 %collective-permute-start = (bf16[4,64,384]{2,1,0:T(8,128)(2,1)}, bf16[4,64,384]{2,1,0:T(8,128)(2,1)S(1)}, u32[]{:S(2)}, u32[]{:S(2)}) collective-permute-start(bf16[4,64,384]{2,1,0:T(8,128)(2,1)} %get-tuple-element.12), channel_id=1, source_target_pairs={{0,1},{1,2},{2,3},{3,4},{4,5},{5,6},{6,7},{8,9},{9,10},{10,11},{11... | collective-permute-start | bytes 589832 | tf_op jit(solution)/shard_map/ppermute | solution.py:21
  14.8 1.2 collective-permute-done.refs_0_
  16.1 0.7 copy-done.11
  16.7 21.1 %shard_map.67.refs_3_.refs_4_.refs_1_ = bf16[64,64,384]{2,1,0:T(8,128)(2,1)} custom-call(bf16[4,64,384]{2,1,0:T(8,128)(2,1)} %copy-done.11, bf16[64,64,384]{2,1,0:T(8,128)(2,1)} %bitcast.111, bf16[4,64,384]{2,1,0:T(8,128)(2,1)} %copy-done.10, bf16[3456,384]{1,0:T(8,128)(2,1)} %refs_3_.4), custom_call_target="tpu_custom_call" | custom-call | flops 169869312 | bytes 1024 | tf_op jit(solution)/shard_map/pallas_call | solution.py:153
  37.9 0.9 copy-done.4
  39.1 22.2 %shard_map.68 = f32[3456,384]{1,0:T(8,128)} custom-call(bf16[16,64,384]{2,1,0:T(8,128)(2,1)} %copy-done.5, bf16[64,64,384]{2,1,0:T(8,128)(2,1)} %bitcast.103, bf16[16,64,384]{2,1,0:T(8,128)(2,1)} %copy-done.4, bf16[64,64,384]{2,1,0:T(8,128)(2,1)} %shard_map.67.refs_3_.refs_4_.refs_1_), custom_call_target="tpu_custom_call" | custom-call | flops 169869312 | bytes 1024 | tf_op jit(solution)/shard_map/pallas_call | solution.py:153
  61.2 2.0 fusion.refs_5_
  63.2 4.3 %collective-permute-start.6 = (bf16[4,432,384]{2,1,0:T(8,128)(2,1)S(1)}, bf16[4,432,384]{2,1,0:T(8,128)(2,1)}, u32[]{:S(2)}, u32[]{:S(2)}) collective-permute-start(bf16[4,432,384]{2,1,0:T(8,128)(2,1)S(1)} %fusion.refs_5_), channel_id=1, source_target_pairs={{0,1},{1,0},{2,3},{3,2},{4,5},{5,4},{6,7},{7,6},{8,9},{9,8},{10,11... | collective-permute-start | bytes 3981320 | tf_op jit(solution)/shard_map/ppermute | solution.py:185
  67.5 21.8 %shard_map.69.refs_3_ = bf16[64,64,384]{2,1,0:T(8,128)(2,1)} custom-call(bf16[16,64,384]{2,1,0:T(8,128)(2,1)} %copy-done.5, bf16[64,64,384]{2,1,0:T(8,128)(2,1)} %bitcast.104, bf16[16,64,384]{2,1,0:T(8,128)(2,1)} %copy-done.4, bf16[3456,384]{1,0:T(8,128)(2,1)} %refs_3_.7, bf16[64,64,384]{2,1,0:T(8,128)(2,1)} %shard_map.67.refs_3_.refs_4_.refs_1_, ...), custom_call_target="tpu_custom_call" | custom-call | flops 169869312 | bytes 1024 | tf_op jit(solution)/shard_map/pallas_call | solution.py:153
  89.4 3.0 %bitcast_add_fusion = f32[4,432,384]{2,1,0:T(8,128)} fusion(bf16[4,432,384]{2,1,0:T(8,128)(2,1)} %collective-permute-done.6, f32[4,2,432,384]{3,2,1,0:T(8,128)S(1)} %bitcast.110, s32[]{:T(128)S(6)} %select_n.44), kind=kLoop, calls=%fused_computation.2 | loop fusion | flops 1327104 | bytes 6635524 | tf_op jit(solution)/shard_map/add | solution.py:185
  92.4 2.2 %copy.14 = f32[1728,384]{0,1:T(8,128)S(1)} copy(f32[1728,384]{1,0:T(8,128)} %bitcast.115) | data formatting | bytes 5308416 | tf_op jit(solution)/shard_map/reshape | solution.py:203
  94.6 1.1 fusion.8
  95.8 0.7 copy-done.1
  96.5 23.6 %shard_map.70 = f32[3456,384]{1,0:T(8,128)} custom-call(bf16[4,64,384]{2,1,0:T(8,128)(2,1)} %copy-done.11, bf16[64,64,384]{2,1,0:T(8,128)(2,1)} %bitcast.112, bf16[4,64,384]{2,1,0:T(8,128)(2,1)} %copy-done.10, bf16[64,64,384]{2,1,0:T(8,128)(2,1)} %shard_map.69.refs_3_, bf16[96,1728]{1,0:T(8,128)(2,1)} %get-tuple-element.18.refs_4_, ...), custom_call_target="tpu_custom_call" | custom-call | flops 169869312 | bytes 1024 | tf_op jit(solution)/shard_map/pallas_call | solution.py:153
  120.1 3.0 %fusion.1.refs_4_ = bf16[4,432,384]{2,1,0:T(8,128)(2,1)} fusion(f32[4,2,432,384]{3,2,1,0:T(8,128)} %bitcast.105, s32[]{:T(128)S(6)} %select_n.43), kind=kLoop, calls=%fused_computation.6 | loop fusion | bytes 2654212 | tf_op jit(solution)/shard_map/convert_element_type | solution.py:195
  123.0 1.1 collective-permute-start.10
  124.1 2.4 %collective-permute-start.9 = (bf16[96,1728]{1,0:T(8,128)(2,1)S(1)}, bf16[96,1728]{1,0:T(8,128)(2,1)}, u32[]{:S(2)}, u32[]{:S(2)}) collective-permute-start(bf16[96,1728]{1,0:T(8,128)(2,1)S(1)} %copy-done.6), channel_id=1, source_target_pairs={{0,24},{8,16},{16,8},{24,0},{1,25},{9,17},{17,9},{25,1},{2,26},{10... | collective-permute-start | bytes 995336 | tf_op jit(solution)/shard_map/ppermute | solution.py:185
  127.6 1.3 fusion.26
  128.9 1.3 collective-permute-start.3
  130.2 5.9 %collective-permute-done.9 = bf16[96,1728]{1,0:T(8,128)(2,1)} collective-permute-done((bf16[96,1728]{1,0:T(8,128)(2,1)S(1)}, bf16[96,1728]{1,0:T(8,128)(2,1)}, u32[]{:S(2)}, u32[]{:S(2)}) %collective-permute-start.9) | collective-permute-done | bytes 331808 | tf_op jit(solution)/shard_map/ppermute | solution.py:185
  136.1 2.2 %collective-permute-start.2 = (bf16[16,64,384]{2,1,0:T(8,128)(2,1)}, bf16[16,64,384]{2,1,0:T(8,128)(2,1)}, u32[]{:S(2)}, u32[]{:S(2)}) collective-permute-start(bf16[16,64,384]{2,1,0:T(8,128)(2,1)} %get-tuple-element.10), channel_id=1, source_target_pairs={{0,1},{1,2},{2,3},{3,4},{4,5},{5,6},{6,7},{8,9},{9,10},{10,11},{11... | collective-permute-start | bytes 2359304 | tf_op jit(solution)/shard_map/ppermute | solution.py:21
  138.3 1.9 dynamic-slice_bitcast_fusion
  140.2 2.2 %collective-permute-done.8 = bf16[96,1728]{1,0:T(8,128)(2,1)S(1)} collective-permute-done((bf16[96,1728]{1,0:T(8,128)(2,1)}, bf16[96,1728]{1,0:T(8,128)(2,1)S(1)}, u32[]{:S(2)}, u32[]{:S(2)}) %collective-permute-start.8) | collective-permute-done | bytes 331808 | tf_op jit(solution)/shard_map/ppermute | solution.py:185
  142.5 2.2 %fusion.5 = f32[96,1728]{1,0:T(8,128)} fusion(bf16[96,1728]{1,0:T(8,128)(2,1)} %collective-permute-done.9, bf16[96,1728]{1,0:T(8,128)(2,1)S(1)} %collective-permute-done.8, bf16[96,1728]{1,0:T(8,128)(2,1)S(1)} %collective-permute-done.7, f32[4,96,1728]{2,1,0:T(8,128)} %bitcast.117, s32[]{:T(128)S(6)} %select_n.48), kind=kLoop, calls=%fused_computation.14 | loop fusion | flops 995328 | bytes 2322436 | tf_op jit(solution)/shard_map/add | solution.py:185
  144.7 2.9 %reshape.76 = f32[96,4,432]{2,1,0:T(4,128)} reshape(f32[96,1728]{1,0:T(8,128)} %fusion.5) | data formatting | bytes 1327104 | tf_op jit(solution)/shard_map/reshape | solution.py:210
  147.5 2.3 %constant_dynamic-slice_fusion.5 = (bf16[96,1,432]{2,1,0:T(2,128)(2,1)S(1)}, bf16[96,1,432]{2,1,0:T(2,128)(2,1)S(1)}, bf16[96,1,432]{2,1,0:T(2,128)(2,1)S(1)}) fusion(f32[96,4,432]{2,1,0:T(4,128)} %reshape.76, s32[]{:T(128)S(6)} %select_n.51, s32[]{:T(128)S(6)} %select_n.50, s32[]{:T(128)S(6)} %select_n.49), kind=kLoop, calls=%fused_computation.56 | loop fusion | bytes 497676 | tf_op jit(solution)/shard_map/dynamic-slice.6
  151.2 2.7 %collective-permute-start.17 = (bf16[96,432]{1,0:T(8,128)(2,1)}, bf16[96,432]{1,0:T(8,128)(2,1)}, u32[]{:S(2)}, u32[]{:S(2)}) collective-permute-start(bf16[96,432]{1,0:T(8,128)(2,1)} %bitcast.97.refs_5_), channel_id=1, source_target_pairs={{0,2},{1,3},{2,0},{3,1},{4,6},{5,7},{6,4},{7,5},{8,10},{9,11},{10,... | collective-permute-start | bytes 248840 | tf_op jit(solution)/shard_map/ppermute | solution.py:185
  153.9 2.6 %collective-permute-start.18 = (bf16[96,432]{1,0:T(8,128)(2,1)}, bf16[96,432]{1,0:T(8,128)(2,1)}, u32[]{:S(2)}, u32[]{:S(2)}) collective-permute-start(bf16[96,432]{1,0:T(8,128)(2,1)} %bitcast.98.refs_6_), channel_id=1, source_target_pairs={{0,4},{1,5},{2,6},{3,7},{4,0},{5,1},{6,2},{7,3},{8,12},{9,13},{10,... | collective-permute-start | bytes 248840 | tf_op jit(solution)/shard_map/ppermute | solution.py:185
  156.5 0.9 copy-done.3
  157.4 8.6 %shard_map.71.refs_4_ = bf16[64,64,384]{2,1,0:T(8,128)(2,1)} custom-call(bf16[16,64,384]{2,1,0:T(8,128)(2,1)} %collective-permute-done.2.refs_0_, bf16[64,64,384]{2,1,0:T(8,128)(2,1)} %shard_map.67.refs_3_.refs_4_.refs_1_, bf16[16,64,384]{2,1,0:T(8,128)(2,1)} %copy-done.3, bf16[3456,384]{1,0:T(8,128)(2,1)} %refs_3_.7, bf16[4,432,384]{2,1,0:T(8,128)(2,1)} %fusion.1.refs_4_, ...), custom_call_target="tpu_custom_call" | custom-call | flops 42467328 | bytes 1024 | tf_op jit(solution)/shard_map/pallas_call | solution.py:153
  166.0 3.0 %convert_add_fusion = f32[4,432,384]{2,1,0:T(8,128)} fusion(f32[4,432,384]{2,1,0:T(8,128)S(1)} %dynamic-slice_bitcast_fusion, bf16[4,432,384]{2,1,0:T(8,128)(2,1)} %collective-permute-done.10), kind=kLoop, calls=%fused_computation.3 | loop fusion | flops 1327104 | bytes 6635520 | tf_op jit(solution)/shard_map/add | solution.py:185
  169.0 2.2 %copy.19 = f32[1728,384]{0,1:T(8,128)S(1)} copy(f32[1728,384]{1,0:T(8,128)} %bitcast.114) | data formatting | bytes 5308416 | tf_op jit(solution)/shard_map/reshape | solution.py:203
  171.4 1.9 collective-permute-start.13
  173.3 1.1 collective-permute-start.12
  174.9 1.3 constant_dynamic-slice_fusion
  176.3 1.7 fusion.15
  178.0 16.8 %shard_map.72 = bf16[64,64,384]{2,1,0:T(8,128)(2,1)} custom-call(bf16[16,64,384]{2,1,0:T(8,128)(2,1)} %collective-permute-done.2.refs_0_, bf16[64,64,384]{2,1,0:T(8,128)(2,1)} %shard_map.67.refs_3_.refs_4_.refs_1_, bf16[16,64,384]{2,1,0:T(8,128)(2,1)} %copy-done.3, bf16[3456,384]{1,0:T(8,128)(2,1)} %refs_3_.7, ...), custom_call_target="tpu_custom_call", output_to_operand_aliasing={{}: (4, {})} | custom-call | flops 127401984 | bytes 1024 | tf_op jit(solution)/shard_map/pallas_call | solution.py:153
  194.9 0.9 reshape.79
  196.4 3.0 %collective-permute-start.16 = (bf16[96,432]{1,0:T(8,128)(2,1)S(1)}, bf16[96,432]{1,0:T(8,128)(2,1)S(1)}, u32[]{:S(2)}, u32[]{:S(2)}) collective-permute-start(bf16[96,432]{1,0:T(8,128)(2,1)S(1)} %bitcast.124), channel_id=1, source_target_pairs={{0,6},{1,7},{2,4},{3,5},{4,2},{5,3},{6,0},{7,1},{8,14},{9,15},{10,... | collective-permute-start | bytes 248840 | tf_op jit(solution)/shard_map/ppermute | solution.py:185
  199.4 1.4 collective-permute-start.14
  201.0 2.6 %collective-permute-done.16 = bf16[96,432]{1,0:T(8,128)(2,1)S(1)} collective-permute-done((bf16[96,432]{1,0:T(8,128)(2,1)S(1)}, bf16[96,432]{1,0:T(8,128)(2,1)S(1)}, u32[]{:S(2)}, u32[]{:S(2)}) %collective-permute-start.16) | collective-permute-done | bytes 82976 | tf_op jit(solution)/shard_map/ppermute | solution.py:185
  203.7 3.2 %collective-permute-done.15 = bf16[96,432]{1,0:T(8,128)(2,1)S(1)} collective-permute-done((bf16[96,432]{1,0:T(8,128)(2,1)S(1)}, bf16[96,432]{1,0:T(8,128)(2,1)S(1)}, u32[]{:S(2)}, u32[]{:S(2)}) %collective-permute-start.15) | collective-permute-done | bytes 82976 | tf_op jit(solution)/shard_map/ppermute | solution.py:185
  206.9 0.7 fusion.19
  (57 shorter events, 4.4 us)
Async XLA Ops:
  2.2 35.7 %collective-permute-start.5 = (bf16[16,64,384]{2,1,0:T(8,128)(2,1)S(1)}, bf16[16,64,384]{2,1,0:T(8,128)(2,1)S(1)}, u32[]{:S(2)}, u32[]{:S(2)}) collective-permute-start(bf16[16,64,384]{2,1,0:T(8,128)(2,1)S(1)} %get-tuple-element.7), channel_id=1, source_target_pairs={{1,0},{2,1},{3,2},{4,3},{5,4},{6,5},{7,6},{9,8},{10,9},{11,10},{12... | collective-permute-start | bytes 2359304 | tf_op jit(solution)/shard_map/ppermute | solution.py:22
  3.5 34.4 %collective-permute-start.4 = (bf16[16,64,384]{2,1,0:T(8,128)(2,1)S(1)}, bf16[16,64,384]{2,1,0:T(8,128)(2,1)S(1)}, u32[]{:S(2)}, u32[]{:S(2)}) collective-permute-start(bf16[16,64,384]{2,1,0:T(8,128)(2,1)S(1)} %get-tuple-element.8), channel_id=1, source_target_pairs={{0,1},{1,2},{2,3},{3,4},{4,5},{5,6},{6,7},{8,9},{9,10},{10,11},{11... | collective-permute-start | bytes 2359304 | tf_op jit(solution)/shard_map/ppermute | solution.py:21
  8.4 6.4 %collective-permute-start.1 = (bf16[4,64,384]{2,1,0:T(8,128)(2,1)}, bf16[4,64,384]{2,1,0:T(8,128)(2,1)S(1)}, u32[]{:S(2)}, u32[]{:S(2)}) collective-permute-start(bf16[4,64,384]{2,1,0:T(8,128)(2,1)} %get-tuple-element.11), channel_id=1, source_target_pairs={{1,0},{2,1},{3,2},{4,3},{5,4},{6,5},{7,6},{9,8},{10,9},{11,10},{12... | collective-permute-start | bytes 589832 | tf_op jit(solution)/shard_map/ppermute | solution.py:22
  9.6 6.4 %collective-permute-start = (bf16[4,64,384]{2,1,0:T(8,128)(2,1)}, bf16[4,64,384]{2,1,0:T(8,128)(2,1)S(1)}, u32[]{:S(2)}, u32[]{:S(2)}) collective-permute-start(bf16[4,64,384]{2,1,0:T(8,128)(2,1)} %get-tuple-element.12), channel_id=1, source_target_pairs={{0,1},{1,2},{2,3},{3,4},{4,5},{5,6},{6,7},{8,9},{9,10},{10,11},{11... | collective-permute-start | bytes 589832 | tf_op jit(solution)/shard_map/ppermute | solution.py:21
  14.8 1.2 copy-start.10
  16.0 0.7 copy-start.11
  37.8 0.9 copy-start.4
  37.8 1.2 copy-start.5
  61.2 28.1 %slice-start = ((s8[5308416]{0:T(1024)(128)(4,1)}), s8[1114112]{0:T(1024)(128)(4,1)S(1)}, s32[]{:S(2)}) async-start(s8[5308416]{0:T(1024)(128)(4,1)} %bitcast.108), calls=%async_computation | async-start | bytes 2228224
  63.2 4.3 %copy-start.2 = (bf16[4,432,384]{2,1,0:T(8,128)(2,1)}, bf16[4,432,384]{2,1,0:T(8,128)(2,1)S(1)}, u32[]{:S(2)}) copy-start(bf16[4,432,384]{2,1,0:T(8,128)(2,1)S(1)} %fusion.refs_5_) | copy-start | bytes 3981316
  63.2 26.1 %collective-permute-start.6 = (bf16[4,432,384]{2,1,0:T(8,128)(2,1)S(1)}, bf16[4,432,384]{2,1,0:T(8,128)(2,1)}, u32[]{:S(2)}, u32[]{:S(2)}) collective-permute-start(bf16[4,432,384]{2,1,0:T(8,128)(2,1)S(1)} %fusion.refs_5_), channel_id=1, source_target_pairs={{0,1},{1,0},{2,3},{3,2},{4,5},{5,4},{6,7},{7,6},{8,9},{9,8},{10,11... | collective-permute-start | bytes 3981320 | tf_op jit(solution)/shard_map/ppermute | solution.py:185
  67.5 21.8 %slice-start.1 = ((s8[5308416]{0:T(1024)(128)(4,1)}), s8[4194304]{0:T(1024)(128)(4,1)S(1)}, s32[]{:S(2)}) async-start(s8[5308416]{0:T(1024)(128)(4,1)} %bitcast.108), calls=%async_computation.1 | async-start | bytes 8388608
  94.6 1.8 copy-start.1
  96.5 27.6 %copy-start.6 = (bf16[96,1728]{1,0:T(8,128)(2,1)S(1)}, bf16[96,1728]{1,0:T(8,128)(2,1)}, u32[]{:S(2)}) copy-start(bf16[96,1728]{1,0:T(8,128)(2,1)} %get-tuple-element.16.refs_6_) | copy-start | bytes 995332
  96.5 31.1 %copy-start = (bf16[64,64,384]{2,1,0:T(8,128)(2,1)S(1)}, bf16[64,64,384]{2,1,0:T(8,128)(2,1)}, u32[]{:S(2)}) copy-start(bf16[64,64,384]{2,1,0:T(8,128)(2,1)} %shard_map.67.refs_3_.refs_4_.refs_1_) | copy-start | bytes 9437188
  123.0 42.9 %collective-permute-start.10 = (bf16[4,432,384]{2,1,0:T(8,128)(2,1)}, bf16[4,432,384]{2,1,0:T(8,128)(2,1)}, u32[]{:S(2)}, u32[]{:S(2)}) collective-permute-start(bf16[4,432,384]{2,1,0:T(8,128)(2,1)} %fusion.1.refs_4_), channel_id=1, source_target_pairs={{0,1},{1,0},{2,3},{3,2},{4,5},{5,4},{6,7},{7,6},{8,9},{9,8},{10,11... | collective-permute-start | bytes 3981320 | tf_op jit(solution)/shard_map/ppermute | solution.py:185
  124.1 12.0 %collective-permute-start.9 = (bf16[96,1728]{1,0:T(8,128)(2,1)S(1)}, bf16[96,1728]{1,0:T(8,128)(2,1)}, u32[]{:S(2)}, u32[]{:S(2)}) collective-permute-start(bf16[96,1728]{1,0:T(8,128)(2,1)S(1)} %copy-done.6), channel_id=1, source_target_pairs={{0,24},{8,16},{16,8},{24,0},{1,25},{9,17},{17,9},{25,1},{2,26},{10... | collective-permute-start | bytes 995336 | tf_op jit(solution)/shard_map/ppermute | solution.py:185
  126.6 15.8 %collective-permute-start.8 = (bf16[96,1728]{1,0:T(8,128)(2,1)}, bf16[96,1728]{1,0:T(8,128)(2,1)S(1)}, u32[]{:S(2)}, u32[]{:S(2)}) collective-permute-start(bf16[96,1728]{1,0:T(8,128)(2,1)} %get-tuple-element.17.refs_5_), channel_id=1, source_target_pairs={{0,16},{8,24},{16,0},{24,8},{1,17},{9,25},{17,1},{25,9},{2,18},{10... | collective-permute-start | bytes 995336 | tf_op jit(solution)/shard_map/ppermute | solution.py:185
  127.1 15.4 %collective-permute-start.7 = (bf16[96,1728]{1,0:T(8,128)(2,1)}, bf16[96,1728]{1,0:T(8,128)(2,1)S(1)}, u32[]{:S(2)}, u32[]{:S(2)}) collective-permute-start(bf16[96,1728]{1,0:T(8,128)(2,1)} %get-tuple-element.18.refs_4_), channel_id=1, source_target_pairs={{0,8},{8,0},{16,24},{24,16},{1,9},{9,1},{17,25},{25,17},{2,10},{10... | collective-permute-start | bytes 995336 | tf_op jit(solution)/shard_map/ppermute | solution.py:185
  128.9 27.5 %collective-permute-start.3 = (bf16[16,64,384]{2,1,0:T(8,128)(2,1)}, bf16[16,64,384]{2,1,0:T(8,128)(2,1)S(1)}, u32[]{:S(2)}, u32[]{:S(2)}) collective-permute-start(bf16[16,64,384]{2,1,0:T(8,128)(2,1)} %get-tuple-element.9), channel_id=1, source_target_pairs={{1,0},{2,1},{3,2},{4,3},{5,4},{6,5},{7,6},{9,8},{10,9},{11,10},{12... | collective-permute-start | bytes 2359304 | tf_op jit(solution)/shard_map/ppermute | solution.py:22
  136.1 20.4 %collective-permute-start.2 = (bf16[16,64,384]{2,1,0:T(8,128)(2,1)}, bf16[16,64,384]{2,1,0:T(8,128)(2,1)}, u32[]{:S(2)}, u32[]{:S(2)}) collective-permute-start(bf16[16,64,384]{2,1,0:T(8,128)(2,1)} %get-tuple-element.10), channel_id=1, source_target_pairs={{0,1},{1,2},{2,3},{3,4},{4,5},{5,6},{6,7},{8,9},{9,10},{10,11},{11... | collective-permute-start | bytes 2359304 | tf_op jit(solution)/shard_map/ppermute | solution.py:21
  149.9 6.6 %copy-start.12 = (bf16[96,1,432]{2,0,1:T(8,128)(2,1)}, bf16[96,1,432]{2,0,1:T(8,128)(2,1)S(1)}, u32[]{:S(2)}) copy-start(bf16[96,1,432]{2,0,1:T(8,128)(2,1)S(1)} %copy.55) | copy-start | bytes 248836
  151.2 23.2 %collective-permute-start.17 = (bf16[96,432]{1,0:T(8,128)(2,1)}, bf16[96,432]{1,0:T(8,128)(2,1)}, u32[]{:S(2)}, u32[]{:S(2)}) collective-permute-start(bf16[96,432]{1,0:T(8,128)(2,1)} %bitcast.97.refs_5_), channel_id=1, source_target_pairs={{0,2},{1,3},{2,0},{3,1},{4,6},{5,7},{6,4},{7,5},{8,10},{9,11},{10,... | collective-permute-start | bytes 248840 | tf_op jit(solution)/shard_map/ppermute | solution.py:185
  153.9 22.4 %collective-permute-start.18 = (bf16[96,432]{1,0:T(8,128)(2,1)}, bf16[96,432]{1,0:T(8,128)(2,1)}, u32[]{:S(2)}, u32[]{:S(2)}) collective-permute-start(bf16[96,432]{1,0:T(8,128)(2,1)} %bitcast.98.refs_6_), channel_id=1, source_target_pairs={{0,4},{1,5},{2,6},{3,7},{4,0},{5,1},{6,2},{7,3},{8,12},{9,13},{10,... | collective-permute-start | bytes 248840 | tf_op jit(solution)/shard_map/ppermute | solution.py:185
  156.5 0.9 copy-start.3
  156.5 19.8 %collective-permute-start.19 = (bf16[96,432]{1,0:T(8,128)(2,1)S(1)}, bf16[96,432]{1,0:T(8,128)(2,1)}, u32[]{:S(2)}, u32[]{:S(2)}) collective-permute-start(bf16[96,432]{1,0:T(8,128)(2,1)S(1)} %bitcast.120), channel_id=1, source_target_pairs={{0,6},{1,7},{2,4},{3,5},{4,2},{5,3},{6,0},{7,1},{8,14},{9,15},{10,... | collective-permute-start | bytes 248840 | tf_op jit(solution)/shard_map/ppermute | solution.py:185
  171.4 6.6 %copy-start.7 = (bf16[96,1728]{1,0:T(8,128)(2,1)}, bf16[96,1728]{1,0:T(8,128)(2,1)S(1)}, u32[]{:S(2)}) copy-start(bf16[96,1728]{1,0:T(8,128)(2,1)S(1)} %get-tuple-element.15.refs_5_) | copy-start | bytes 995332
  171.4 6.6 %copy-start.8 = (bf16[96,1728]{1,0:T(8,128)(2,1)}, bf16[96,1728]{1,0:T(8,128)(2,1)S(1)}, u32[]{:S(2)}) copy-start(bf16[96,1728]{1,0:T(8,128)(2,1)S(1)} %get-tuple-element.14.refs_6_) | copy-start | bytes 995332
  171.4 6.6 %copy-start.9 = (bf16[96,1728]{1,0:T(8,128)(2,1)}, bf16[96,1728]{1,0:T(8,128)(2,1)S(1)}, u32[]{:S(2)}) copy-start(bf16[96,1728]{1,0:T(8,128)(2,1)S(1)} %get-tuple-element.13.refs_7_) | copy-start | bytes 995332
  171.4 23.4 %collective-permute-start.13 = (bf16[96,1728]{1,0:T(8,128)(2,1)S(1)}, bf16[96,1728]{1,0:T(8,128)(2,1)S(1)}, u32[]{:S(2)}, u32[]{:S(2)}) collective-permute-start(bf16[96,1728]{1,0:T(8,128)(2,1)S(1)} %get-tuple-element.13.refs_7_), channel_id=1, source_target_pairs={{0,24},{8,16},{16,8},{24,0},{1,25},{9,17},{17,9},{25,1},{2,26},{10... | collective-permute-start | bytes 995336 | tf_op jit(solution)/shard_map/ppermute | solution.py:185
  173.3 21.5 %collective-permute-start.12 = (bf16[96,1728]{1,0:T(8,128)(2,1)S(1)}, bf16[96,1728]{1,0:T(8,128)(2,1)S(1)}, u32[]{:S(2)}, u32[]{:S(2)}) collective-permute-start(bf16[96,1728]{1,0:T(8,128)(2,1)S(1)} %get-tuple-element.14.refs_6_), channel_id=1, source_target_pairs={{0,16},{8,24},{16,0},{24,8},{1,17},{9,25},{17,1},{25,9},{2,18},{10... | collective-permute-start | bytes 995336 | tf_op jit(solution)/shard_map/ppermute | solution.py:185
  174.4 20.4 %collective-permute-start.11 = (bf16[96,1728]{1,0:T(8,128)(2,1)S(1)}, bf16[96,1728]{1,0:T(8,128)(2,1)S(1)}, u32[]{:S(2)}, u32[]{:S(2)}) collective-permute-start(bf16[96,1728]{1,0:T(8,128)(2,1)S(1)} %get-tuple-element.15.refs_5_), channel_id=1, source_target_pairs={{0,8},{8,0},{16,24},{24,16},{1,9},{9,1},{17,25},{25,17},{2,10},{10... | collective-permute-start | bytes 995336 | tf_op jit(solution)/shard_map/ppermute | solution.py:185
  196.4 7.3 %collective-permute-start.16 = (bf16[96,432]{1,0:T(8,128)(2,1)S(1)}, bf16[96,432]{1,0:T(8,128)(2,1)S(1)}, u32[]{:S(2)}, u32[]{:S(2)}) collective-permute-start(bf16[96,432]{1,0:T(8,128)(2,1)S(1)} %bitcast.124), channel_id=1, source_target_pairs={{0,6},{1,7},{2,4},{3,5},{4,2},{5,3},{6,0},{7,1},{8,14},{9,15},{10,... | collective-permute-start | bytes 248840 | tf_op jit(solution)/shard_map/ppermute | solution.py:185
  199.4 7.5 %collective-permute-start.15 = (bf16[96,432]{1,0:T(8,128)(2,1)S(1)}, bf16[96,432]{1,0:T(8,128)(2,1)S(1)}, u32[]{:S(2)}, u32[]{:S(2)}) collective-permute-start(bf16[96,432]{1,0:T(8,128)(2,1)S(1)} %bitcast.123), channel_id=1, source_target_pairs={{0,4},{1,5},{2,6},{3,7},{4,0},{5,1},{6,2},{7,3},{8,12},{9,13},{10,... | collective-permute-start | bytes 248840 | tf_op jit(solution)/shard_map/ppermute | solution.py:185
  199.4 7.5 %collective-permute-start.14 = (bf16[96,432]{1,0:T(8,128)(2,1)S(1)}, bf16[96,432]{1,0:T(8,128)(2,1)S(1)}, u32[]{:S(2)}, u32[]{:S(2)}) collective-permute-start(bf16[96,432]{1,0:T(8,128)(2,1)S(1)} %bitcast.122), channel_id=1, source_target_pairs={{0,2},{1,3},{2,0},{3,1},{4,6},{5,7},{6,4},{7,5},{8,10},{9,11},{10,... | collective-permute-start | bytes 248840 | tf_op jit(solution)/shard_map/ppermute | solution.py:185

commit v3 on v2

--- a/solution.py
+++ b/solution.py
@@ -48,11 +48,19 @@
             scratch[2, start + r] = jnp.concatenate([line[NEAR:], zero], axis=0).astype(BF16)
 
 
-def near_kernel(tile, low, mid, high, weight, hidden, shifted):
+def flat_product(matrix, stacked):
+    product = lax.dot_general(
+        matrix, stacked, (((1,), (1,)), ((), ())), preferred_element_type=F32
+    )
+    return product.T
+
+
+def near_kernel(tile, low, mid, high, weight, hidden, shifted, matrix):
     step = pl.program_id(0)
 
     @pl.when(step == 0)
     def _():
+        matrix[...] = weight[...].T
         fill_shifted(shifted, low, mid, high)
 
     cols, channels = mid.shape[1:]
@@ -61,7 +69,7 @@
         for b in range(3):
             window = shifted[b, pl.ds(step * tile + a * NEAR, tile)]
             pieces.append(window.reshape(tile * cols, channels))
-    before = jnp.dot(jnp.concatenate(pieces, axis=1), weight[...], preferred_element_type=F32)
+    before = flat_product(matrix[...], jnp.concatenate(pieces, axis=1))
     hidden[...] = jnp.maximum(before, 0.0).astype(BF16).reshape(tile, cols, channels)
 
 
@@ -79,16 +87,17 @@
     return jnp.concatenate(pieces, axis=1)
 
 
-def output_kernel(tile, spacing, first, low, mid, high, weight, out, padded):
+def output_kernel(tile, spacing, first, low, mid, high, weight, out, padded, matrix):
     step = pl.program_id(0)
 
     @pl.when(step == 0)
     def _():
+        matrix[...] = weight[...].T
         fill_padded(padded, low, mid, high, spacing)
 
     cols, channels = mid.shape[1:]
     stacked = far_windows(padded, first + step, tile, spacing, cols, 1)
-    result = jnp.dot(stacked, weight[...], preferred_element_type=F32)
+    result = flat_product(matrix[...], stacked)
     out[...] = result.astype(BF16).reshape(tile, cols, channels)
 
 
@@ -100,45 +109,52 @@
     def _():
         fill_padded(padded, low, mid, high, spacing)
         for t in range(9):
-            turned[t * channels : (t + 1) * channels, :] = weight[
+            turned[:, t * channels : (t + 1) * channels] = weight[
                 t * channels : (t + 1) * channels, :
-            ].T
+            ]
 
     stacked = far_windows(padded, step, tile, spacing, cols, -1)
-    back = jnp.dot(stacked, turned[...], preferred_element_type=F32).astype(BF16)
+    back = flat_product(turned[...], stacked).astype(BF16)
     back = back.reshape(tile, cols, channels)
     masked[...] = jnp.where(hidden[...] > 0, back, jnp.zeros_like(back))
 
 
 def far_grad_kernel(spacing, low, mid, high, hidden, out, padded, turned):
-    tap = pl.program_id(0)
+    a = pl.program_id(0)
     rows, cols, channels = mid.shape
 
-    @pl.when(tap == 0)
+    @pl.when(a == 0)
     def _():
         fill_padded(padded, low, mid, high, spacing)
         turned[...] = hidden[...].reshape(rows * cols, channels).T
 
-    first_row = (2 - tap // 3) * spacing
-    first_col = pl.multiple_of((2 - tap % 3) * spacing, 16)
-    window = padded[pl.ds(first_row, rows), pl.ds(first_col, cols), :]
-    out[...] = jnp.dot(
-        turned[...], window.reshape(rows * cols, channels), preferred_element_type=F32
-    )
+    windows = [
+        padded[
+            pl.ds((2 - a) * spacing, rows), (2 - b) * spacing : (2 - b) * spacing + cols, :
+        ].reshape(rows * cols, channels)
+        for b in range(3)
+    ]
+    product = jnp.dot(
+        turned[...], jnp.concatenate(windows, axis=1), preferred_element_type=F32
+    )
+    for b in range(3):
+        out[b * channels : (b + 1) * channels, :] = product[:, b * channels : (b + 1) * channels]
 
 
 def near_grad_kernel(low, mid, high, masked, out, shifted, turned):
-    tap = pl.program_id(0)
+    a = pl.program_id(0)
     rows, cols, channels = mid.shape
 
-    @pl.when(tap == 0)
+    @pl.when(a == 0)
     def _():
         fill_shifted(shifted, low, mid, high)
         turned[...] = masked[...].reshape(rows * cols, channels).T
 
-    window = shifted[tap % 3, pl.ds((tap // 3) * NEAR, rows)]
+    windows = [
+        shifted[b, pl.ds(a * NEAR, rows)].reshape(rows * cols, channels) for b in range(3)
+    ]
     product = jnp.dot(
-        turned[...], window.reshape(rows * cols, channels), preferred_element_type=F32
+        turned[...], jnp.concatenate(windows, axis=1), preferred_element_type=F32
     )
     out[...] = product.T
 
@@ -204,15 +220,12 @@
     return shared(turned.reshape(dp, channels // dp, turned.shape[1]), "dp", 0)
 
 
-def split_rows(kept, sent):
-    total = joined(kept, sent, "dp", 0)
+def reduce_rows(*totals):
     outer = lax.axis_size("rows") // 2
-    pieces = jnp.moveaxis(total.reshape(total.shape[0], outer, -1), 1, 0)
-    return shared(pieces, "rows", 1)
-
-
-def finish(kept, sent):
-    return joined(kept, sent, "rows", 1).T
+    pieces = [jnp.moveaxis(t.reshape(t.shape[0], outer, -1), 1, 0) for t in totals]
+    height = pieces[0].shape[1]
+    total = joined(*shared(jnp.concatenate(pieces, axis=1), "rows", 1), "rows", 1)
+    return [total[i * height : (i + 1) * height].T for i in range(len(totals))]
 
 
 def on_device(inputs, cotangent, weight_one, weight_two):
@@ -227,10 +240,11 @@
     map_shape = jax.ShapeDtypeStruct((rows, cols, channels), BF16)
     map_spec = pl.BlockSpec((tile, cols, channels), lambda i: (i, 0, 0))
     grad_shape = jax.ShapeDtypeStruct(weight_one.shape, F32)
-    grad_spec = pl.BlockSpec((channels, channels), lambda t: (t, 0))
+    grad_spec = pl.BlockSpec((3 * channels, channels), lambda a: (a, 0))
     padded = pltpu.VMEM((rows + 2 * spacing, cols + 2 * spacing, channels), BF16)
     shifted = pltpu.VMEM((3, rows + 2 * NEAR, cols, channels), BF16)
     turned = pltpu.VMEM((channels, rows * cols), BF16)
+    matrix = pltpu.VMEM(weight_one.shape[::-1], BF16)
 
     near_low, near_high = edge_rows(picture, NEAR)
     far_low, far_high = edge_rows(upstream, spacing)
@@ -239,48 +253,49 @@
 
     hidden = run(
         functools.partial(near_kernel, tile),
-        map_shape, steps, map_spec, [shifted],
+        map_shape, steps, map_spec, [shifted, matrix],
         (*near, weight_one), [None] * 4, flops,
     )
     hidden_low, hidden_high = edge_rows(hidden, spacing)
     grad_two = run(
         functools.partial(far_grad_kernel, spacing),
-        grad_shape, 9, grad_spec, [padded, turned],
+        grad_shape, 3, grad_spec, [padded, turned],
         (*far, hidden), [None] * 4, flops,
     )
     pair_two = split_pair(grad_two)
     masked = run(
         functools.partial(back_kernel, tile, spacing),
-        map_shape, steps, map_spec, [padded, pltpu.VMEM(weight_two.shape, BF16)],
+        map_shape, steps, map_spec, [padded, matrix],
         (*far, weight_two, hidden), [None] * 4 + [map_spec], flops, pair_two[1],
     )
     samples_two = split_samples(*pair_two)
     grad_one = run(
         near_grad_kernel,
-        grad_shape, 9, grad_spec, [shifted, turned],
+        grad_shape, 3, grad_spec, [shifted, turned],
         (*near, masked), [None] * 4, flops, samples_two[1],
     )
     pair_one = split_pair(grad_one)
-    rows_two = split_rows(*samples_two)
     early = max(1, steps // 4)
     output = run(
         functools.partial(output_kernel, tile, spacing, 0),
-        map_shape, early, map_spec, [padded],
+        map_shape, early, map_spec, [padded, matrix],
         (hidden_low, hidden, hidden_high, weight_two), [None] * 4,
-        flops * early // steps, pair_one[1] + rows_two[1],
-    )
-    kept_one, output = lax.optimization_barrier((pair_one[0], output))
+        flops * early // steps, pair_one[1],
+    )
+    kept_one, kept_two, output = lax.optimization_barrier((pair_one[0], samples_two[0], output))
     samples_one = split_samples(kept_one, pair_one[1])
+    total_two = joined(kept_two, samples_two[1], "dp", 0)
     if early < steps:
         output = run(
             functools.partial(output_kernel, tile, spacing, early),
             map_shape, steps - early,
-            pl.BlockSpec((tile, cols, channels), lambda i: (i + early, 0, 0)), [padded],
+            pl.BlockSpec((tile, cols, channels), lambda i: (i + early, 0, 0)), [padded, matrix],
             (hidden_low, hidden, hidden_high, weight_two), [None] * 4,
             flops * (steps - early) // steps, [output] + samples_one[1], {4: 0},
         )
-    grad_two = finish(*rows_two)
-    grad_one = finish(*split_rows(*samples_one))
+    kept_one, total_two, output = lax.optimization_barrier((samples_one[0], total_two, output))
+    total_one = joined(kept_one, samples_one[1], "dp", 0)
+    grad_one, grad_two = reduce_rows(total_one, total_two)
     return (output[None], grad_one * factor, grad_two * factor)
 
 

time: 208 us -> 192 us (0.923)
  Pallas kernels: 114 us -> 101 us
  local copies, waits for them, and re-layouts: 30.2 us -> 22.7 us
  waiting for transfers between devices: 15.2 us -> 21.5 us
  other arithmetic: 10.9 us -> 8.24 us
    pallas_call x6, Pallas kernels: 114 us -> 101 us  [run(): pl.pallas_call(body, out_shape=out_shape, grid=(grid,), in_specs=[whole i...]
    another operation x4 -> x0, local copies, waits for them, and re-layouts: 4.31 us -> none
    ppermute x3, waiting for transfers between devices: 0.01 us -> 4.16 us  [edge_rows(): high = lax.ppermute(block[:width], 'rows', backward)]
    unnamed x36 -> x24, local copies, waits for them, and re-layouts: 4.93 us -> 1.27 us
    ppermute x14 -> x11, waiting for transfers between devices: 14 us -> 17.3 us  [joined(): total = total + lax.ppermute(piece, axis, pairs).astype(F32)]
    convert_element_type x2, local copies, waits for them, and re-layouts: 1.23 us -> 3.66 us  [shared(): lax.dynamic_index_in_dim(pieces, mine ^ k, 0, keepdims=False).astype(BF16)]
    squeeze x0 -> x2, local copies, waits for them, and re-layouts: none -> 2.29 us  [shared(): kept = lax.dynamic_index_in_dim(pieces, mine, 0, keepdims=False)]
    ppermute x14 -> x11, starting transfers between devices: 22.2 us -> 24.1 us  [joined(): total = total + lax.ppermute(piece, axis, pairs).astype(F32)]
  transfers between devices with their start and end apart: 20 -> 17, of which waited for: 6 -> 4; matrix products, arithmetic and copies ran while one was open for 11% -> 7% of each run, Pallas kernels for 33% -> 32%
where the time goes in v3:
time: 192 us
  Pallas kernels  101 us (53%)
  starting transfers between devices  37.7 us (20%)
  local copies, waits for them, and re-layouts  22.7 us (12%)
  waiting for transfers between devices  21.5 us (11%)
  other arithmetic  8.24 us (4%)
    pallas_call x6, Pallas kernels, run(): pl.pallas_call(body, out_shape=out_shape, grid=(grid,), in_specs=[whole i...  101 us
    ppermute x11, starting transfers between devices, joined(): total = total + lax.ppermute(piece, axis, pairs).astype(F32)  24.1 us
    ppermute x11, waiting for transfers between devices, joined(): total = total + lax.ppermute(piece, axis, pairs).astype(F32)  17.3 us
    ppermute x3, starting transfers between devices, edge_rows(): low = lax.ppermute(block[block.shape[0] - width:], 'rows', forward)  9.71 us
    add x5, other arithmetic, joined(): total = total + lax.ppermute(piece, axis, pairs).astype(F32)  7.37 us
    slice x3, local copies, waits for them, and re-layouts, edge_rows(): high = lax.ppermute(block[:width], 'rows', backward)  4.67 us
    reshape x2, local copies, waits for them, and re-layouts, split_samples(): turned = total.reshape(-1, channels).T  4.56 us
    ppermute x3, waiting for transfers between devices, edge_rows(): high = lax.ppermute(block[:width], 'rows', backward)  4.16 us
  transfers between devices with their start and end apart: 17, of which 4 were waited for; matrix products, arithmetic and copies ran while one was open for 7% of the time, Pallas kernels for 32%

profile of v3, /device:TPU:0, one launch (start us, length us, event | category | flops | bytes accessed | tf_op | source)
XLA Modules:
  0.0 191.6 jit_solution(13335742015650746675)
XLA Ops:
  0.6 1.5 slice_bitcast_fusion
  2.2 2.4 %collective-permute-start.2 = (bf16[16,64,384]{2,1,0:T(8,128)(2,1)S(1)}, bf16[16,64,384]{2,1,0:T(8,128)(2,1)S(1)}, u32[]{:S(2)}, u32[]{:S(2)}) collective-permute-start(bf16[16,64,384]{2,1,0:T(8,128)(2,1)S(1)} %get-tuple-element.18), channel_id=1, source_target_pairs={{0,1},{1,2},{2,3},{3,4},{4,5},{5,6},{6,7},{8,9},{9,10},{10,11},{11... | collective-permute-start | bytes 2359304 | tf_op jit(solution)/shard_map/ppermute | solution.py:21
  4.6 1.3 collective-permute-start.3
  5.9 1.8 slice_bitcast_fusion.2
  7.7 5.2 %collective-permute-start = (bf16[4,64,384]{2,1,0:T(8,128)(2,1)}, bf16[4,64,384]{2,1,0:T(8,128)(2,1)S(1)}, u32[]{:S(2)}, u32[]{:S(2)}) collective-permute-start(bf16[4,64,384]{2,1,0:T(8,128)(2,1)} %get-tuple-element.20), channel_id=1, source_target_pairs={{0,1},{1,2},{2,3},{3,4},{4,5},{5,6},{6,7},{8,9},{9,10},{10,11},{11... | collective-permute-start | bytes 589832 | tf_op jit(solution)/shard_map/ppermute | solution.py:21
  12.9 1.3 collective-permute-start.1
  14.2 3.6 %collective-permute-done.1.refs_2_ = bf16[4,64,384]{2,1,0:T(8,128)(2,1)} collective-permute-done((bf16[4,64,384]{2,1,0:T(8,128)(2,1)}, bf16[4,64,384]{2,1,0:T(8,128)(2,1)}, u32[]{:S(2)}, u32[]{:S(2)}) %collective-permute-start.1) | collective-permute-done | bytes 196640 | tf_op jit(solution)/shard_map/ppermute | solution.py:22
  17.8 19.3 %shard_map.67.refs_3_.refs_4_.refs_1_ = bf16[64,64,384]{2,1,0:T(8,128)(2,1)} custom-call(bf16[4,64,384]{2,1,0:T(8,128)(2,1)} %copy-done.7, bf16[64,64,384]{2,1,0:T(8,128)(2,1)} %bitcast.85, bf16[4,64,384]{2,1,0:T(8,128)(2,1)} %collective-permute-done.1.refs_2_, bf16[3456,384]{1,0:T(8,128)(2,1)} %refs_3_.4), custom_call_target="tpu_custom_call" | custom-call | flops 169869312 | bytes 1024 | tf_op jit(solution)/shard_map/pallas_call | solution.py:169
  37.1 0.9 copy-done.5
  37.9 0.3 copy-done.6
  38.3 18.7 %shard_map.68 = f32[3456,384]{1,0:T(8,128)} custom-call(bf16[16,64,384]{2,1,0:T(8,128)(2,1)} %copy-done.5, bf16[64,64,384]{2,1,0:T(8,128)(2,1)} %bitcast.75, bf16[16,64,384]{2,1,0:T(8,128)(2,1)} %copy-done.6, bf16[64,64,384]{2,1,0:T(8,128)(2,1)} %shard_map.67.refs_3_.refs_4_.refs_1_), custom_call_target="tpu_custom_call" | custom-call | flops 169869312 | bytes 1024 | tf_op jit(solution)/shard_map/pallas_call | solution.py:169
  57.0 2.0 %fusion.refs_5_ = bf16[4,432,384]{2,1,0:T(8,128)(2,1)S(1)} fusion(f32[4,2,432,384]{3,2,1,0:T(8,128)} %bitcast.81, s32[]{:T(128)S(6)} %select_n.39), kind=kLoop, calls=%fused_computation.13 | loop fusion | bytes 2654212 | tf_op jit(solution)/shard_map/convert_element_type | solution.py:211
  59.0 5.0 %collective-permute-start.4 = (bf16[4,432,384]{2,1,0:T(8,128)(2,1)S(1)}, bf16[4,432,384]{2,1,0:T(8,128)(2,1)}, u32[]{:S(2)}, u32[]{:S(2)}) collective-permute-start(bf16[4,432,384]{2,1,0:T(8,128)(2,1)S(1)} %fusion.refs_5_), channel_id=1, source_target_pairs={{0,1},{1,0},{2,3},{3,2},{4,5},{5,4},{6,7},{7,6},{8,9},{9,8},{10,11... | collective-permute-start | bytes 3981320 | tf_op jit(solution)/shard_map/ppermute | solution.py:201
  64.0 18.8 %shard_map.69.refs_3_ = bf16[64,64,384]{2,1,0:T(8,128)(2,1)} custom-call(bf16[16,64,384]{2,1,0:T(8,128)(2,1)} %copy-done.5, bf16[64,64,384]{2,1,0:T(8,128)(2,1)} %bitcast.76, bf16[16,64,384]{2,1,0:T(8,128)(2,1)} %copy-done.6, bf16[3456,384]{1,0:T(8,128)(2,1)} %refs_3_.7, bf16[64,64,384]{2,1,0:T(8,128)(2,1)} %shard_map.67.refs_3_.refs_4_.refs_1_, ...), custom_call_target="tpu_custom_call" | custom-call | flops 169869312 | bytes 1024 | tf_op jit(solution)/shard_map/pallas_call | solution.py:169
  82.8 3.0 %bitcast_add_fusion = f32[4,432,384]{2,1,0:T(8,128)} fusion(bf16[4,432,384]{2,1,0:T(8,128)(2,1)} %collective-permute-done.4, f32[4,2,432,384]{3,2,1,0:T(8,128)S(1)} %bitcast.84, s32[]{:T(128)S(6)} %select_n.40), kind=kLoop, calls=%fused_computation.2 | loop fusion | flops 1327104 | bytes 6635524 | tf_op jit(solution)/shard_map/add | solution.py:201
  85.9 2.2 %copy.13 = f32[1728,384]{0,1:T(8,128)S(1)} copy(f32[1728,384]{1,0:T(8,128)} %bitcast.89) | data formatting | bytes 5308416 | tf_op jit(solution)/shard_map/reshape | solution.py:219
  88.1 1.1 fusion.15
  89.2 19.6 %shard_map.70 = f32[3456,384]{1,0:T(8,128)} custom-call(bf16[4,64,384]{2,1,0:T(8,128)(2,1)} %copy-done.7, bf16[64,64,384]{2,1,0:T(8,128)(2,1)} %bitcast.86, bf16[4,64,384]{2,1,0:T(8,128)(2,1)} %collective-permute-done.1.refs_2_, bf16[64,64,384]{2,1,0:T(8,128)(2,1)} %shard_map.69.refs_3_, bf16[96,1728]{1,0:T(8,128)(2,1)} %get-tuple-element.26.refs_4_, ...), custom_call_target="tpu_custom_call" | custom-call | flops 169869312 | bytes 1024 | tf_op jit(solution)/shard_map/pallas_call | solution.py:169
  108.9 1.9 fusion.1.refs_4_
  110.8 1.1 collective-permute-start.7
  111.9 1.3 fusion.24
  113.2 2.1 %collective-permute-start.5 = (bf16[16,64,384]{2,1,0:T(8,128)(2,1)}, bf16[16,64,384]{2,1,0:T(8,128)(2,1)S(1)}, u32[]{:S(2)}, u32[]{:S(2)}) collective-permute-start(bf16[16,64,384]{2,1,0:T(8,128)(2,1)} %get-tuple-element.16), channel_id=1, source_target_pairs={{0,1},{1,2},{2,3},{3,4},{4,5},{5,6},{6,7},{8,9},{9,10},{10,11},{11... | collective-permute-start | bytes 2359304 | tf_op jit(solution)/shard_map/ppermute | solution.py:21
  115.4 1.3 collective-permute-start.6
  116.7 2.5 %collective-permute-start.10 = (bf16[96,1728]{1,0:T(8,128)(2,1)}, bf16[96,1728]{1,0:T(8,128)(2,1)}, u32[]{:S(2)}, u32[]{:S(2)}) collective-permute-start(bf16[96,1728]{1,0:T(8,128)(2,1)} %get-tuple-element.24.refs_6_), channel_id=1, source_target_pairs={{0,24},{8,16},{16,8},{24,0},{1,25},{9,17},{17,9},{25,1},{2,26},{10... | collective-permute-start | bytes 995336 | tf_op jit(solution)/shard_map/ppermute | solution.py:201
  119.2 0.5 collective-permute-start.9
  119.7 0.5 collective-permute-start.8
  120.3 0.6 collective-permute-done.6.refs_2_
  120.8 8.6 %shard_map.71.refs_4_ = bf16[64,64,384]{2,1,0:T(8,128)(2,1)} custom-call(bf16[16,64,384]{2,1,0:T(8,128)(2,1)} %copy-done.4, bf16[64,64,384]{2,1,0:T(8,128)(2,1)} %shard_map.67.refs_3_.refs_4_.refs_1_, bf16[16,64,384]{2,1,0:T(8,128)(2,1)} %collective-permute-done.6.refs_2_, bf16[3456,384]{1,0:T(8,128)(2,1)} %refs_3_.7, bf16[4,432,384]{2,1,0:T(8,128)(2,1)} %copy-done.3), custom_call_target="tpu_custom_call" | custom-call | flops 42467328 | bytes 1024 | tf_op jit(solution)/shard_map/pallas_call | solution.py:169
  129.5 0.2 dynamic-slice_bitcast_fusion
  129.7 1.2 dynamic-slice_bitcast_fusion.2
  130.8 1.6 convert_add_fusion
  132.4 2.3 %copy.15 = f32[1728,384]{0,1:T(8,128)} copy(f32[1728,384]{1,0:T(8,128)S(1)} %bitcast.88) | data formatting | bytes 5308416 | tf_op jit(solution)/shard_map/reshape | solution.py:219
  134.8 2.5 %fusion.18 = (bf16[96,1728]{1,0:T(8,128)(2,1)}, bf16[96,1728]{1,0:T(8,128)(2,1)}, bf16[96,1728]{1,0:T(8,128)(2,1)}) fusion(f32[4,96,1728]{2,1,0:T(8,128)} %bitcast.92, s32[]{:T(128)S(6)} %select_n.43, s32[]{:T(128)S(6)} %select_n.42, s32[]{:T(128)S(6)} %select_n.41), kind=kLoop, calls=%fused_computation.45 | loop fusion | bytes 1990668 | tf_op jit(solution)/shard_map/convert_element_type | solution.py:190
  137.3 2.4 %collective-permute-start.13 = (bf16[96,1728]{1,0:T(8,128)(2,1)}, bf16[96,1728]{1,0:T(8,128)(2,1)}, u32[]{:S(2)}, u32[]{:S(2)}) collective-permute-start(bf16[96,1728]{1,0:T(8,128)(2,1)} %get-tuple-element.21.refs_7_), channel_id=1, source_target_pairs={{0,24},{8,16},{16,8},{24,0},{1,25},{9,17},{17,9},{25,1},{2,26},{10... | collective-permute-start | bytes 995336 | tf_op jit(solution)/shard_map/ppermute | solution.py:201
  139.8 0.5 collective-permute-start.12
  140.3 0.5 collective-permute-start.11
  140.8 1.3 convert_add_fusion.2
  142.1 15.5 %shard_map.72 = bf16[64,64,384]{2,1,0:T(8,128)(2,1)} custom-call(bf16[16,64,384]{2,1,0:T(8,128)(2,1)} %copy-done.4, bf16[64,64,384]{2,1,0:T(8,128)(2,1)} %shard_map.67.refs_3_.refs_4_.refs_1_, bf16[16,64,384]{2,1,0:T(8,128)(2,1)} %collective-permute-done.6.refs_2_, bf16[3456,384]{1,0:T(8,128)(2,1)} %refs_3_.7, ...), custom_call_target="tpu_custom_call", output_to_operand_aliasing={{}: (4, {})} | custom-call | flops 127401984 | bytes 1024 | tf_op jit(solution)/shard_map/pallas_call | solution.py:169
  157.6 1.1 dynamic-slice_bitcast_fusion.1
  158.8 0.9 reshape.60
  159.7 1.3 convert_add_fusion.1
  161.0 0.9 reshape.59
  161.9 0.5 copy_bitcast_fusion
  162.4 9.9 %collective-permute-start.16 = (bf16[192,432]{1,0:T(8,128)(2,1)S(1)}, bf16[192,432]{1,0:T(8,128)(2,1)S(1)}, u32[]{:S(2)}, u32[]{:S(2)}) collective-permute-start(bf16[192,432]{1,0:T(8,128)(2,1)S(1)} %get-tuple-element.29), channel_id=1, source_target_pairs={{0,6},{1,7},{2,4},{3,5},{4,2},{5,3},{6,0},{7,1},{8,14},{9,15},{10,... | collective-permute-start | bytes 497672 | tf_op jit(solution)/shard_map/ppermute | solution.py:201
  172.3 0.9 collective-permute-start.15
  173.4 4.4 %collective-permute-done.16 = bf16[192,432]{1,0:T(8,128)(2,1)S(1)} collective-permute-done((bf16[192,432]{1,0:T(8,128)(2,1)S(1)}, bf16[192,432]{1,0:T(8,128)(2,1)S(1)}, u32[]{:S(2)}, u32[]{:S(2)}) %collective-permute-start.16) | collective-permute-done | bytes 165920 | tf_op jit(solution)/shard_map/ppermute | solution.py:201
  177.7 13.0 %collective-permute-done.15 = bf16[192,432]{1,0:T(8,128)(2,1)S(1)} collective-permute-done((bf16[192,432]{1,0:T(8,128)(2,1)S(1)}, bf16[192,432]{1,0:T(8,128)(2,1)S(1)}, u32[]{:S(2)}, u32[]{:S(2)}) %collective-permute-start.15) | collective-permute-done | bytes 165920 | tf_op jit(solution)/shard_map/ppermute | solution.py:201
  190.8 0.8 fusion.19
  (40 shorter events, 0.4 us)
Async XLA Ops:
  2.2 34.9 %collective-permute-start.2 = (bf16[16,64,384]{2,1,0:T(8,128)(2,1)S(1)}, bf16[16,64,384]{2,1,0:T(8,128)(2,1)S(1)}, u32[]{:S(2)}, u32[]{:S(2)}) collective-permute-start(bf16[16,64,384]{2,1,0:T(8,128)(2,1)S(1)} %get-tuple-element.18), channel_id=1, source_target_pairs={{0,1},{1,2},{2,3},{3,4},{4,5},{5,6},{6,7},{8,9},{9,10},{10,11},{11... | collective-permute-start | bytes 2359304 | tf_op jit(solution)/shard_map/ppermute | solution.py:21
  4.6 32.5 %collective-permute-start.3 = (bf16[16,64,384]{2,1,0:T(8,128)(2,1)S(1)}, bf16[16,64,384]{2,1,0:T(8,128)(2,1)S(1)}, u32[]{:S(2)}, u32[]{:S(2)}) collective-permute-start(bf16[16,64,384]{2,1,0:T(8,128)(2,1)S(1)} %get-tuple-element.17), channel_id=1, source_target_pairs={{1,0},{2,1},{3,2},{4,3},{5,4},{6,5},{7,6},{9,8},{10,9},{11,10},{12... | collective-permute-start | bytes 2359304 | tf_op jit(solution)/shard_map/ppermute | solution.py:22
  7.7 6.5 %collective-permute-start = (bf16[4,64,384]{2,1,0:T(8,128)(2,1)}, bf16[4,64,384]{2,1,0:T(8,128)(2,1)S(1)}, u32[]{:S(2)}, u32[]{:S(2)}) collective-permute-start(bf16[4,64,384]{2,1,0:T(8,128)(2,1)} %get-tuple-element.20), channel_id=1, source_target_pairs={{0,1},{1,2},{2,3},{3,4},{4,5},{5,6},{6,7},{8,9},{9,10},{10,11},{11... | collective-permute-start | bytes 589832 | tf_op jit(solution)/shard_map/ppermute | solution.py:21
  12.9 4.9 %collective-permute-start.1 = (bf16[4,64,384]{2,1,0:T(8,128)(2,1)}, bf16[4,64,384]{2,1,0:T(8,128)(2,1)}, u32[]{:S(2)}, u32[]{:S(2)}) collective-permute-start(bf16[4,64,384]{2,1,0:T(8,128)(2,1)} %get-tuple-element.19), channel_id=1, source_target_pairs={{1,0},{2,1},{3,2},{4,3},{5,4},{6,5},{7,6},{9,8},{10,9},{11,10},{12... | collective-permute-start | bytes 589832 | tf_op jit(solution)/shard_map/ppermute | solution.py:22
  14.2 3.6 %copy-start.7 = (bf16[4,64,384]{2,1,0:T(8,128)(2,1)}, bf16[4,64,384]{2,1,0:T(8,128)(2,1)S(1)}, u32[]{:S(2)}) copy-start(bf16[4,64,384]{2,1,0:T(8,128)(2,1)S(1)} %collective-permute-done.refs_0_) | copy-start | bytes 589828
  37.0 0.9 copy-start.5
  37.0 1.2 copy-start.6
  57.0 25.8 %slice-start.2 = ((s8[5308416]{0:T(1024)(128)(4,1)}), s8[1114112]{0:T(1024)(128)(4,1)S(1)}, s32[]{:S(2)}) async-start(s8[5308416]{0:T(1024)(128)(4,1)} %bitcast.82), calls=%async_computation.2 | async-start | bytes 2228224
  59.0 5.0 %copy-start.2 = (bf16[4,432,384]{2,1,0:T(8,128)(2,1)}, bf16[4,432,384]{2,1,0:T(8,128)(2,1)S(1)}, u32[]{:S(2)}) copy-start(bf16[4,432,384]{2,1,0:T(8,128)(2,1)S(1)} %fusion.refs_5_) | copy-start | bytes 3981316
  59.0 23.8 %collective-permute-start.4 = (bf16[4,432,384]{2,1,0:T(8,128)(2,1)S(1)}, bf16[4,432,384]{2,1,0:T(8,128)(2,1)}, u32[]{:S(2)}, u32[]{:S(2)}) collective-permute-start(bf16[4,432,384]{2,1,0:T(8,128)(2,1)S(1)} %fusion.refs_5_), channel_id=1, source_target_pairs={{0,1},{1,0},{2,3},{3,2},{4,5},{5,4},{6,7},{7,6},{8,9},{9,8},{10,11... | collective-permute-start | bytes 3981320 | tf_op jit(solution)/shard_map/ppermute | solution.py:201
  64.0 18.8 %slice-start.3 = ((s8[5308416]{0:T(1024)(128)(4,1)}), s8[4194304]{0:T(1024)(128)(4,1)S(1)}, s32[]{:S(2)}) async-start(s8[5308416]{0:T(1024)(128)(4,1)} %bitcast.82), calls=%async_computation.3 | async-start | bytes 8388608
  88.1 20.8 %copy-start.1 = (f32[1728,384]{0,1:T(8,128)}, f32[1728,384]{0,1:T(8,128)S(1)}, u32[]{:S(2)}) copy-start(f32[1728,384]{0,1:T(8,128)S(1)} %copy.13) | copy-start | bytes 7962628
  89.2 22.7 %copy-start = (bf16[64,64,384]{2,1,0:T(8,128)(2,1)S(1)}, bf16[64,64,384]{2,1,0:T(8,128)(2,1)}, u32[]{:S(2)}) copy-start(bf16[64,64,384]{2,1,0:T(8,128)(2,1)} %shard_map.67.refs_3_.refs_4_.refs_1_) | copy-start | bytes 9437188
  110.8 10.1 %copy-start.3 = (bf16[4,432,384]{2,1,0:T(8,128)(2,1)}, bf16[4,432,384]{2,1,0:T(8,128)(2,1)S(1)}, u32[]{:S(2)}) copy-start(bf16[4,432,384]{2,1,0:T(8,128)(2,1)S(1)} %fusion.1.refs_4_) | copy-start | bytes 3981316
  110.8 20.1 %collective-permute-start.7 = (bf16[4,432,384]{2,1,0:T(8,128)(2,1)S(1)}, bf16[4,432,384]{2,1,0:T(8,128)(2,1)}, u32[]{:S(2)}, u32[]{:S(2)}) collective-permute-start(bf16[4,432,384]{2,1,0:T(8,128)(2,1)S(1)} %fusion.1.refs_4_), channel_id=1, source_target_pairs={{0,1},{1,0},{2,3},{3,2},{4,5},{5,4},{6,7},{7,6},{8,9},{9,8},{10,11... | collective-permute-start | bytes 3981320 | tf_op jit(solution)/shard_map/ppermute | solution.py:201
  113.2 6.5 %collective-permute-start.5 = (bf16[16,64,384]{2,1,0:T(8,128)(2,1)}, bf16[16,64,384]{2,1,0:T(8,128)(2,1)S(1)}, u32[]{:S(2)}, u32[]{:S(2)}) collective-permute-start(bf16[16,64,384]{2,1,0:T(8,128)(2,1)} %get-tuple-element.16), channel_id=1, source_target_pairs={{0,1},{1,2},{2,3},{3,4},{4,5},{5,6},{6,7},{8,9},{9,10},{10,11},{11... | collective-permute-start | bytes 2359304 | tf_op jit(solution)/shard_map/ppermute | solution.py:21
  115.4 5.5 %collective-permute-start.6 = (bf16[16,64,384]{2,1,0:T(8,128)(2,1)}, bf16[16,64,384]{2,1,0:T(8,128)(2,1)}, u32[]{:S(2)}, u32[]{:S(2)}) collective-permute-start(bf16[16,64,384]{2,1,0:T(8,128)(2,1)} %get-tuple-element.15), channel_id=1, source_target_pairs={{1,0},{2,1},{3,2},{4,3},{5,4},{6,5},{7,6},{9,8},{10,9},{11,10},{12... | collective-permute-start | bytes 2359304 | tf_op jit(solution)/shard_map/ppermute | solution.py:22
  116.7 12.8 %slice-start = ((s8[5308416]{0:T(1024)(128)(4,1)}), s8[1114112]{0:T(1024)(128)(4,1)S(1)}, s32[]{:S(2)}) async-start(s8[5308416]{0:T(1024)(128)(4,1)} %bitcast.78), calls=%async_computation | async-start | bytes 2228224
  116.7 12.8 %slice-start.1 = ((s8[5308416]{0:T(1024)(128)(4,1)}), s8[4194304]{0:T(1024)(128)(4,1)S(1)}, s32[]{:S(2)}) async-start(s8[5308416]{0:T(1024)(128)(4,1)} %bitcast.78), calls=%async_computation.1 | async-start | bytes 8388608
  116.7 23.6 %collective-permute-start.10 = (bf16[96,1728]{1,0:T(8,128)(2,1)}, bf16[96,1728]{1,0:T(8,128)(2,1)}, u32[]{:S(2)}, u32[]{:S(2)}) collective-permute-start(bf16[96,1728]{1,0:T(8,128)(2,1)} %get-tuple-element.24.refs_6_), channel_id=1, source_target_pairs={{0,24},{8,16},{16,8},{24,0},{1,25},{9,17},{17,9},{25,1},{2,26},{10... | collective-permute-start | bytes 995336 | tf_op jit(solution)/shard_map/ppermute | solution.py:201
  119.2 21.6 %collective-permute-start.9 = (bf16[96,1728]{1,0:T(8,128)(2,1)}, bf16[96,1728]{1,0:T(8,128)(2,1)}, u32[]{:S(2)}, u32[]{:S(2)}) collective-permute-start(bf16[96,1728]{1,0:T(8,128)(2,1)} %get-tuple-element.25.refs_5_), channel_id=1, source_target_pairs={{0,16},{8,24},{16,0},{24,8},{1,17},{9,25},{17,1},{25,9},{2,18},{10... | collective-permute-start | bytes 995336 | tf_op jit(solution)/shard_map/ppermute | solution.py:201
  119.7 1.1 copy-start.4
  119.7 21.1 %collective-permute-start.8 = (bf16[96,1728]{1,0:T(8,128)(2,1)}, bf16[96,1728]{1,0:T(8,128)(2,1)}, u32[]{:S(2)}, u32[]{:S(2)}) collective-permute-start(bf16[96,1728]{1,0:T(8,128)(2,1)} %get-tuple-element.26.refs_4_), channel_id=1, source_target_pairs={{0,8},{8,0},{16,24},{24,16},{1,9},{9,1},{17,25},{25,17},{2,10},{10... | collective-permute-start | bytes 995336 | tf_op jit(solution)/shard_map/ppermute | solution.py:201
  137.3 22.3 %collective-permute-start.13 = (bf16[96,1728]{1,0:T(8,128)(2,1)}, bf16[96,1728]{1,0:T(8,128)(2,1)}, u32[]{:S(2)}, u32[]{:S(2)}) collective-permute-start(bf16[96,1728]{1,0:T(8,128)(2,1)} %get-tuple-element.21.refs_7_), channel_id=1, source_target_pairs={{0,24},{8,16},{16,8},{24,0},{1,25},{9,17},{17,9},{25,1},{2,26},{10... | collective-permute-start | bytes 995336 | tf_op jit(solution)/shard_map/ppermute | solution.py:201
  139.8 19.9 %collective-permute-start.12 = (bf16[96,1728]{1,0:T(8,128)(2,1)}, bf16[96,1728]{1,0:T(8,128)(2,1)}, u32[]{:S(2)}, u32[]{:S(2)}) collective-permute-start(bf16[96,1728]{1,0:T(8,128)(2,1)} %get-tuple-element.22.refs_6_), channel_id=1, source_target_pairs={{0,16},{8,24},{16,0},{24,8},{1,17},{9,25},{17,1},{25,9},{2,18},{10... | collective-permute-start | bytes 995336 | tf_op jit(solution)/shard_map/ppermute | solution.py:201
  140.3 19.4 %collective-permute-start.11 = (bf16[96,1728]{1,0:T(8,128)(2,1)}, bf16[96,1728]{1,0:T(8,128)(2,1)}, u32[]{:S(2)}, u32[]{:S(2)}) collective-permute-start(bf16[96,1728]{1,0:T(8,128)(2,1)} %get-tuple-element.23.refs_5_), channel_id=1, source_target_pairs={{0,8},{8,0},{16,24},{24,16},{1,9},{9,1},{17,25},{25,17},{2,10},{10... | collective-permute-start | bytes 995336 | tf_op jit(solution)/shard_map/ppermute | solution.py:201
  162.4 15.3 %collective-permute-start.16 = (bf16[192,432]{1,0:T(8,128)(2,1)S(1)}, bf16[192,432]{1,0:T(8,128)(2,1)S(1)}, u32[]{:S(2)}, u32[]{:S(2)}) collective-permute-start(bf16[192,432]{1,0:T(8,128)(2,1)S(1)} %get-tuple-element.29), channel_id=1, source_target_pairs={{0,6},{1,7},{2,4},{3,5},{4,2},{5,3},{6,0},{7,1},{8,14},{9,15},{10,... | collective-permute-start | bytes 497672 | tf_op jit(solution)/shard_map/ppermute | solution.py:201
  172.3 18.4 %collective-permute-start.15 = (bf16[192,432]{1,0:T(8,128)(2,1)S(1)}, bf16[192,432]{1,0:T(8,128)(2,1)S(1)}, u32[]{:S(2)}, u32[]{:S(2)}) collective-permute-start(bf16[192,432]{1,0:T(8,128)(2,1)S(1)} %get-tuple-element.28), channel_id=1, source_target_pairs={{0,4},{1,5},{2,6},{3,7},{4,0},{5,1},{6,2},{7,3},{8,12},{9,13},{10,... | collective-permute-start | bytes 497672 | tf_op jit(solution)/shard_map/ppermute | solution.py:201
  173.3 17.4 %collective-permute-start.14 = (bf16[192,432]{1,0:T(8,128)(2,1)S(1)}, bf16[192,432]{1,0:T(8,128)(2,1)S(1)}, u32[]{:S(2)}, u32[]{:S(2)}) collective-permute-start(bf16[192,432]{1,0:T(8,128)(2,1)S(1)} %get-tuple-element.27), channel_id=1, source_target_pairs={{0,2},{1,3},{2,0},{3,1},{4,6},{5,7},{6,4},{7,5},{8,10},{9,11},{10,... | collective-permute-start | bytes 497672 | tf_op jit(solution)/shard_map/ppermute | solution.py:201

commit v4 on v3

--- a/solution.py
+++ b/solution.py
@@ -220,12 +220,10 @@
     return shared(turned.reshape(dp, channels // dp, turned.shape[1]), "dp", 0)
 
 
-def reduce_rows(*totals):
+def split_rows(total):
     outer = lax.axis_size("rows") // 2
-    pieces = [jnp.moveaxis(t.reshape(t.shape[0], outer, -1), 1, 0) for t in totals]
-    height = pieces[0].shape[1]
-    total = joined(*shared(jnp.concatenate(pieces, axis=1), "rows", 1), "rows", 1)
-    return [total[i * height : (i + 1) * height].T for i in range(len(totals))]
+    pieces = jnp.moveaxis(total.reshape(total.shape[0], outer, -1), 1, 0)
+    return shared(pieces, "rows", 1)
 
 
 def on_device(inputs, cotangent, weight_one, weight_two):
@@ -284,18 +282,19 @@
     )
     kept_one, kept_two, output = lax.optimization_barrier((pair_one[0], samples_two[0], output))
     samples_one = split_samples(kept_one, pair_one[1])
-    total_two = joined(kept_two, samples_two[1], "dp", 0)
+    rows_two = split_rows(joined(kept_two, samples_two[1], "dp", 0))
     if early < steps:
         output = run(
             functools.partial(output_kernel, tile, spacing, early),
             map_shape, steps - early,
             pl.BlockSpec((tile, cols, channels), lambda i: (i + early, 0, 0)), [padded, matrix],
             (hidden_low, hidden, hidden_high, weight_two), [None] * 4,
-            flops * (steps - early) // steps, [output] + samples_one[1], {4: 0},
+            flops * (steps - early) // steps, [output] + samples_one[1] + rows_two[1], {4: 0},
         )
-    kept_one, total_two, output = lax.optimization_barrier((samples_one[0], total_two, output))
-    total_one = joined(kept_one, samples_one[1], "dp", 0)
-    grad_one, grad_two = reduce_rows(total_one, total_two)
+    kept_one, kept_two, output = lax.optimization_barrier((samples_one[0], rows_two[0], output))
+    rows_one = split_rows(joined(kept_one, samples_one[1], "dp", 0))
+    grad_two = joined(kept_two, rows_two[1], "rows", 1).T
+    grad_one = joined(*rows_one, "rows", 1).T
     return (output[None], grad_one * factor, grad_two * factor)
 
 

time: 192 us -> 187 us (0.974)
  waiting for transfers between devices: 21.5 us -> 12.1 us
  local copies, waits for them, and re-layouts: 22.7 us -> 28.7 us
    ppermute x11 -> x14, waiting for transfers between devices: 17.3 us -> 8.62 us  [joined(): total = total + lax.ppermute(piece, axis, pairs).astype(F32)]
    unnamed x24 -> x39, local copies, waits for them, and re-layouts: 1.27 us -> 3.33 us
    convert_element_type x2, local copies, waits for them, and re-layouts: 3.88 us -> 5.92 us  [split_pair(): lax.dynamic_index_in_dim(pieces, 1 - mine, 0, keepdims=False).astype(BF16)]
    add x5 -> x4, other arithmetic: 7.37 us -> 5.75 us  [joined(): total = total + lax.ppermute(piece, axis, pairs).astype(F32)]
    ppermute x11 -> x14, starting transfers between devices: 24.1 us -> 22.7 us  [joined(): total = total + lax.ppermute(piece, axis, pairs).astype(F32)]
  transfers between devices with their start and end apart: 17 -> 20, of which waited for: 4 -> 5; matrix products, arithmetic and copies ran while one was open for 7% -> 14% of each run, Pallas kernels for 32% -> 44%
where the time goes in v4:
time: 187 us
  Pallas kernels  100 us (53%)
  starting transfers between devices  37.4 us (20%)
  local copies, waits for them, and re-layouts  28.7 us (15%)
  waiting for transfers between devices  12.1 us (6%)
  other arithmetic  7.2 us (4%)
    pallas_call x6, Pallas kernels, run(): pl.pallas_call(body, out_shape=out_shape, grid=(grid,), in_specs=[whole i...  100 us
    ppermute x14, starting transfers between devices, joined(): total = total + lax.ppermute(piece, axis, pairs).astype(F32)  22.7 us
    ppermute x3, starting transfers between devices, edge_rows(): low = lax.ppermute(block[block.shape[0] - width:], 'rows', forward)  10.4 us
    ppermute x14, waiting for transfers between devices, joined(): total = total + lax.ppermute(piece, axis, pairs).astype(F32)  8.62 us
    convert_element_type x2, local copies, waits for them, and re-layouts, split_pair(): lax.dynamic_index_in_dim(pieces, 1 - mine, 0, keepdims=False).astype(BF16)  5.92 us
    add x4, other arithmetic, joined(): total = total + lax.ppermute(piece, axis, pairs).astype(F32)  5.75 us
    reshape x2, local copies, waits for them, and re-layouts, split_samples(): turned = total.reshape(-1, channels).T  4.8 us
    slice x3, local copies, waits for them, and re-layouts, edge_rows(): high = lax.ppermute(block[:width], 'rows', backward)  4.64 us
  transfers between devices with their start and end apart: 20, of which 5 were waited for; matrix products, arithmetic and copies ran while one was open for 14% of the time, Pallas kernels for 44%

profile of v4, /device:TPU:0, one launch (start us, length us, event | category | flops | bytes accessed | tf_op | source)
XLA Modules:
  0.0 186.9 jit_solution(16151999960919826227)
XLA Ops:
  0.6 1.5 slice_bitcast_fusion
  2.2 2.4 %collective-permute-start.2 = (bf16[16,64,384]{2,1,0:T(8,128)(2,1)S(1)}, bf16[16,64,384]{2,1,0:T(8,128)(2,1)S(1)}, u32[]{:S(2)}, u32[]{:S(2)}) collective-permute-start(bf16[16,64,384]{2,1,0:T(8,128)(2,1)S(1)} %get-tuple-element.18), channel_id=1, source_target_pairs={{0,1},{1,2},{2,3},{3,4},{4,5},{5,6},{6,7},{8,9},{9,10},{10,11},{11... | collective-permute-start | bytes 2359304 | tf_op jit(solution)/shard_map/ppermute | solution.py:21
  4.6 1.3 collective-permute-start.3
  5.9 1.8 slice_bitcast_fusion.2
  7.7 5.2 %collective-permute-start = (bf16[4,64,384]{2,1,0:T(8,128)(2,1)}, bf16[4,64,384]{2,1,0:T(8,128)(2,1)S(1)}, u32[]{:S(2)}, u32[]{:S(2)}) collective-permute-start(bf16[4,64,384]{2,1,0:T(8,128)(2,1)} %get-tuple-element.20), channel_id=1, source_target_pairs={{0,1},{1,2},{2,3},{3,4},{4,5},{5,6},{6,7},{8,9},{9,10},{10,11},{11... | collective-permute-start | bytes 589832 | tf_op jit(solution)/shard_map/ppermute | solution.py:21
  12.9 1.3 collective-permute-start.1
  14.2 3.4 %collective-permute-done.1.refs_2_ = bf16[4,64,384]{2,1,0:T(8,128)(2,1)S(1)} collective-permute-done((bf16[4,64,384]{2,1,0:T(8,128)(2,1)}, bf16[4,64,384]{2,1,0:T(8,128)(2,1)S(1)}, u32[]{:S(2)}, u32[]{:S(2)}) %collective-permute-start.1) | collective-permute-done | bytes 196640 | tf_op jit(solution)/shard_map/ppermute | solution.py:22
  17.6 0.7 copy-done.10
  18.3 19.3 %shard_map.67.refs_3_.refs_4_.refs_1_ = bf16[64,64,384]{2,1,0:T(8,128)(2,1)} custom-call(bf16[4,64,384]{2,1,0:T(8,128)(2,1)} %copy-done.9, bf16[64,64,384]{2,1,0:T(8,128)(2,1)} %bitcast.96, bf16[4,64,384]{2,1,0:T(8,128)(2,1)} %copy-done.10, bf16[3456,384]{1,0:T(8,128)(2,1)} %refs_3_.4), custom_call_target="tpu_custom_call" | custom-call | flops 169869312 | bytes 1024 | tf_op jit(solution)/shard_map/pallas_call | solution.py:169
  37.6 0.9 copy-done.1
  38.5 0.9 copy-done.2
  39.4 18.9 %shard_map.68 = f32[3456,384]{1,0:T(8,128)} custom-call(bf16[16,64,384]{2,1,0:T(8,128)(2,1)} %copy-done.1, bf16[64,64,384]{2,1,0:T(8,128)(2,1)} %bitcast.88, bf16[16,64,384]{2,1,0:T(8,128)(2,1)} %copy-done.2, bf16[64,64,384]{2,1,0:T(8,128)(2,1)} %shard_map.67.refs_3_.refs_4_.refs_1_), custom_call_target="tpu_custom_call" | custom-call | flops 169869312 | bytes 1024 | tf_op jit(solution)/shard_map/pallas_call | solution.py:169
  58.3 3.0 %fusion.refs_5_ = bf16[4,432,384]{2,1,0:T(8,128)(2,1)} fusion(f32[4,2,432,384]{3,2,1,0:T(8,128)} %bitcast.92, s32[]{:T(128)S(6)} %select_n.43), kind=kLoop, calls=%fused_computation.5 | loop fusion | bytes 2654212 | tf_op jit(solution)/shard_map/convert_element_type | solution.py:211
  61.2 5.0 %collective-permute-start.4 = (bf16[4,432,384]{2,1,0:T(8,128)(2,1)}, bf16[4,432,384]{2,1,0:T(8,128)(2,1)}, u32[]{:S(2)}, u32[]{:S(2)}) collective-permute-start(bf16[4,432,384]{2,1,0:T(8,128)(2,1)} %fusion.refs_5_), channel_id=1, source_target_pairs={{0,1},{1,0},{2,3},{3,2},{4,5},{5,4},{6,7},{7,6},{8,9},{9,8},{10,11... | collective-permute-start | bytes 3981320 | tf_op jit(solution)/shard_map/ppermute | solution.py:201
  66.2 1.3 fusion.18
  67.5 2.8 %collective-permute-start.5 = (bf16[16,64,384]{2,1,0:T(8,128)(2,1)}, bf16[16,64,384]{2,1,0:T(8,128)(2,1)}, u32[]{:S(2)}, u32[]{:S(2)}) collective-permute-start(bf16[16,64,384]{2,1,0:T(8,128)(2,1)} %get-tuple-element.16), channel_id=1, source_target_pairs={{0,1},{1,2},{2,3},{3,4},{4,5},{5,6},{6,7},{8,9},{9,10},{10,11},{11... | collective-permute-start | bytes 2359304 | tf_op jit(solution)/shard_map/ppermute | solution.py:21
  70.3 1.7 collective-permute-start.6
  72.1 18.7 %shard_map.69.refs_3_ = bf16[64,64,384]{2,1,0:T(8,128)(2,1)} custom-call(bf16[16,64,384]{2,1,0:T(8,128)(2,1)} %copy-done.1, bf16[64,64,384]{2,1,0:T(8,128)(2,1)} %bitcast.89, bf16[16,64,384]{2,1,0:T(8,128)(2,1)} %copy-done.2, bf16[3456,384]{1,0:T(8,128)(2,1)} %refs_3_.7, bf16[64,64,384]{2,1,0:T(8,128)(2,1)} %shard_map.67.refs_3_.refs_4_.refs_1_, ...), custom_call_target="tpu_custom_call" | custom-call | flops 169869312 | bytes 1024 | tf_op jit(solution)/shard_map/pallas_call | solution.py:169
  90.8 1.6 bitcast_add_fusion
  92.3 2.3 %copy.11 = f32[1728,384]{0,1:T(8,128)} copy(f32[1728,384]{1,0:T(8,128)S(1)} %bitcast.100) | data formatting | bytes 5308416 | tf_op jit(solution)/shard_map/reshape | solution.py:219
  94.7 2.5 %fusion.4 = (bf16[96,1728]{1,0:T(8,128)(2,1)}, bf16[96,1728]{1,0:T(8,128)(2,1)}, bf16[96,1728]{1,0:T(8,128)(2,1)}) fusion(f32[4,96,1728]{2,1,0:T(8,128)} %bitcast.101, s32[]{:T(128)S(6)} %select_n.47, s32[]{:T(128)S(6)} %select_n.46, s32[]{:T(128)S(6)} %select_n.45), kind=kLoop, calls=%fused_computation.21 | loop fusion | bytes 1990668 | tf_op jit(solution)/shard_map/convert_element_type | solution.py:190
  97.2 19.5 %shard_map.70 = f32[3456,384]{1,0:T(8,128)} custom-call(bf16[4,64,384]{2,1,0:T(8,128)(2,1)} %copy-done.9, bf16[64,64,384]{2,1,0:T(8,128)(2,1)} %bitcast.97, bf16[4,64,384]{2,1,0:T(8,128)(2,1)} %copy-done.10, bf16[64,64,384]{2,1,0:T(8,128)(2,1)} %shard_map.69.refs_3_, bf16[96,1728]{1,0:T(8,128)(2,1)} %get-tuple-element.26.refs_4_, ...), custom_call_target="tpu_custom_call" | custom-call | flops 169869312 | bytes 1024 | tf_op jit(solution)/shard_map/pallas_call | solution.py:169
  116.7 2.9 %fusion.1.refs_4_ = bf16[4,432,384]{2,1,0:T(8,128)(2,1)} fusion(f32[4,2,432,384]{3,2,1,0:T(8,128)} %bitcast.90, s32[]{:T(128)S(6)} %select_n.43), kind=kLoop, calls=%fused_computation.6 | loop fusion | bytes 2654212 | tf_op jit(solution)/shard_map/convert_element_type | solution.py:211
  119.7 1.7 collective-permute-start.7
  121.3 2.5 %collective-permute-start.10 = (bf16[96,1728]{1,0:T(8,128)(2,1)}, bf16[96,1728]{1,0:T(8,128)(2,1)S(1)}, u32[]{:S(2)}, u32[]{:S(2)}) collective-permute-start(bf16[96,1728]{1,0:T(8,128)(2,1)} %get-tuple-element.24.refs_6_), channel_id=1, source_target_pairs={{0,24},{8,16},{16,8},{24,0},{1,25},{9,17},{17,9},{25,1},{2,26},{10... | collective-permute-start | bytes 995336 | tf_op jit(solution)/shard_map/ppermute | solution.py:201
  124.8 1.9 %dynamic-slice_bitcast_fusion = f32[4,432,384]{2,1,0:T(8,128)S(1)} fusion(f32[4,2,432,384]{3,2,1,0:T(8,128)} %bitcast.91, s32[]{:T(128)S(6)} %select_n.44), kind=kLoop, calls=%fused_computation.4 | loop fusion | bytes 5308420 | tf_op jit(solution)/shard_map/jit(dynamic_index_in_dim)/squeeze | solution.py:210
  126.8 8.6 %shard_map.71.refs_4_ = bf16[64,64,384]{2,1,0:T(8,128)(2,1)} custom-call(bf16[16,64,384]{2,1,0:T(8,128)(2,1)} %collective-permute-done.5.refs_0_, bf16[64,64,384]{2,1,0:T(8,128)(2,1)} %shard_map.67.refs_3_.refs_4_.refs_1_, bf16[16,64,384]{2,1,0:T(8,128)(2,1)} %collective-permute-done.6.refs_2_, bf16[3456,384]{1,0:T(8,128)(2,1)} %refs_3_.7, ...), custom_call_target="tpu_custom_call" | custom-call | flops 42467328 | bytes 1024 | tf_op jit(solution)/shard_map/pallas_call | solution.py:169
  135.4 1.1 dynamic-slice_bitcast_fusion.2
  136.6 3.2 %collective-permute-done.9 = bf16[96,1728]{1,0:T(8,128)(2,1)S(1)} collective-permute-done((bf16[96,1728]{1,0:T(8,128)(2,1)S(1)}, bf16[96,1728]{1,0:T(8,128)(2,1)S(1)}, u32[]{:S(2)}, u32[]{:S(2)}) %collective-permute-start.9) | collective-permute-done | bytes 331808 | tf_op jit(solution)/shard_map/ppermute | solution.py:201
  139.9 1.0 convert_add_fusion.2
  140.9 2.0 %reshape.78 = f32[96,4,432]{2,1,0:T(4,128)S(1)} reshape(f32[96,1728]{1,0:T(8,128)} %convert_add_fusion.2) | data formatting | bytes 1327104 | tf_op jit(solution)/shard_map/reshape | solution.py:225
  143.1 0.7 copy.50
  144.4 2.3 %collective-permute-start.19 = (bf16[96,432]{1,0:T(8,128)(2,1)S(1)}, bf16[96,432]{1,0:T(8,128)(2,1)S(1)}, u32[]{:S(2)}, u32[]{:S(2)}) collective-permute-start(bf16[96,432]{1,0:T(8,128)(2,1)S(1)} %bitcast.110), channel_id=1, source_target_pairs={{0,6},{1,7},{2,4},{3,5},{4,2},{5,3},{6,0},{7,1},{8,14},{9,15},{10,... | collective-permute-start | bytes 248840 | tf_op jit(solution)/shard_map/ppermute | solution.py:201
  146.8 1.1 collective-permute-start.18
  147.9 1.0 collective-permute-start.17
  148.9 3.0 %convert_add_fusion = f32[4,432,384]{2,1,0:T(8,128)} fusion(f32[4,432,384]{2,1,0:T(8,128)S(1)} %dynamic-slice_bitcast_fusion, bf16[4,432,384]{2,1,0:T(8,128)(2,1)} %collective-permute-done.7), kind=kLoop, calls=%fused_computation.3 | loop fusion | flops 1327104 | bytes 6635520 | tf_op jit(solution)/shard_map/add | solution.py:201
  151.9 2.5 %copy.13 = f32[1728,384]{0,1:T(8,128)S(1)} copy(f32[1728,384]{1,0:T(8,128)} %bitcast.99) | data formatting | bytes 5308416 | tf_op jit(solution)/shard_map/reshape | solution.py:219
  154.6 1.5 collective-permute-start.13
  156.1 1.5 collective-permute-start.12
  158.2 15.5 %shard_map.72 = bf16[64,64,384]{2,1,0:T(8,128)(2,1)} custom-call(bf16[16,64,384]{2,1,0:T(8,128)(2,1)} %collective-permute-done.5.refs_0_, bf16[64,64,384]{2,1,0:T(8,128)(2,1)} %shard_map.67.refs_3_.refs_4_.refs_1_, bf16[16,64,384]{2,1,0:T(8,128)(2,1)} %collective-permute-done.6.refs_2_, bf16[3456,384]{1,0:T(8,128)(2,1)} %refs_3_.7, ...), custom_call_target="tpu_custom_call", output_to_operand_aliasing={{}: (4, {})} | custom-call | flops 127401984 | bytes 1024 | tf_op jit(solution)/shard_map/pallas_call | solution.py:169
  173.8 0.7 multiply_bitcast_fusion
  174.6 0.9 reshape.79
  175.5 0.5 constant_dynamic-slice_fusion.2
  176.1 2.3 %collective-permute-start.16 = (bf16[96,432]{1,0:T(8,128)(2,1)S(1)}, bf16[96,432]{1,0:T(8,128)(2,1)S(1)}, u32[]{:S(2)}, u32[]{:S(2)}) collective-permute-start(bf16[96,432]{1,0:T(8,128)(2,1)S(1)} %bitcast.112), channel_id=1, source_target_pairs={{0,6},{1,7},{2,4},{3,5},{4,2},{5,3},{6,0},{7,1},{8,14},{9,15},{10,... | collective-permute-start | bytes 248840 | tf_op jit(solution)/shard_map/ppermute | solution.py:201
  178.7 2.0 %collective-permute-start.14 = (bf16[96,432]{1,0:T(8,128)(2,1)S(1)}, bf16[96,432]{1,0:T(8,128)(2,1)S(1)}, u32[]{:S(2)}, u32[]{:S(2)}) collective-permute-start(bf16[96,432]{1,0:T(8,128)(2,1)S(1)} %bitcast.114), channel_id=1, source_target_pairs={{0,2},{1,3},{2,0},{3,1},{4,6},{5,7},{6,4},{7,5},{8,10},{9,11},{10,... | collective-permute-start | bytes 248840 | tf_op jit(solution)/shard_map/ppermute | solution.py:201
  180.9 2.6 %collective-permute-done.16 = bf16[96,432]{1,0:T(8,128)(2,1)S(1)} collective-permute-done((bf16[96,432]{1,0:T(8,128)(2,1)S(1)}, bf16[96,432]{1,0:T(8,128)(2,1)S(1)}, u32[]{:S(2)}, u32[]{:S(2)}) %collective-permute-start.16) | collective-permute-done | bytes 82976 | tf_op jit(solution)/shard_map/ppermute | solution.py:201
  183.5 2.7 %collective-permute-done.15 = bf16[96,432]{1,0:T(8,128)(2,1)S(1)} collective-permute-done((bf16[96,432]{1,0:T(8,128)(2,1)S(1)}, bf16[96,432]{1,0:T(8,128)(2,1)S(1)}, u32[]{:S(2)}, u32[]{:S(2)}) %collective-permute-start.15) | collective-permute-done | bytes 82976 | tf_op jit(solution)/shard_map/ppermute | solution.py:201
  186.1 0.7 fusion.11
  (62 shorter events, 3.3 us)
Async XLA Ops:
  2.2 35.4 %collective-permute-start.2 = (bf16[16,64,384]{2,1,0:T(8,128)(2,1)S(1)}, bf16[16,64,384]{2,1,0:T(8,128)(2,1)S(1)}, u32[]{:S(2)}, u32[]{:S(2)}) collective-permute-start(bf16[16,64,384]{2,1,0:T(8,128)(2,1)S(1)} %get-tuple-element.18), channel_id=1, source_target_pairs={{0,1},{1,2},{2,3},{3,4},{4,5},{5,6},{6,7},{8,9},{9,10},{10,11},{11... | collective-permute-start | bytes 2359304 | tf_op jit(solution)/shard_map/ppermute | solution.py:21
  4.6 33.0 %collective-permute-start.3 = (bf16[16,64,384]{2,1,0:T(8,128)(2,1)S(1)}, bf16[16,64,384]{2,1,0:T(8,128)(2,1)S(1)}, u32[]{:S(2)}, u32[]{:S(2)}) collective-permute-start(bf16[16,64,384]{2,1,0:T(8,128)(2,1)S(1)} %get-tuple-element.17), channel_id=1, source_target_pairs={{1,0},{2,1},{3,2},{4,3},{5,4},{6,5},{7,6},{9,8},{10,9},{11,10},{12... | collective-permute-start | bytes 2359304 | tf_op jit(solution)/shard_map/ppermute | solution.py:22
  7.7 6.5 %collective-permute-start = (bf16[4,64,384]{2,1,0:T(8,128)(2,1)}, bf16[4,64,384]{2,1,0:T(8,128)(2,1)S(1)}, u32[]{:S(2)}, u32[]{:S(2)}) collective-permute-start(bf16[4,64,384]{2,1,0:T(8,128)(2,1)} %get-tuple-element.20), channel_id=1, source_target_pairs={{0,1},{1,2},{2,3},{3,4},{4,5},{5,6},{6,7},{8,9},{9,10},{10,11},{11... | collective-permute-start | bytes 589832 | tf_op jit(solution)/shard_map/ppermute | solution.py:21
  12.9 4.8 %collective-permute-start.1 = (bf16[4,64,384]{2,1,0:T(8,128)(2,1)}, bf16[4,64,384]{2,1,0:T(8,128)(2,1)S(1)}, u32[]{:S(2)}, u32[]{:S(2)}) collective-permute-start(bf16[4,64,384]{2,1,0:T(8,128)(2,1)} %get-tuple-element.19), channel_id=1, source_target_pairs={{1,0},{2,1},{3,2},{4,3},{5,4},{6,5},{7,6},{9,8},{10,9},{11,10},{12... | collective-permute-start | bytes 589832 | tf_op jit(solution)/shard_map/ppermute | solution.py:22
  14.2 3.5 %copy-start.9 = (bf16[4,64,384]{2,1,0:T(8,128)(2,1)}, bf16[4,64,384]{2,1,0:T(8,128)(2,1)S(1)}, u32[]{:S(2)}) copy-start(bf16[4,64,384]{2,1,0:T(8,128)(2,1)S(1)} %collective-permute-done.refs_0_) | copy-start | bytes 589828
  17.6 0.7 copy-start.10
  37.6 0.9 copy-start.1
  38.5 0.9 copy-start.2
  39.4 26.8 %copy-start = (bf16[64,64,384]{2,1,0:T(8,128)(2,1)S(1)}, bf16[64,64,384]{2,1,0:T(8,128)(2,1)}, u32[]{:S(2)}) copy-start(bf16[64,64,384]{2,1,0:T(8,128)(2,1)} %shard_map.67.refs_3_.refs_4_.refs_1_) | copy-start | bytes 9437188
  61.2 29.5 %collective-permute-start.4 = (bf16[4,432,384]{2,1,0:T(8,128)(2,1)}, bf16[4,432,384]{2,1,0:T(8,128)(2,1)}, u32[]{:S(2)}, u32[]{:S(2)}) collective-permute-start(bf16[4,432,384]{2,1,0:T(8,128)(2,1)} %fusion.refs_5_), channel_id=1, source_target_pairs={{0,1},{1,0},{2,3},{3,2},{4,5},{5,4},{6,7},{7,6},{8,9},{9,8},{10,11... | collective-permute-start | bytes 3981320 | tf_op jit(solution)/shard_map/ppermute | solution.py:201
  67.5 56.8 %collective-permute-start.5 = (bf16[16,64,384]{2,1,0:T(8,128)(2,1)}, bf16[16,64,384]{2,1,0:T(8,128)(2,1)}, u32[]{:S(2)}, u32[]{:S(2)}) collective-permute-start(bf16[16,64,384]{2,1,0:T(8,128)(2,1)} %get-tuple-element.16), channel_id=1, source_target_pairs={{0,1},{1,2},{2,3},{3,4},{4,5},{5,6},{6,7},{8,9},{9,10},{10,11},{11... | collective-permute-start | bytes 2359304 | tf_op jit(solution)/shard_map/ppermute | solution.py:21
  70.3 20.4 %slice-start = ((s8[5308416]{0:T(1024)(128)(4,1)}), s8[4194304]{0:T(1024)(128)(4,1)S(1)}, s32[]{:S(2)}) async-start(s8[5308416]{0:T(1024)(128)(4,1)} %bitcast.93), calls=%async_computation | async-start | bytes 8388608
  70.3 20.4 %slice-start.1 = ((s8[5308416]{0:T(1024)(128)(4,1)}), s8[1114112]{0:T(1024)(128)(4,1)S(1)}, s32[]{:S(2)}) async-start(s8[5308416]{0:T(1024)(128)(4,1)} %bitcast.93), calls=%async_computation.1 | async-start | bytes 2228224
  70.3 56.4 %collective-permute-start.6 = (bf16[16,64,384]{2,1,0:T(8,128)(2,1)}, bf16[16,64,384]{2,1,0:T(8,128)(2,1)}, u32[]{:S(2)}, u32[]{:S(2)}) collective-permute-start(bf16[16,64,384]{2,1,0:T(8,128)(2,1)} %get-tuple-element.15), channel_id=1, source_target_pairs={{1,0},{2,1},{3,2},{4,3},{5,4},{6,5},{7,6},{9,8},{10,9},{11,10},{12... | collective-permute-start | bytes 2359304 | tf_op jit(solution)/shard_map/ppermute | solution.py:22
  97.2 26.6 %copy-start.4 = (bf16[96,1728]{1,0:T(8,128)(2,1)S(1)}, bf16[96,1728]{1,0:T(8,128)(2,1)}, u32[]{:S(2)}) copy-start(bf16[96,1728]{1,0:T(8,128)(2,1)} %get-tuple-element.25.refs_5_) | copy-start | bytes 995332
  97.2 27.1 %copy-start.3 = (bf16[96,1728]{1,0:T(8,128)(2,1)S(1)}, bf16[96,1728]{1,0:T(8,128)(2,1)}, u32[]{:S(2)}) copy-start(bf16[96,1728]{1,0:T(8,128)(2,1)} %get-tuple-element.26.refs_4_) | copy-start | bytes 995332
  119.7 29.2 %collective-permute-start.7 = (bf16[4,432,384]{2,1,0:T(8,128)(2,1)}, bf16[4,432,384]{2,1,0:T(8,128)(2,1)}, u32[]{:S(2)}, u32[]{:S(2)}) collective-permute-start(bf16[4,432,384]{2,1,0:T(8,128)(2,1)} %fusion.1.refs_4_), channel_id=1, source_target_pairs={{0,1},{1,0},{2,3},{3,2},{4,5},{5,4},{6,7},{7,6},{8,9},{9,8},{10,11... | collective-permute-start | bytes 3981320 | tf_op jit(solution)/shard_map/ppermute | solution.py:201
  121.3 15.2 %collective-permute-start.10 = (bf16[96,1728]{1,0:T(8,128)(2,1)}, bf16[96,1728]{1,0:T(8,128)(2,1)S(1)}, u32[]{:S(2)}, u32[]{:S(2)}) collective-permute-start(bf16[96,1728]{1,0:T(8,128)(2,1)} %get-tuple-element.24.refs_6_), channel_id=1, source_target_pairs={{0,24},{8,16},{16,8},{24,0},{1,25},{9,17},{17,9},{25,1},{2,26},{10... | collective-permute-start | bytes 995336 | tf_op jit(solution)/shard_map/ppermute | solution.py:201
  123.8 16.0 %collective-permute-start.9 = (bf16[96,1728]{1,0:T(8,128)(2,1)S(1)}, bf16[96,1728]{1,0:T(8,128)(2,1)S(1)}, u32[]{:S(2)}, u32[]{:S(2)}) collective-permute-start(bf16[96,1728]{1,0:T(8,128)(2,1)S(1)} %copy-done.4), channel_id=1, source_target_pairs={{0,16},{8,24},{16,0},{24,8},{1,17},{9,25},{17,1},{25,9},{2,18},{10... | collective-permute-start | bytes 995336 | tf_op jit(solution)/shard_map/ppermute | solution.py:201
  124.3 15.6 %collective-permute-start.8 = (bf16[96,1728]{1,0:T(8,128)(2,1)S(1)}, bf16[96,1728]{1,0:T(8,128)(2,1)S(1)}, u32[]{:S(2)}, u32[]{:S(2)}) collective-permute-start(bf16[96,1728]{1,0:T(8,128)(2,1)S(1)} %copy-done.3), channel_id=1, source_target_pairs={{0,8},{8,0},{16,24},{24,16},{1,9},{9,1},{17,25},{25,17},{2,10},{10... | collective-permute-start | bytes 995336 | tf_op jit(solution)/shard_map/ppermute | solution.py:201
  144.4 7.6 %copy-start.11 = (bf16[96,1,432]{2,0,1:T(8,128)(2,1)}, bf16[96,1,432]{2,0,1:T(8,128)(2,1)S(1)}, u32[]{:S(2)}) copy-start(bf16[96,1,432]{2,0,1:T(8,128)(2,1)S(1)} %copy.51) | copy-start | bytes 248836
  144.4 7.5 %copy-start.12 = (bf16[96,1,432]{2,0,1:T(8,128)(2,1)}, bf16[96,1,432]{2,0,1:T(8,128)(2,1)S(1)}, u32[]{:S(2)}) copy-start(bf16[96,1,432]{2,0,1:T(8,128)(2,1)S(1)} %copy.52) | copy-start | bytes 248836
  144.4 7.5 %copy-start.13 = (bf16[96,1,432]{2,0,1:T(8,128)(2,1)}, bf16[96,1,432]{2,0,1:T(8,128)(2,1)S(1)}, u32[]{:S(2)}) copy-start(bf16[96,1,432]{2,0,1:T(8,128)(2,1)S(1)} %copy.53) | copy-start | bytes 248836
  144.4 13.1 %collective-permute-start.19 = (bf16[96,432]{1,0:T(8,128)(2,1)S(1)}, bf16[96,432]{1,0:T(8,128)(2,1)S(1)}, u32[]{:S(2)}, u32[]{:S(2)}) collective-permute-start(bf16[96,432]{1,0:T(8,128)(2,1)S(1)} %bitcast.110), channel_id=1, source_target_pairs={{0,6},{1,7},{2,4},{3,5},{4,2},{5,3},{6,0},{7,1},{8,14},{9,15},{10,... | collective-permute-start | bytes 248840 | tf_op jit(solution)/shard_map/ppermute | solution.py:201
  146.8 27.0 %collective-permute-start.18 = (bf16[96,432]{1,0:T(8,128)(2,1)S(1)}, bf16[96,432]{1,0:T(8,128)(2,1)S(1)}, u32[]{:S(2)}, u32[]{:S(2)}) collective-permute-start(bf16[96,432]{1,0:T(8,128)(2,1)S(1)} %bitcast.108), channel_id=1, source_target_pairs={{0,4},{1,5},{2,6},{3,7},{4,0},{5,1},{6,2},{7,3},{8,12},{9,13},{10,... | collective-permute-start | bytes 248840 | tf_op jit(solution)/shard_map/ppermute | solution.py:201
  147.9 25.8 %collective-permute-start.17 = (bf16[96,432]{1,0:T(8,128)(2,1)S(1)}, bf16[96,432]{1,0:T(8,128)(2,1)S(1)}, u32[]{:S(2)}, u32[]{:S(2)}) collective-permute-start(bf16[96,432]{1,0:T(8,128)(2,1)S(1)} %bitcast.106), channel_id=1, source_target_pairs={{0,2},{1,3},{2,0},{3,1},{4,6},{5,7},{6,4},{7,5},{8,10},{9,11},{10,... | collective-permute-start | bytes 248840 | tf_op jit(solution)/shard_map/ppermute | solution.py:201
  154.5 3.6 %copy-start.5 = (bf16[96,1728]{1,0:T(8,128)(2,1)}, bf16[96,1728]{1,0:T(8,128)(2,1)S(1)}, u32[]{:S(2)}) copy-start(bf16[96,1728]{1,0:T(8,128)(2,1)S(1)} %get-tuple-element.23.refs_5_) | copy-start | bytes 995332
  154.5 3.6 %copy-start.6 = (bf16[96,1728]{1,0:T(8,128)(2,1)}, bf16[96,1728]{1,0:T(8,128)(2,1)S(1)}, u32[]{:S(2)}) copy-start(bf16[96,1728]{1,0:T(8,128)(2,1)S(1)} %get-tuple-element.22.refs_6_) | copy-start | bytes 995332
  154.5 3.6 %copy-start.7 = (bf16[96,1728]{1,0:T(8,128)(2,1)}, bf16[96,1728]{1,0:T(8,128)(2,1)S(1)}, u32[]{:S(2)}) copy-start(bf16[96,1728]{1,0:T(8,128)(2,1)S(1)} %get-tuple-element.21.refs_7_) | copy-start | bytes 995332
  154.6 19.9 %collective-permute-start.13 = (bf16[96,1728]{1,0:T(8,128)(2,1)S(1)}, bf16[96,1728]{1,0:T(8,128)(2,1)S(1)}, u32[]{:S(2)}, u32[]{:S(2)}) collective-permute-start(bf16[96,1728]{1,0:T(8,128)(2,1)S(1)} %get-tuple-element.21.refs_7_), channel_id=1, source_target_pairs={{0,24},{8,16},{16,8},{24,0},{1,25},{9,17},{17,9},{25,1},{2,26},{10... | collective-permute-start | bytes 995336 | tf_op jit(solution)/shard_map/ppermute | solution.py:201
  156.1 18.4 %collective-permute-start.12 = (bf16[96,1728]{1,0:T(8,128)(2,1)S(1)}, bf16[96,1728]{1,0:T(8,128)(2,1)S(1)}, u32[]{:S(2)}, u32[]{:S(2)}) collective-permute-start(bf16[96,1728]{1,0:T(8,128)(2,1)S(1)} %get-tuple-element.22.refs_6_), channel_id=1, source_target_pairs={{0,16},{8,24},{16,0},{24,8},{1,17},{9,25},{17,1},{25,9},{2,18},{10... | collective-permute-start | bytes 995336 | tf_op jit(solution)/shard_map/ppermute | solution.py:201
  157.6 16.9 %collective-permute-start.11 = (bf16[96,1728]{1,0:T(8,128)(2,1)S(1)}, bf16[96,1728]{1,0:T(8,128)(2,1)S(1)}, u32[]{:S(2)}, u32[]{:S(2)}) collective-permute-start(bf16[96,1728]{1,0:T(8,128)(2,1)S(1)} %get-tuple-element.23.refs_5_), channel_id=1, source_target_pairs={{0,8},{8,0},{16,24},{24,16},{1,9},{9,1},{17,25},{25,17},{2,10},{10... | collective-permute-start | bytes 995336 | tf_op jit(solution)/shard_map/ppermute | solution.py:201
  158.2 15.5 %copy-start.8 = (f32[96,1,432]{2,0,1:T(8,128)S(1)}, f32[96,1,432]{2,0,1:T(8,128)}, u32[]{:S(2)}) copy-start(f32[96,1,432]{2,0,1:T(8,128)} %copy.50) | copy-start | bytes 497668
  176.1 7.4 %collective-permute-start.16 = (bf16[96,432]{1,0:T(8,128)(2,1)S(1)}, bf16[96,432]{1,0:T(8,128)(2,1)S(1)}, u32[]{:S(2)}, u32[]{:S(2)}) collective-permute-start(bf16[96,432]{1,0:T(8,128)(2,1)S(1)} %bitcast.112), channel_id=1, source_target_pairs={{0,6},{1,7},{2,4},{3,5},{4,2},{5,3},{6,0},{7,1},{8,14},{9,15},{10,... | collective-permute-start | bytes 248840 | tf_op jit(solution)/shard_map/ppermute | solution.py:201
  178.4 7.7 %collective-permute-start.15 = (bf16[96,432]{1,0:T(8,128)(2,1)S(1)}, bf16[96,432]{1,0:T(8,128)(2,1)S(1)}, u32[]{:S(2)}, u32[]{:S(2)}) collective-permute-start(bf16[96,432]{1,0:T(8,128)(2,1)S(1)} %bitcast.113), channel_id=1, source_target_pairs={{0,4},{1,5},{2,6},{3,7},{4,0},{5,1},{6,2},{7,3},{8,12},{9,13},{10,... | collective-permute-start | bytes 248840 | tf_op jit(solution)/shard_map/ppermute | solution.py:201
  178.7 7.4 %collective-permute-start.14 = (bf16[96,432]{1,0:T(8,128)(2,1)S(1)}, bf16[96,432]{1,0:T(8,128)(2,1)S(1)}, u32[]{:S(2)}, u32[]{:S(2)}) collective-permute-start(bf16[96,432]{1,0:T(8,128)(2,1)S(1)} %bitcast.114), channel_id=1, source_target_pairs={{0,2},{1,3},{2,0},{3,1},{4,6},{5,7},{6,4},{7,5},{8,10},{9,11},{10,... | collective-permute-start | bytes 248840 | tf_op jit(solution)/shard_map/ppermute | solution.py:201

commit v5 on v4

--- a/solution.py
+++ b/solution.py
@@ -233,7 +233,7 @@
     spacing = 2 * group
     factor = 1.0 / math.sqrt(lax.axis_size("dp") * rows * group * cols)
     flops = 2 * rows * cols * weight_one.shape[0] * channels
-    tile = 8
+    tile = 16
     steps = rows // tile
     map_shape = jax.ShapeDtypeStruct((rows, cols, channels), BF16)
     map_spec = pl.BlockSpec((tile, cols, channels), lambda i: (i, 0, 0))

time: 187 us -> 185 us (0.989)
  Pallas kernels: 100 us -> 96.3 us
    pallas_call x6, Pallas kernels: 100 us -> 96.3 us  [run(): pl.pallas_call(body, out_shape=out_shape, grid=(grid,), in_specs=[whole i...]
  transfers between devices with their start and end apart: 20 -> 20, of which waited for: 5 -> 5; matrix products, arithmetic and copies ran while one was open for 14% -> 14% of each run, Pallas kernels for 44% -> 42%
where the time goes in v5:
time: 185 us; the launch traced here: 184 us
  Pallas kernels  96.3 us (52%)
  starting transfers between devices  37.4 us (20%)
  local copies, waits for them, and re-layouts  28.5 us (15%)
  waiting for transfers between devices  13.5 us (7%)
  other arithmetic  7.2 us (4%)
    pallas_call x6, Pallas kernels, run(): pl.pallas_call(body, out_shape=out_shape, grid=(grid,), in_specs=[whole i...  96.3 us
    ppermute x14, starting transfers between devices, joined(): total = total + lax.ppermute(piece, axis, pairs).astype(F32)  22.7 us
    ppermute x3, starting transfers between devices, edge_rows(): low = lax.ppermute(block[block.shape[0] - width:], 'rows', forward)  10.4 us
    ppermute x14, waiting for transfers between devices, joined(): total = total + lax.ppermute(piece, axis, pairs).astype(F32)  10.1 us
    convert_element_type x2, local copies, waits for them, and re-layouts, split_pair(): lax.dynamic_index_in_dim(pieces, 1 - mine, 0, keepdims=False).astype(BF16)  5.92 us
    add x4, other arithmetic, joined(): total = total + lax.ppermute(piece, axis, pairs).astype(F32)  5.75 us
    slice x3, local copies, waits for them, and re-layouts, edge_rows(): high = lax.ppermute(block[:width], 'rows', backward)  4.64 us
    reshape x2, local copies, waits for them, and re-layouts, split_samples(): turned = total.reshape(-1, channels).T  4.58 us
  transfers between devices with their start and end apart: 20, of which 5 were waited for; matrix products, arithmetic and copies ran while one was open for 14% of the time, Pallas kernels for 42%

profile of v5, /device:TPU:0, one launch (start us, length us, event | category | flops | bytes accessed | tf_op | source)
XLA Modules:
  0.0 183.9 jit_solution(7235150132587644406)
XLA Ops:
  0.6 1.5 slice_bitcast_fusion
  2.2 2.4 %collective-permute-start.2 = (bf16[16,64,384]{2,1,0:T(8,128)(2,1)S(1)}, bf16[16,64,384]{2,1,0:T(8,128)(2,1)S(1)}, u32[]{:S(2)}, u32[]{:S(2)}) collective-permute-start(bf16[16,64,384]{2,1,0:T(8,128)(2,1)S(1)} %get-tuple-element.18), channel_id=1, source_target_pairs={{0,1},{1,2},{2,3},{3,4},{4,5},{5,6},{6,7},{8,9},{9,10},{10,11},{11... | collective-permute-start | bytes 2359304 | tf_op jit(solution)/shard_map/ppermute | solution.py:21
  4.6 1.3 collective-permute-start.3
  5.9 1.8 slice_bitcast_fusion.2
  7.7 5.2 %collective-permute-start = (bf16[4,64,384]{2,1,0:T(8,128)(2,1)}, bf16[4,64,384]{2,1,0:T(8,128)(2,1)S(1)}, u32[]{:S(2)}, u32[]{:S(2)}) collective-permute-start(bf16[4,64,384]{2,1,0:T(8,128)(2,1)} %get-tuple-element.20), channel_id=1, source_target_pairs={{0,1},{1,2},{2,3},{3,4},{4,5},{5,6},{6,7},{8,9},{9,10},{10,11},{11... | collective-permute-start | bytes 589832 | tf_op jit(solution)/shard_map/ppermute | solution.py:21
  12.9 1.3 collective-permute-start.1
  14.2 3.4 %collective-permute-done.1.refs_2_ = bf16[4,64,384]{2,1,0:T(8,128)(2,1)S(1)} collective-permute-done((bf16[4,64,384]{2,1,0:T(8,128)(2,1)}, bf16[4,64,384]{2,1,0:T(8,128)(2,1)S(1)}, u32[]{:S(2)}, u32[]{:S(2)}) %collective-permute-start.1) | collective-permute-done | bytes 196640 | tf_op jit(solution)/shard_map/ppermute | solution.py:22
  17.6 0.7 copy-done.10
  18.3 18.2 %shard_map.67.refs_3_.refs_4_.refs_1_ = bf16[64,64,384]{2,1,0:T(8,128)(2,1)} custom-call(bf16[4,64,384]{2,1,0:T(8,128)(2,1)} %copy-done.9, bf16[64,64,384]{2,1,0:T(8,128)(2,1)} %bitcast.96, bf16[4,64,384]{2,1,0:T(8,128)(2,1)} %copy-done.10, bf16[3456,384]{1,0:T(8,128)(2,1)} %refs_3_.4), custom_call_target="tpu_custom_call" | custom-call | flops 169869312 | bytes 1024 | tf_op jit(solution)/shard_map/pallas_call | solution.py:169
  36.6 0.9 copy-done.1
  37.4 0.9 copy-done.2
  38.4 18.9 %shard_map.68 = f32[3456,384]{1,0:T(8,128)} custom-call(bf16[16,64,384]{2,1,0:T(8,128)(2,1)} %copy-done.1, bf16[64,64,384]{2,1,0:T(8,128)(2,1)} %bitcast.88, bf16[16,64,384]{2,1,0:T(8,128)(2,1)} %copy-done.2, bf16[64,64,384]{2,1,0:T(8,128)(2,1)} %shard_map.67.refs_3_.refs_4_.refs_1_), custom_call_target="tpu_custom_call" | custom-call | flops 169869312 | bytes 1024 | tf_op jit(solution)/shard_map/pallas_call | solution.py:169
  57.2 3.0 %fusion.refs_5_ = bf16[4,432,384]{2,1,0:T(8,128)(2,1)} fusion(f32[4,2,432,384]{3,2,1,0:T(8,128)} %bitcast.92, s32[]{:T(128)S(6)} %select_n.43), kind=kLoop, calls=%fused_computation.5 | loop fusion | bytes 2654212 | tf_op jit(solution)/shard_map/convert_element_type | solution.py:211
  60.2 5.0 %collective-permute-start.4 = (bf16[4,432,384]{2,1,0:T(8,128)(2,1)}, bf16[4,432,384]{2,1,0:T(8,128)(2,1)}, u32[]{:S(2)}, u32[]{:S(2)}) collective-permute-start(bf16[4,432,384]{2,1,0:T(8,128)(2,1)} %fusion.refs_5_), channel_id=1, source_target_pairs={{0,1},{1,0},{2,3},{3,2},{4,5},{5,4},{6,7},{7,6},{8,9},{9,8},{10,11... | collective-permute-start | bytes 3981320 | tf_op jit(solution)/shard_map/ppermute | solution.py:201
  65.2 1.3 fusion.18
  66.5 2.8 %collective-permute-start.5 = (bf16[16,64,384]{2,1,0:T(8,128)(2,1)}, bf16[16,64,384]{2,1,0:T(8,128)(2,1)}, u32[]{:S(2)}, u32[]{:S(2)}) collective-permute-start(bf16[16,64,384]{2,1,0:T(8,128)(2,1)} %get-tuple-element.16), channel_id=1, source_target_pairs={{0,1},{1,2},{2,3},{3,4},{4,5},{5,6},{6,7},{8,9},{9,10},{10,11},{11... | collective-permute-start | bytes 2359304 | tf_op jit(solution)/shard_map/ppermute | solution.py:21
  69.3 1.7 collective-permute-start.6
  71.0 17.7 %shard_map.69.refs_3_ = bf16[64,64,384]{2,1,0:T(8,128)(2,1)} custom-call(bf16[16,64,384]{2,1,0:T(8,128)(2,1)} %copy-done.1, bf16[64,64,384]{2,1,0:T(8,128)(2,1)} %bitcast.89, bf16[16,64,384]{2,1,0:T(8,128)(2,1)} %copy-done.2, bf16[3456,384]{1,0:T(8,128)(2,1)} %refs_3_.7, bf16[64,64,384]{2,1,0:T(8,128)(2,1)} %shard_map.67.refs_3_.refs_4_.refs_1_, ...), custom_call_target="tpu_custom_call" | custom-call | flops 169869312 | bytes 1024 | tf_op jit(solution)/shard_map/pallas_call | solution.py:169
  88.8 1.6 bitcast_add_fusion
  90.3 2.3 %copy.11 = f32[1728,384]{0,1:T(8,128)} copy(f32[1728,384]{1,0:T(8,128)S(1)} %bitcast.100) | data formatting | bytes 5308416 | tf_op jit(solution)/shard_map/reshape | solution.py:219
  92.7 2.5 %fusion.4 = (bf16[96,1728]{1,0:T(8,128)(2,1)}, bf16[96,1728]{1,0:T(8,128)(2,1)}, bf16[96,1728]{1,0:T(8,128)(2,1)}) fusion(f32[4,96,1728]{2,1,0:T(8,128)} %bitcast.101, s32[]{:T(128)S(6)} %select_n.47, s32[]{:T(128)S(6)} %select_n.46, s32[]{:T(128)S(6)} %select_n.45), kind=kLoop, calls=%fused_computation.21 | loop fusion | bytes 1990668 | tf_op jit(solution)/shard_map/convert_element_type | solution.py:190
  95.2 19.5 %shard_map.70 = f32[3456,384]{1,0:T(8,128)} custom-call(bf16[4,64,384]{2,1,0:T(8,128)(2,1)} %copy-done.9, bf16[64,64,384]{2,1,0:T(8,128)(2,1)} %bitcast.97, bf16[4,64,384]{2,1,0:T(8,128)(2,1)} %copy-done.10, bf16[64,64,384]{2,1,0:T(8,128)(2,1)} %shard_map.69.refs_3_, bf16[96,1728]{1,0:T(8,128)(2,1)} %get-tuple-element.26.refs_4_, ...), custom_call_target="tpu_custom_call" | custom-call | flops 169869312 | bytes 1024 | tf_op jit(solution)/shard_map/pallas_call | solution.py:169
  114.8 2.9 %fusion.1.refs_4_ = bf16[4,432,384]{2,1,0:T(8,128)(2,1)} fusion(f32[4,2,432,384]{3,2,1,0:T(8,128)} %bitcast.90, s32[]{:T(128)S(6)} %select_n.43), kind=kLoop, calls=%fused_computation.6 | loop fusion | bytes 2654212 | tf_op jit(solution)/shard_map/convert_element_type | solution.py:211
  117.7 1.7 collective-permute-start.7
  119.4 2.5 %collective-permute-start.10 = (bf16[96,1728]{1,0:T(8,128)(2,1)}, bf16[96,1728]{1,0:T(8,128)(2,1)S(1)}, u32[]{:S(2)}, u32[]{:S(2)}) collective-permute-start(bf16[96,1728]{1,0:T(8,128)(2,1)} %get-tuple-element.24.refs_6_), channel_id=1, source_target_pairs={{0,24},{8,16},{16,8},{24,0},{1,25},{9,17},{17,9},{25,1},{2,26},{10... | collective-permute-start | bytes 995336 | tf_op jit(solution)/shard_map/ppermute | solution.py:201
  122.9 1.9 %dynamic-slice_bitcast_fusion = f32[4,432,384]{2,1,0:T(8,128)S(1)} fusion(f32[4,2,432,384]{3,2,1,0:T(8,128)} %bitcast.91, s32[]{:T(128)S(6)} %select_n.44), kind=kLoop, calls=%fused_computation.4 | loop fusion | bytes 5308420 | tf_op jit(solution)/shard_map/jit(dynamic_index_in_dim)/squeeze | solution.py:210
  124.8 7.2 %shard_map.71.refs_4_ = bf16[64,64,384]{2,1,0:T(8,128)(2,1)} custom-call(bf16[16,64,384]{2,1,0:T(8,128)(2,1)} %collective-permute-done.5.refs_0_, bf16[64,64,384]{2,1,0:T(8,128)(2,1)} %shard_map.67.refs_3_.refs_4_.refs_1_, bf16[16,64,384]{2,1,0:T(8,128)(2,1)} %collective-permute-done.6.refs_2_, bf16[3456,384]{1,0:T(8,128)(2,1)} %refs_3_.7, ...), custom_call_target="tpu_custom_call" | custom-call | flops 42467328 | bytes 1024 | tf_op jit(solution)/shard_map/pallas_call | solution.py:169
  132.0 1.1 dynamic-slice_bitcast_fusion.2
  133.2 4.6 %collective-permute-done.9 = bf16[96,1728]{1,0:T(8,128)(2,1)S(1)} collective-permute-done((bf16[96,1728]{1,0:T(8,128)(2,1)S(1)}, bf16[96,1728]{1,0:T(8,128)(2,1)S(1)}, u32[]{:S(2)}, u32[]{:S(2)}) %collective-permute-start.9) | collective-permute-done | bytes 331808 | tf_op jit(solution)/shard_map/ppermute | solution.py:201
  137.9 1.0 convert_add_fusion.2
  139.0 2.0 %reshape.78 = f32[96,4,432]{2,1,0:T(4,128)S(1)} reshape(f32[96,1728]{1,0:T(8,128)} %convert_add_fusion.2) | data formatting | bytes 1327104 | tf_op jit(solution)/shard_map/reshape | solution.py:225
  141.1 0.7 copy.50
  142.5 2.3 %collective-permute-start.19 = (bf16[96,432]{1,0:T(8,128)(2,1)S(1)}, bf16[96,432]{1,0:T(8,128)(2,1)S(1)}, u32[]{:S(2)}, u32[]{:S(2)}) collective-permute-start(bf16[96,432]{1,0:T(8,128)(2,1)S(1)} %bitcast.110), channel_id=1, source_target_pairs={{0,6},{1,7},{2,4},{3,5},{4,2},{5,3},{6,0},{7,1},{8,14},{9,15},{10,... | collective-permute-start | bytes 248840 | tf_op jit(solution)/shard_map/ppermute | solution.py:201
  144.8 1.1 collective-permute-start.18
  145.9 1.0 collective-permute-start.17
  146.9 3.0 %convert_add_fusion = f32[4,432,384]{2,1,0:T(8,128)} fusion(f32[4,432,384]{2,1,0:T(8,128)S(1)} %dynamic-slice_bitcast_fusion, bf16[4,432,384]{2,1,0:T(8,128)(2,1)} %collective-permute-done.7), kind=kLoop, calls=%fused_computation.3 | loop fusion | flops 1327104 | bytes 6635520 | tf_op jit(solution)/shard_map/add | solution.py:201
  150.0 2.2 %copy.13 = f32[1728,384]{0,1:T(8,128)S(1)} copy(f32[1728,384]{1,0:T(8,128)} %bitcast.99) | data formatting | bytes 5308416 | tf_op jit(solution)/shard_map/reshape | solution.py:219
  152.4 1.5 collective-permute-start.13
  153.9 1.5 collective-permute-start.12
  156.0 14.8 %shard_map.72 = bf16[64,64,384]{2,1,0:T(8,128)(2,1)} custom-call(bf16[16,64,384]{2,1,0:T(8,128)(2,1)} %collective-permute-done.5.refs_0_, bf16[64,64,384]{2,1,0:T(8,128)(2,1)} %shard_map.67.refs_3_.refs_4_.refs_1_, bf16[16,64,384]{2,1,0:T(8,128)(2,1)} %collective-permute-done.6.refs_2_, bf16[3456,384]{1,0:T(8,128)(2,1)} %refs_3_.7, ...), custom_call_target="tpu_custom_call", output_to_operand_aliasing={{}: (4, {})} | custom-call | flops 127401984 | bytes 1024 | tf_op jit(solution)/shard_map/pallas_call | solution.py:169
  170.8 0.7 multiply_bitcast_fusion
  171.7 0.9 reshape.79
  172.5 0.5 constant_dynamic-slice_fusion.2
  173.1 2.3 %collective-permute-start.16 = (bf16[96,432]{1,0:T(8,128)(2,1)S(1)}, bf16[96,432]{1,0:T(8,128)(2,1)S(1)}, u32[]{:S(2)}, u32[]{:S(2)}) collective-permute-start(bf16[96,432]{1,0:T(8,128)(2,1)S(1)} %bitcast.112), channel_id=1, source_target_pairs={{0,6},{1,7},{2,4},{3,5},{4,2},{5,3},{6,0},{7,1},{8,14},{9,15},{10,... | collective-permute-start | bytes 248840 | tf_op jit(solution)/shard_map/ppermute | solution.py:201
  175.8 2.0 %collective-permute-start.14 = (bf16[96,432]{1,0:T(8,128)(2,1)S(1)}, bf16[96,432]{1,0:T(8,128)(2,1)S(1)}, u32[]{:S(2)}, u32[]{:S(2)}) collective-permute-start(bf16[96,432]{1,0:T(8,128)(2,1)S(1)} %bitcast.114), channel_id=1, source_target_pairs={{0,2},{1,3},{2,0},{3,1},{4,6},{5,7},{6,4},{7,5},{8,10},{9,11},{10,... | collective-permute-start | bytes 248840 | tf_op jit(solution)/shard_map/ppermute | solution.py:201
  177.9 2.6 %collective-permute-done.16 = bf16[96,432]{1,0:T(8,128)(2,1)S(1)} collective-permute-done((bf16[96,432]{1,0:T(8,128)(2,1)S(1)}, bf16[96,432]{1,0:T(8,128)(2,1)S(1)}, u32[]{:S(2)}, u32[]{:S(2)}) %collective-permute-start.16) | collective-permute-done | bytes 82976 | tf_op jit(solution)/shard_map/ppermute | solution.py:201
  180.5 2.7 %collective-permute-done.15 = bf16[96,432]{1,0:T(8,128)(2,1)S(1)} collective-permute-done((bf16[96,432]{1,0:T(8,128)(2,1)S(1)}, bf16[96,432]{1,0:T(8,128)(2,1)S(1)}, u32[]{:S(2)}, u32[]{:S(2)}) %collective-permute-start.15) | collective-permute-done | bytes 82976 | tf_op jit(solution)/shard_map/ppermute | solution.py:201
  183.2 0.7 fusion.11
  (62 shorter events, 3.4 us)
Async XLA Ops:
  2.2 34.4 %collective-permute-start.2 = (bf16[16,64,384]{2,1,0:T(8,128)(2,1)S(1)}, bf16[16,64,384]{2,1,0:T(8,128)(2,1)S(1)}, u32[]{:S(2)}, u32[]{:S(2)}) collective-permute-start(bf16[16,64,384]{2,1,0:T(8,128)(2,1)S(1)} %get-tuple-element.18), channel_id=1, source_target_pairs={{0,1},{1,2},{2,3},{3,4},{4,5},{5,6},{6,7},{8,9},{9,10},{10,11},{11... | collective-permute-start | bytes 2359304 | tf_op jit(solution)/shard_map/ppermute | solution.py:21
  4.6 32.0 %collective-permute-start.3 = (bf16[16,64,384]{2,1,0:T(8,128)(2,1)S(1)}, bf16[16,64,384]{2,1,0:T(8,128)(2,1)S(1)}, u32[]{:S(2)}, u32[]{:S(2)}) collective-permute-start(bf16[16,64,384]{2,1,0:T(8,128)(2,1)S(1)} %get-tuple-element.17), channel_id=1, source_target_pairs={{1,0},{2,1},{3,2},{4,3},{5,4},{6,5},{7,6},{9,8},{10,9},{11,10},{12... | collective-permute-start | bytes 2359304 | tf_op jit(solution)/shard_map/ppermute | solution.py:22
  7.7 6.5 %collective-permute-start = (bf16[4,64,384]{2,1,0:T(8,128)(2,1)}, bf16[4,64,384]{2,1,0:T(8,128)(2,1)S(1)}, u32[]{:S(2)}, u32[]{:S(2)}) collective-permute-start(bf16[4,64,384]{2,1,0:T(8,128)(2,1)} %get-tuple-element.20), channel_id=1, source_target_pairs={{0,1},{1,2},{2,3},{3,4},{4,5},{5,6},{6,7},{8,9},{9,10},{10,11},{11... | collective-permute-start | bytes 589832 | tf_op jit(solution)/shard_map/ppermute | solution.py:21
  12.9 4.8 %collective-permute-start.1 = (bf16[4,64,384]{2,1,0:T(8,128)(2,1)}, bf16[4,64,384]{2,1,0:T(8,128)(2,1)S(1)}, u32[]{:S(2)}, u32[]{:S(2)}) collective-permute-start(bf16[4,64,384]{2,1,0:T(8,128)(2,1)} %get-tuple-element.19), channel_id=1, source_target_pairs={{1,0},{2,1},{3,2},{4,3},{5,4},{6,5},{7,6},{9,8},{10,9},{11,10},{12... | collective-permute-start | bytes 589832 | tf_op jit(solution)/shard_map/ppermute | solution.py:22
  14.2 3.5 %copy-start.9 = (bf16[4,64,384]{2,1,0:T(8,128)(2,1)}, bf16[4,64,384]{2,1,0:T(8,128)(2,1)S(1)}, u32[]{:S(2)}) copy-start(bf16[4,64,384]{2,1,0:T(8,128)(2,1)S(1)} %collective-permute-done.refs_0_) | copy-start | bytes 589828
  17.6 0.7 copy-start.10
  36.6 0.9 copy-start.1
  37.4 0.9 copy-start.2
  38.4 26.8 %copy-start = (bf16[64,64,384]{2,1,0:T(8,128)(2,1)S(1)}, bf16[64,64,384]{2,1,0:T(8,128)(2,1)}, u32[]{:S(2)}) copy-start(bf16[64,64,384]{2,1,0:T(8,128)(2,1)} %shard_map.67.refs_3_.refs_4_.refs_1_) | copy-start | bytes 9437188
  60.2 28.5 %collective-permute-start.4 = (bf16[4,432,384]{2,1,0:T(8,128)(2,1)}, bf16[4,432,384]{2,1,0:T(8,128)(2,1)}, u32[]{:S(2)}, u32[]{:S(2)}) collective-permute-start(bf16[4,432,384]{2,1,0:T(8,128)(2,1)} %fusion.refs_5_), channel_id=1, source_target_pairs={{0,1},{1,0},{2,3},{3,2},{4,5},{5,4},{6,7},{7,6},{8,9},{9,8},{10,11... | collective-permute-start | bytes 3981320 | tf_op jit(solution)/shard_map/ppermute | solution.py:201
  66.5 55.8 %collective-permute-start.5 = (bf16[16,64,384]{2,1,0:T(8,128)(2,1)}, bf16[16,64,384]{2,1,0:T(8,128)(2,1)}, u32[]{:S(2)}, u32[]{:S(2)}) collective-permute-start(bf16[16,64,384]{2,1,0:T(8,128)(2,1)} %get-tuple-element.16), channel_id=1, source_target_pairs={{0,1},{1,2},{2,3},{3,4},{4,5},{5,6},{6,7},{8,9},{9,10},{10,11},{11... | collective-permute-start | bytes 2359304 | tf_op jit(solution)/shard_map/ppermute | solution.py:21
  69.3 19.4 %slice-start = ((s8[5308416]{0:T(1024)(128)(4,1)}), s8[4194304]{0:T(1024)(128)(4,1)S(1)}, s32[]{:S(2)}) async-start(s8[5308416]{0:T(1024)(128)(4,1)} %bitcast.93), calls=%async_computation | async-start | bytes 8388608
  69.3 19.4 %slice-start.1 = ((s8[5308416]{0:T(1024)(128)(4,1)}), s8[1114112]{0:T(1024)(128)(4,1)S(1)}, s32[]{:S(2)}) async-start(s8[5308416]{0:T(1024)(128)(4,1)} %bitcast.93), calls=%async_computation.1 | async-start | bytes 2228224
  69.3 55.5 %collective-permute-start.6 = (bf16[16,64,384]{2,1,0:T(8,128)(2,1)}, bf16[16,64,384]{2,1,0:T(8,128)(2,1)}, u32[]{:S(2)}, u32[]{:S(2)}) collective-permute-start(bf16[16,64,384]{2,1,0:T(8,128)(2,1)} %get-tuple-element.15), channel_id=1, source_target_pairs={{1,0},{2,1},{3,2},{4,3},{5,4},{6,5},{7,6},{9,8},{10,9},{11,10},{12... | collective-permute-start | bytes 2359304 | tf_op jit(solution)/shard_map/ppermute | solution.py:22
  95.2 26.6 %copy-start.4 = (bf16[96,1728]{1,0:T(8,128)(2,1)S(1)}, bf16[96,1728]{1,0:T(8,128)(2,1)}, u32[]{:S(2)}) copy-start(bf16[96,1728]{1,0:T(8,128)(2,1)} %get-tuple-element.25.refs_5_) | copy-start | bytes 995332
  95.2 27.1 %copy-start.3 = (bf16[96,1728]{1,0:T(8,128)(2,1)S(1)}, bf16[96,1728]{1,0:T(8,128)(2,1)}, u32[]{:S(2)}) copy-start(bf16[96,1728]{1,0:T(8,128)(2,1)} %get-tuple-element.26.refs_4_) | copy-start | bytes 995332
  117.7 29.2 %collective-permute-start.7 = (bf16[4,432,384]{2,1,0:T(8,128)(2,1)}, bf16[4,432,384]{2,1,0:T(8,128)(2,1)}, u32[]{:S(2)}, u32[]{:S(2)}) collective-permute-start(bf16[4,432,384]{2,1,0:T(8,128)(2,1)} %fusion.1.refs_4_), channel_id=1, source_target_pairs={{0,1},{1,0},{2,3},{3,2},{4,5},{5,4},{6,7},{7,6},{8,9},{9,8},{10,11... | collective-permute-start | bytes 3981320 | tf_op jit(solution)/shard_map/ppermute | solution.py:201
  119.4 13.8 %collective-permute-start.10 = (bf16[96,1728]{1,0:T(8,128)(2,1)}, bf16[96,1728]{1,0:T(8,128)(2,1)S(1)}, u32[]{:S(2)}, u32[]{:S(2)}) collective-permute-start(bf16[96,1728]{1,0:T(8,128)(2,1)} %get-tuple-element.24.refs_6_), channel_id=1, source_target_pairs={{0,24},{8,16},{16,8},{24,0},{1,25},{9,17},{17,9},{25,1},{2,26},{10... | collective-permute-start | bytes 995336 | tf_op jit(solution)/shard_map/ppermute | solution.py:201
  121.8 16.0 %collective-permute-start.9 = (bf16[96,1728]{1,0:T(8,128)(2,1)S(1)}, bf16[96,1728]{1,0:T(8,128)(2,1)S(1)}, u32[]{:S(2)}, u32[]{:S(2)}) collective-permute-start(bf16[96,1728]{1,0:T(8,128)(2,1)S(1)} %copy-done.4), channel_id=1, source_target_pairs={{0,16},{8,24},{16,0},{24,8},{1,17},{9,25},{17,1},{25,9},{2,18},{10... | collective-permute-start | bytes 995336 | tf_op jit(solution)/shard_map/ppermute | solution.py:201
  122.3 15.6 %collective-permute-start.8 = (bf16[96,1728]{1,0:T(8,128)(2,1)S(1)}, bf16[96,1728]{1,0:T(8,128)(2,1)S(1)}, u32[]{:S(2)}, u32[]{:S(2)}) collective-permute-start(bf16[96,1728]{1,0:T(8,128)(2,1)S(1)} %copy-done.3), channel_id=1, source_target_pairs={{0,8},{8,0},{16,24},{24,16},{1,9},{9,1},{17,25},{25,17},{2,10},{10... | collective-permute-start | bytes 995336 | tf_op jit(solution)/shard_map/ppermute | solution.py:201
  142.4 7.6 %copy-start.11 = (bf16[96,1,432]{2,0,1:T(8,128)(2,1)}, bf16[96,1,432]{2,0,1:T(8,128)(2,1)S(1)}, u32[]{:S(2)}) copy-start(bf16[96,1,432]{2,0,1:T(8,128)(2,1)S(1)} %copy.51) | copy-start | bytes 248836
  142.4 7.5 %copy-start.12 = (bf16[96,1,432]{2,0,1:T(8,128)(2,1)}, bf16[96,1,432]{2,0,1:T(8,128)(2,1)S(1)}, u32[]{:S(2)}) copy-start(bf16[96,1,432]{2,0,1:T(8,128)(2,1)S(1)} %copy.52) | copy-start | bytes 248836
  142.5 7.5 %copy-start.13 = (bf16[96,1,432]{2,0,1:T(8,128)(2,1)}, bf16[96,1,432]{2,0,1:T(8,128)(2,1)S(1)}, u32[]{:S(2)}) copy-start(bf16[96,1,432]{2,0,1:T(8,128)(2,1)S(1)} %copy.53) | copy-start | bytes 248836
  142.5 12.9 %collective-permute-start.19 = (bf16[96,432]{1,0:T(8,128)(2,1)S(1)}, bf16[96,432]{1,0:T(8,128)(2,1)S(1)}, u32[]{:S(2)}, u32[]{:S(2)}) collective-permute-start(bf16[96,432]{1,0:T(8,128)(2,1)S(1)} %bitcast.110), channel_id=1, source_target_pairs={{0,6},{1,7},{2,4},{3,5},{4,2},{5,3},{6,0},{7,1},{8,14},{9,15},{10,... | collective-permute-start | bytes 248840 | tf_op jit(solution)/shard_map/ppermute | solution.py:201
  144.8 26.0 %collective-permute-start.18 = (bf16[96,432]{1,0:T(8,128)(2,1)S(1)}, bf16[96,432]{1,0:T(8,128)(2,1)S(1)}, u32[]{:S(2)}, u32[]{:S(2)}) collective-permute-start(bf16[96,432]{1,0:T(8,128)(2,1)S(1)} %bitcast.108), channel_id=1, source_target_pairs={{0,4},{1,5},{2,6},{3,7},{4,0},{5,1},{6,2},{7,3},{8,12},{9,13},{10,... | collective-permute-start | bytes 248840 | tf_op jit(solution)/shard_map/ppermute | solution.py:201
  145.9 24.9 %collective-permute-start.17 = (bf16[96,432]{1,0:T(8,128)(2,1)S(1)}, bf16[96,432]{1,0:T(8,128)(2,1)S(1)}, u32[]{:S(2)}, u32[]{:S(2)}) collective-permute-start(bf16[96,432]{1,0:T(8,128)(2,1)S(1)} %bitcast.106), channel_id=1, source_target_pairs={{0,2},{1,3},{2,0},{3,1},{4,6},{5,7},{6,4},{7,5},{8,10},{9,11},{10,... | collective-permute-start | bytes 248840 | tf_op jit(solution)/shard_map/ppermute | solution.py:201
  152.3 3.6 %copy-start.5 = (bf16[96,1728]{1,0:T(8,128)(2,1)}, bf16[96,1728]{1,0:T(8,128)(2,1)S(1)}, u32[]{:S(2)}) copy-start(bf16[96,1728]{1,0:T(8,128)(2,1)S(1)} %get-tuple-element.23.refs_5_) | copy-start | bytes 995332
  152.3 3.6 %copy-start.6 = (bf16[96,1728]{1,0:T(8,128)(2,1)}, bf16[96,1728]{1,0:T(8,128)(2,1)S(1)}, u32[]{:S(2)}) copy-start(bf16[96,1728]{1,0:T(8,128)(2,1)S(1)} %get-tuple-element.22.refs_6_) | copy-start | bytes 995332
  152.3 3.6 %copy-start.7 = (bf16[96,1728]{1,0:T(8,128)(2,1)}, bf16[96,1728]{1,0:T(8,128)(2,1)S(1)}, u32[]{:S(2)}) copy-start(bf16[96,1728]{1,0:T(8,128)(2,1)S(1)} %get-tuple-element.21.refs_7_) | copy-start | bytes 995332
  152.4 19.2 %collective-permute-start.13 = (bf16[96,1728]{1,0:T(8,128)(2,1)S(1)}, bf16[96,1728]{1,0:T(8,128)(2,1)S(1)}, u32[]{:S(2)}, u32[]{:S(2)}) collective-permute-start(bf16[96,1728]{1,0:T(8,128)(2,1)S(1)} %get-tuple-element.21.refs_7_), channel_id=1, source_target_pairs={{0,24},{8,16},{16,8},{24,0},{1,25},{9,17},{17,9},{25,1},{2,26},{10... | collective-permute-start | bytes 995336 | tf_op jit(solution)/shard_map/ppermute | solution.py:201
  153.9 17.7 %collective-permute-start.12 = (bf16[96,1728]{1,0:T(8,128)(2,1)S(1)}, bf16[96,1728]{1,0:T(8,128)(2,1)S(1)}, u32[]{:S(2)}, u32[]{:S(2)}) collective-permute-start(bf16[96,1728]{1,0:T(8,128)(2,1)S(1)} %get-tuple-element.22.refs_6_), channel_id=1, source_target_pairs={{0,16},{8,24},{16,0},{24,8},{1,17},{9,25},{17,1},{25,9},{2,18},{10... | collective-permute-start | bytes 995336 | tf_op jit(solution)/shard_map/ppermute | solution.py:201
  155.4 16.2 %collective-permute-start.11 = (bf16[96,1728]{1,0:T(8,128)(2,1)S(1)}, bf16[96,1728]{1,0:T(8,128)(2,1)S(1)}, u32[]{:S(2)}, u32[]{:S(2)}) collective-permute-start(bf16[96,1728]{1,0:T(8,128)(2,1)S(1)} %get-tuple-element.23.refs_5_), channel_id=1, source_target_pairs={{0,8},{8,0},{16,24},{24,16},{1,9},{9,1},{17,25},{25,17},{2,10},{10... | collective-permute-start | bytes 995336 | tf_op jit(solution)/shard_map/ppermute | solution.py:201
  156.0 14.8 %copy-start.8 = (f32[96,1,432]{2,0,1:T(8,128)S(1)}, f32[96,1,432]{2,0,1:T(8,128)}, u32[]{:S(2)}) copy-start(f32[96,1,432]{2,0,1:T(8,128)} %copy.50) | copy-start | bytes 497668
  173.1 7.4 %collective-permute-start.16 = (bf16[96,432]{1,0:T(8,128)(2,1)S(1)}, bf16[96,432]{1,0:T(8,128)(2,1)S(1)}, u32[]{:S(2)}, u32[]{:S(2)}) collective-permute-start(bf16[96,432]{1,0:T(8,128)(2,1)S(1)} %bitcast.112), channel_id=1, source_target_pairs={{0,6},{1,7},{2,4},{3,5},{4,2},{5,3},{6,0},{7,1},{8,14},{9,15},{10,... | collective-permute-start | bytes 248840 | tf_op jit(solution)/shard_map/ppermute | solution.py:201
  175.4 7.7 %collective-permute-start.15 = (bf16[96,432]{1,0:T(8,128)(2,1)S(1)}, bf16[96,432]{1,0:T(8,128)(2,1)S(1)}, u32[]{:S(2)}, u32[]{:S(2)}) collective-permute-start(bf16[96,432]{1,0:T(8,128)(2,1)S(1)} %bitcast.113), channel_id=1, source_target_pairs={{0,4},{1,5},{2,6},{3,7},{4,0},{5,1},{6,2},{7,3},{8,12},{9,13},{10,... | collective-permute-start | bytes 248840 | tf_op jit(solution)/shard_map/ppermute | solution.py:201
  175.8 7.4 %collective-permute-start.14 = (bf16[96,432]{1,0:T(8,128)(2,1)S(1)}, bf16[96,432]{1,0:T(8,128)(2,1)S(1)}, u32[]{:S(2)}, u32[]{:S(2)}) collective-permute-start(bf16[96,432]{1,0:T(8,128)(2,1)S(1)} %bitcast.114), channel_id=1, source_target_pairs={{0,2},{1,3},{2,0},{3,1},{4,6},{5,7},{6,4},{7,5},{8,10},{9,11},{10,... | collective-permute-start | bytes 248840 | tf_op jit(solution)/shard_map/ppermute | solution.py:201
